TPU v7x, 256 devices: a whole 4x4x8 slice. The times are simulated.
256 devices in a mesh: dp: 8 (over y, core), seq: 32 (over x, z).
Axes of the slice: x: 4, y: 4, z: 8, core: 2. Of those that a mesh axis runs over, the one named last changes fastest.
Arguments:
- hidden_in: bfloat16 [8, 64, 64, 1152], P('dp', 'seq'), may hold values from -2.5 to 2.5
- spatial_qkv: bfloat16 [8, 64, 64, 3456], P('dp', 'seq'), may hold values from -6 to 6
- temporal_qkv: bfloat16 [8, 64, 64, 3456], P('dp', 'seq'), may hold values from -6 to 6
- teacher_target: bfloat16 [8, 64, 64, 1152], P('dp', 'seq'), may hold values from -5 to 5
- spatial_proj: bfloat16 [1152, 1152], P('seq'), may hold values from -0.1875 to 0.1875
- temporal_proj: bfloat16 [1152, 1152], P('seq'), may hold values from -0.1875 to 0.1875
Outputs:
- clip_loss: float32 [8], P('dp')
- spatial_qkv_grad: bfloat16 [8, 64, 64, 3456], P('dp', 'seq')
- temporal_qkv_grad: bfloat16 [8, 64, 64, 3456], P('dp', 'seq')
- spatial_proj_grad: float32 [1152, 1152], P('seq')
- temporal_proj_grad: float32 [1152, 1152], P('seq')
All inputs are finite; a program needn't handle non-finite values.
Results may differ from a plain program's by a relative error of at most 0.018.
Values may be sent and summed in bfloat16 or wider, within the bound.
No kernel may reach another device: no remote copies, remote signals or barrier semaphores. Data moves between devices by JAX's collectives and lax.ppermute only.
A program may use at most 128 MiB of HBM per device.

v0:
```python
import jax
import jax.numpy as jnp
from jax import lax
from jax.sharding import PartitionSpec as P

HEADS = 16


huber_delta = 0.03


def split_qkv(packed):
    channels = packed.shape[-1] // 3
    heads_split = packed.reshape(packed.shape[:-1] + (3, HEADS, channels // HEADS))
    return (heads_split[..., 0, :, :], heads_split[..., 1, :, :], heads_split[..., 2, :, :])


def attend(packed):
    queries, key_rows, values = split_qkv(packed)
    scaling = queries.shape[-1] ** (-0.5)
    scores = (
        jnp.einsum("nqhe,nkhe->nhqk", queries, key_rows, preferred_element_type=jnp.float32)
        * scaling
    )
    attn_probs = jax.nn.softmax(scores, axis=-1)
    rounded = attn_probs.astype(jnp.bfloat16)
    mixed = jnp.einsum("nhqk,nkhe->nqhe", rounded, values, preferred_element_type=jnp.float32)
    mixed = mixed.astype(jnp.bfloat16)
    return (attn_probs, rounded, mixed.reshape(packed.shape[:-1] + (packed.shape[-1] // 3,)))


def attend_back(packed, attn_probs, rounded, mix_grad):
    queries, key_rows, values = split_qkv(packed)
    scaling = queries.shape[-1] ** (-0.5)
    out_heads = mix_grad.reshape(queries.shape)
    value_grad = jnp.einsum(
        "nhqk,nqhe->nkhe", rounded, out_heads, preferred_element_type=jnp.float32
    )
    prob_grad = jnp.einsum("nqhe,nkhe->nhqk", out_heads, values, preferred_element_type=jnp.float32)
    inner = jnp.sum(prob_grad * attn_probs, axis=-1, keepdims=True)
    score_grad = (attn_probs * (prob_grad - inner) * scaling).astype(jnp.bfloat16)
    query_grad = jnp.einsum(
        "nhqk,nkhe->nqhe", score_grad, key_rows, preferred_element_type=jnp.float32
    )
    key_grad = jnp.einsum(
        "nhqk,nqhe->nkhe", score_grad, queries, preferred_element_type=jnp.float32
    )
    joined = jnp.stack([query_grad, key_grad, value_grad], axis=-3).astype(jnp.bfloat16)
    return joined.reshape(packed.shape)


def by_patch(block):
    clip_count, frame_count, patch_count, channels = block.shape
    return jnp.swapaxes(block, 1, 2).reshape(clip_count * patch_count, frame_count, channels)


def by_frame(block, clip_count, patch_count):
    rows_count, frame_count, channels = block.shape
    return jnp.swapaxes(block.reshape(clip_count, patch_count, frame_count, channels), 1, 2)


def project(mixed, weight):
    return jnp.einsum("cfpd,de->cfpe", mixed, weight, preferred_element_type=jnp.float32)


def project_back(out_grad, weight):
    return jnp.einsum("cfpe,de->cfpd", out_grad, weight, preferred_element_type=jnp.float32).astype(
        jnp.bfloat16
    )


def token_sum(mixed, out_grad):
    return jnp.einsum("cfpd,cfpe->de", mixed, out_grad, preferred_element_type=jnp.float32)


def pseudo_huber(resid, cell_count):
    partial_sums = jnp.sum(resid * resid, axis=(1, 2, 3))
    totals = lax.psum(partial_sums, "seq")
    spread = jnp.sqrt(totals / cell_count + huber_delta**2)
    out_grad = (resid / spread[:, None, None, None]).astype(jnp.bfloat16)
    return (out_grad, spread - huber_delta)


def temporal_forward(time_packed):
    clip_count, frame_count, patch_count, channels = time_packed.shape
    flat_time = by_patch(time_packed)
    time_probs, time_round, time_mix_flat = attend(flat_time)
    return (flat_time, time_probs, time_round, by_frame(time_mix_flat, clip_count, patch_count))


def temporal_backward(flat_time, time_probs, time_round, time_mix_grad):
    clip_count, frame_count, patch_count, channels = time_mix_grad.shape
    time_grad = attend_back(flat_time, time_probs, time_round, by_patch(time_mix_grad))
    return by_frame(time_grad, clip_count, patch_count)


def per_device(hidden_in, spatial_qkv, temporal_qkv, teacher_target, spatial_proj, temporal_proj):
    clip_count, frames_here, patch_count, channels = hidden_in.shape
    cell_count = frames_here * lax.axis_size("seq") * patch_count * channels
    spatial_whole, temporal_whole = (
        lax.all_gather(spatial_proj, "seq", axis=0, tiled=True),
        lax.all_gather(temporal_proj, "seq", axis=0, tiled=True),
    )
    flat_space = spatial_qkv.reshape(clip_count * frames_here, patch_count, 3 * channels)
    space_probs, space_round, space_mix_flat = attend(flat_space)
    spatial_mix = space_mix_flat.reshape(clip_count, frames_here, patch_count, channels)
    time_packed = lax.all_to_all(temporal_qkv, "seq", split_axis=2, concat_axis=1, tiled=True)
    flat_time, time_probs, time_round, time_mix_patch = temporal_forward(time_packed)
    temporal_mix = lax.all_to_all(time_mix_patch, "seq", split_axis=1, concat_axis=2, tiled=True)
    after = hidden_in.astype(jnp.float32) + project(spatial_mix, spatial_whole)
    output = after + project(temporal_mix, temporal_whole)
    resid = output - teacher_target.astype(jnp.float32)
    out_grad, clip_loss = pseudo_huber(resid, cell_count)
    space_weight = token_sum(spatial_mix, out_grad)
    time_weight = token_sum(temporal_mix, out_grad)
    space_mix_grad = project_back(out_grad, spatial_whole)
    time_mix_grad = lax.all_to_all(
        project_back(out_grad, temporal_whole), "seq", split_axis=2, concat_axis=1, tiled=True
    )
    time_grad_patch = temporal_backward(flat_time, time_probs, time_round, time_mix_grad)
    temporal_qkv_grad = lax.all_to_all(
        time_grad_patch, "seq", split_axis=1, concat_axis=2, tiled=True
    )
    space_grad = attend_back(
        flat_space,
        space_probs,
        space_round,
        space_mix_grad.reshape(clip_count * frames_here, patch_count, channels),
    )
    spatial_qkv_grad = space_grad.reshape(spatial_qkv.shape)
    space_rows, time_rows = (
        lax.psum_scatter(
            space_weight.astype(jnp.bfloat16), "seq", scatter_dimension=0, tiled=True
        ).astype(jnp.float32),
        lax.psum_scatter(
            time_weight.astype(jnp.bfloat16), "seq", scatter_dimension=0, tiled=True
        ).astype(jnp.float32),
    )
    space_piece, time_piece = (
        lax.psum_scatter(
            space_rows.astype(jnp.bfloat16), "dp", scatter_dimension=1, tiled=True
        ).astype(jnp.float32),
        lax.psum_scatter(
            time_rows.astype(jnp.bfloat16), "dp", scatter_dimension=1, tiled=True
        ).astype(jnp.float32),
    )
    spatial_proj_grad, temporal_proj_grad = (
        lax.all_gather(space_piece.astype(jnp.bfloat16), "dp", axis=1, tiled=True).astype(
            space_piece.dtype
        ),
        lax.all_gather(time_piece.astype(jnp.bfloat16), "dp", axis=1, tiled=True).astype(
            time_piece.dtype
        ),
    )
    return (clip_loss, spatial_qkv_grad, temporal_qkv_grad, spatial_proj_grad, temporal_proj_grad)


def solution(mesh):
    placed = (
        P("dp", "seq", None, None),
        P("dp", "seq", None, None),
        P("dp", "seq", None, None),
        P("dp", "seq", None, None),
        P("seq", None),
        P("seq", None),
    )
    return jax.shard_map(
        per_device,
        mesh=mesh,
        in_specs=placed,
        out_specs=(
            P("dp"),
            P("dp", "seq", None, None),
            P("dp", "seq", None, None),
            P("seq", None),
            P("seq", None),
        ),
        check_vma=False,
    )
```

profile of v0, /device:TPU:1, one launch (start us, length us, event | category | flops | bytes accessed | tf_op | source)
XLA Modules:
  0.0 580.1 jit_solution(10780470106564393415)
XLA Ops:
  8.7 3.0 copy.109
  11.6 11.9 %all-to-all-start = ((bf16[1,2,64,3456]{3,1,0,2:T(2,128)(2,1)}), bf16[1,2,64,3456]{3,1,0,2:T(2,128)(2,1)S(1)}, u32[]{:S(2)}, u32[]{:S(2)}) async-start(bf16[1,2,64,3456]{3,1,0,2:T(2,128)(2,1)} %copy.109), calls=%async_computation | async-start | bytes 1769472 | tf_op jit(solution)/shard_map/all_to_all | solution.py:107
  23.5 2.8 reshape_reshape.20
  26.3 20.9 %all-to-all-done = bf16[1,2,64,3456]{3,1,0,2:T(2,128)(2,1)S(1)} async-done(((bf16[1,2,64,3456]{3,1,0,2:T(2,128)(2,1)}), bf16[1,2,64,3456]{3,1,0,2:T(2,128)(2,1)S(1)}, u32[]{:S(2)}, u32[]{:S(2)}) %all-to-all-start) | async-done | bytes 884768 | tf_op jit(solution)/shard_map/all_to_all | solution.py:107
  48.8 4.8 reshape.92
  54.9 1.9 fusion.76
  59.7 8.6 %all-to-all-start.1 = ((bf16[1,64,2,1152]{3,2,0,1:T(2,128)(2,1)}), bf16[1,64,2,1152]{3,2,0,1:T(2,128)(2,1)S(1)}, u32[]{:S(2)}, u32[]{:S(2)}) async-start(bf16[1,64,2,1152]{3,2,0,1:T(2,128)(2,1)} %copy.117), calls=%async_computation.1 | async-start | bytes 589824 | tf_op jit(solution)/shard_map/all_to_all | solution.py:109
  73.9 6.3 %all-to-all-done.1 = bf16[1,64,2,1152]{3,2,0,1:T(2,128)(2,1)S(1)} async-done(((bf16[1,64,2,1152]{3,2,0,1:T(2,128)(2,1)}), bf16[1,64,2,1152]{3,2,0,1:T(2,128)(2,1)S(1)}, u32[]{:S(2)}, u32[]{:S(2)}) %all-to-all-start.1) | async-done | bytes 294944 | tf_op jit(solution)/shard_map/all_to_all | solution.py:109
  80.6 14.7 %all-gather.7.cloned.1.call-done = bf16[32,36,1152]{2,1,0:T(8,128)(2,1)} async-done(((bf16[1,36,1152]{2,1,0:T(8,128)(2,1)}), bf16[32,36,1152]{2,1,0:T(8,128)(2,1)}) %all-gather.7.cloned.1.call-update) | async-done | bytes 2654224 | tf_op jit(solution)/shard_map/all_gather | solution.py:101
  95.3 3.6 reshape.80
  100.3 75.2 %all-gather.9.cloned.1.call-done = bf16[32,36,1152]{2,1,0:T(8,128)(2,1)} async-done(((bf16[1,36,1152]{2,1,0:T(8,128)(2,1)}), bf16[32,36,1152]{2,1,0:T(8,128)(2,1)}) %all-gather.9.cloned.1.call-update) | async-done | bytes 2654224 | tf_op jit(solution)/shard_map/all_gather | solution.py:102
  175.6 5.2 reshape.81
  180.7 3.9 multiply_reduce_fusion.2
  184.6 58.7 %psum.7 = f32[1]{0:T(128)} all-reduce(f32[1]{0:T(128)} %bitcast.19), channel_id=1, replica_groups=mesh['dp'=8,'seq'=32] {'seq'}, use_global_device_ids=true, to_apply=%region_5.0 | all-reduce | flops 1 | bytes 8 | tf_op jit(solution)/shard_map/psum | solution.py:78
  245.1 2.7 fusion.11
  247.8 2.4 fusion.6
  250.2 2.4 fusion.7
  253.6 4.6 all-to-all-start.2
  258.2 85.9 %fusion.72 = (bf16[48,1152]{1,0:T(8,128)(2,1)}, bf16[48,1152]{1,0:T(8,128)(2,1)}) fusion(bf16[1152,1152]{1,0:T(8,128)(2,1)} %fusion.6, bf16[1152,1152]{1,0:T(8,128)(2,1)} %fusion.7), kind=kCustom, calls=%all-reduce-scatter.2 | all-reduce-scatter fusion | flops 3538945 | bytes 5530624
  345.7 1.9 collective-permute-start.6
  347.6 1.9 collective-permute-start.5
  349.6 1.9 collective-permute-start.4
  351.5 3.6 collective-permute-start.3
  358.5 5.0 collective-permute-start.15
  368.9 3.0 fusion.29
  371.9 3.1 fusion.30
  377.4 1.8 convert_element_type.100
  381.1 4.2 all-to-all-start.3
  385.4 3.8 collective-permute-start.7
  390.4 4.9 collective-permute-start.2
  395.4 4.9 collective-permute-start.1
  400.2 1.9 collective-permute-start
  402.1 6.3 %collective-permute-start.14 = (bf16[48,1152]{1,0:T(8,128)(2,1)S(1)}, bf16[48,1152]{1,0:T(8,128)(2,1)S(1)}, u32[]{:S(2)}, u32[]{:S(2)}) collective-permute-start(bf16[48,1152]{1,0:T(8,128)(2,1)S(1)} %copy-done.4), channel_id=1, source_target_pairs={{0,7},{1,8},{2,9},{3,10},{4,11},{5,12},{6,13},{7,14},{8,15},{9,16}... | collective-permute-start | bytes 331784
  408.4 3.3 collective-permute-start.13
  411.7 2.3 fusion.28
  414.0 3.8 collective-permute-start.12
  417.8 8.2 %collective-permute-start.11 = (bf16[48,1152]{1,0:T(8,128)(2,1)S(1)}, bf16[48,1152]{1,0:T(8,128)(2,1)S(1)}, u32[]{:S(2)}, u32[]{:S(2)}) collective-permute-start(bf16[48,1152]{1,0:T(8,128)(2,1)S(1)} %copy-done.4), channel_id=1, source_target_pairs={{0,4},{1,5},{2,6},{3,7},{4,8},{5,9},{6,10},{7,11},{8,12},{9,13},{1... | collective-permute-start | bytes 331784
  427.4 4.4 collective-permute-start.9
  432.4 3.7 collective-permute-start.8
  436.2 3.1 fusion.27
  439.3 6.9 %concatenate = bf16[420,1152]{1,0:T(8,128)(2,1)S(1)} concatenate(bf16[36,1152]{1,0:T(8,128)(2,1)} %collective-permute-done.7, bf16[48,1152]{1,0:T(8,128)(2,1)} %collective-permute-done.6, bf16[48,1152]{1,0:T(8,128)(2,1)} %collective-permute-done.5, bf16[48,1152]{1,0:T(8,128)(2,1)} %collective-permute-done.4, bf16[48,1152]{1,0:T(8,128)(2,1)} %collective-permute-done.3, ...), dimensions={0} | concatenate | bytes 1935360
  446.9 8.3 %concatenate.1 = bf16[420,1152]{1,0:T(8,128)(2,1)S(1)} concatenate(bf16[36,1152]{1,0:T(8,128)(2,1)} %collective-permute-done.15, bf16[48,1152]{1,0:T(8,128)(2,1)} %copy-done.17, bf16[48,1152]{1,0:T(8,128)(2,1)} %copy-done.18, bf16[48,1152]{1,0:T(8,128)(2,1)} %copy-done.21, bf16[48,1152]{1,0:T(8,128)(2,1)} %copy-done.22, bf16[48,1152]{1,0:T(8,128)(2,1)} %copy-done.23, ...), dimensions={0} | concatenate | bytes 1935360
  458.1 2.8 fusion.26
  462.3 2.6 convert_element_type.96
  465.9 53.0 %reduce-scatter.13.cloned.1.call-done = bf16[144,36]{1,0:T(8,128)(2,1)} async-done(((bf16[1152,36]{1,0:T(8,128)(2,1)}), bf16[144,36]{1,0:T(8,128)(2,1)}) %reduce-scatter.13.cloned.1.call-update) | async-done | bytes 10384
  519.8 15.6 %all-gather.3 = bf16[8,144,36]{1,2,0:T(8,128)(2,1)S(1)} all-gather(bf16[1,144,36]{1,2,0:T(8,128)(2,1)S(1)} %bitcast.188), channel_id=1, replica_groups=mesh['dp'=8,'seq'=32] {'dp'}, dimensions={0}, use_global_device_ids=true | all-gather | bytes 93312 | tf_op jit(solution)/shard_map/all_gather | solution.py:151
  536.2 17.2 %reduce-scatter.11.cloned.1.call-done = bf16[144,36]{1,0:T(8,128)(2,1)} async-done(((bf16[1152,36]{1,0:T(8,128)(2,1)}), bf16[144,36]{1,0:T(8,128)(2,1)}) %reduce-scatter.11.cloned.1.call-update) | async-done | bytes 10384
  554.3 15.6 %all-gather.2 = bf16[8,144,36]{1,2,0:T(8,128)(2,1)S(1)} all-gather(bf16[1,144,36]{1,2,0:T(8,128)(2,1)S(1)} %bitcast.189), channel_id=1, replica_groups=mesh['dp'=8,'seq'=32] {'dp'}, dimensions={0}, use_global_device_ids=true | all-gather | bytes 93312 | tf_op jit(solution)/shard_map/all_gather | solution.py:148
  (125 shorter events, 44.7 us)
Async XLA Ops:
  7.2 16.4 %copy-start.6 = (bf16[1,2,64,3456]{3,2,1,0:T(8,128)(2,1)S(1)}, bf16[1,2,64,3456]{3,2,1,0:T(8,128)(2,1)}, u32[]{:S(2)}) copy-start(bf16[1,2,64,3456]{3,2,1,0:T(8,128)(2,1)} %param.7) | copy-start | bytes 2654212
  7.2 88.2 %all-gather.7.cloned.1.call-start = ((), (), s32[]{:S(2)}) async-start(), calls=%async_computation.6 | async-start | bytes 3041280 | tf_op jit(solution)/shard_map/all_gather | solution.py:101
  7.9 167.7 %all-gather.9.cloned.1.call-start = ((), (), s32[]{:S(2)}) async-start(), calls=%async_computation.7 | async-start | bytes 3041280 | tf_op jit(solution)/shard_map/all_gather | solution.py:102
  11.6 35.6 %all-to-all-start = ((bf16[1,2,64,3456]{3,1,0,2:T(2,128)(2,1)}), bf16[1,2,64,3456]{3,1,0,2:T(2,128)(2,1)S(1)}, u32[]{:S(2)}, u32[]{:S(2)}) async-start(bf16[1,2,64,3456]{3,1,0,2:T(2,128)(2,1)} %copy.109), calls=%async_computation | async-start | bytes 1769472 | tf_op jit(solution)/shard_map/all_to_all | solution.py:107
  54.9 1.9 copy-start.2
  56.8 1.0 copy-start.25
  56.8 1.4 copy-start.26
  59.7 20.6 %all-to-all-start.1 = ((bf16[1,64,2,1152]{3,2,0,1:T(2,128)(2,1)}), bf16[1,64,2,1152]{3,2,0,1:T(2,128)(2,1)S(1)}, u32[]{:S(2)}, u32[]{:S(2)}) async-start(bf16[1,64,2,1152]{3,2,0,1:T(2,128)(2,1)} %copy.117), calls=%async_computation.1 | async-start | bytes 589824 | tf_op jit(solution)/shard_map/all_to_all | solution.py:109
  68.6 3.2 copy-start
  68.6 3.2 copy-start.7
  68.6 3.2 copy-start.9
  70.2 2.5 copy-start.24
  80.6 18.3 %copy-start.16 = (bf16[1,2,64,1152]{3,2,1,0:T(8,128)(2,1)S(1)}, bf16[1,2,64,1152]{3,2,1,0:T(8,128)(2,1)}, u32[]{:S(2)}) copy-start(bf16[1,2,64,1152]{3,2,1,0:T(8,128)(2,1)} %param.6) | copy-start | bytes 884740
  100.3 80.4 %copy-start.15 = (bf16[1,2,64,1152]{3,2,1,0:T(8,128)(2,1)S(1)}, bf16[1,2,64,1152]{3,2,1,0:T(8,128)(2,1)}, u32[]{:S(2)}) copy-start(bf16[1,2,64,1152]{3,2,1,0:T(8,128)(2,1)} %param.9) | copy-start | bytes 884740
  253.6 109.8 %all-to-all-start.2 = ((bf16[1,2,64,1152]{3,1,0,2:T(2,128)(2,1)}), bf16[1,2,64,1152]{3,1,0,2:T(2,128)(2,1)}, u32[]{:S(2)}, u32[]{:S(2)}) async-start(bf16[1,2,64,1152]{3,1,0,2:T(2,128)(2,1)} %copy.123), calls=%async_computation.2 | async-start | bytes 589824 | tf_op jit(solution)/shard_map/all_to_all | solution.py:117
  345.7 49.7 %collective-permute-start.6 = (bf16[48,1152]{1,0:T(8,128)(2,1)}, bf16[48,1152]{1,0:T(8,128)(2,1)}, u32[]{:S(2)}, u32[]{:S(2)}) collective-permute-start(bf16[48,1152]{1,0:T(8,128)(2,1)} %get-tuple-element.22), channel_id=1, source_target_pairs={{0,7},{1,8},{2,9},{3,10},{4,11},{5,12},{6,13},{7,14},{8,15},{9,16}... | collective-permute-start | bytes 331784
  347.6 52.6 %collective-permute-start.5 = (bf16[48,1152]{1,0:T(8,128)(2,1)}, bf16[48,1152]{1,0:T(8,128)(2,1)}, u32[]{:S(2)}, u32[]{:S(2)}) collective-permute-start(bf16[48,1152]{1,0:T(8,128)(2,1)} %get-tuple-element.22), channel_id=1, source_target_pairs={{0,6},{1,7},{2,8},{3,9},{4,10},{5,11},{6,12},{7,13},{8,14},{9,15},... | collective-permute-start | bytes 331784
  349.6 52.5 %collective-permute-start.4 = (bf16[48,1152]{1,0:T(8,128)(2,1)}, bf16[48,1152]{1,0:T(8,128)(2,1)}, u32[]{:S(2)}, u32[]{:S(2)}) collective-permute-start(bf16[48,1152]{1,0:T(8,128)(2,1)} %get-tuple-element.22), channel_id=1, source_target_pairs={{0,5},{1,6},{2,7},{3,8},{4,9},{5,10},{6,11},{7,12},{8,13},{9,14},{... | collective-permute-start | bytes 331784
  351.5 56.9 %collective-permute-start.3 = (bf16[48,1152]{1,0:T(8,128)(2,1)}, bf16[48,1152]{1,0:T(8,128)(2,1)}, u32[]{:S(2)}, u32[]{:S(2)}) collective-permute-start(bf16[48,1152]{1,0:T(8,128)(2,1)} %get-tuple-element.22), channel_id=1, source_target_pairs={{0,4},{1,5},{2,6},{3,7},{4,8},{5,9},{6,10},{7,11},{8,12},{9,13},{1... | collective-permute-start | bytes 331784
  356.0 11.3 %copy-start.27 = (f32[2,16,64]{2,1,0:T(8,128)S(1)}, f32[2,16,64]{2,1,0:T(8,128)}, u32[]{:S(2)}) copy-start(f32[2,16,64]{2,1,0:T(8,128)} %copy-done.26) | copy-start | bytes 24580
  358.5 26.9 %collective-permute-start.15 = (bf16[36,1152]{1,0:T(8,128)(2,1)}, bf16[36,1152]{1,0:T(8,128)(2,1)}, u32[]{:S(2)}, u32[]{:S(2)}) collective-permute-start(bf16[36,1152]{1,0:T(8,128)(2,1)} %slice.37), channel_id=1, source_target_pairs={{0,8},{1,9},{2,10},{3,11},{4,12},{5,13},{6,14},{7,15},{8,16},{9,17... | collective-permute-start | bytes 248840
  365.7 3.1 copy-start.11
  368.8 3.0 copy-start.10
  371.8 3.1 copy-start.14
  377.4 11.7 %copy-start.1 = (bf16[2,64,1,16,72]{4,3,2,1,0:T(8,128)(2,1)S(1)}, bf16[2,64,1,16,72]{4,3,2,1,0:T(8,128)(2,1)}, u32[]{:S(2)}) copy-start(bf16[2,64,1,16,72]{4,3,2,1,0:T(8,128)(2,1)} %copy-done) | copy-start | bytes 884740
  381.1 21.0 %copy-start.4 = (bf16[48,1152]{1,0:T(8,128)(2,1)S(1)}, bf16[48,1152]{1,0:T(8,128)(2,1)}, u32[]{:S(2)}) copy-start(bf16[48,1152]{1,0:T(8,128)(2,1)} %get-tuple-element.23) | copy-start | bytes 331780
  381.1 189.7 %all-to-all-start.3 = ((bf16[1,64,2,3456]{3,2,0,1:T(2,128)(2,1)}), bf16[1,64,2,3456]{3,2,0,1:T(2,128)(2,1)S(1)}, u32[]{:S(2)}, u32[]{:S(2)}) async-start(bf16[1,64,2,3456]{3,2,0,1:T(2,128)(2,1)} %copy.130), calls=%async_computation.3 | async-start | bytes 1769472 | tf_op jit(solution)/shard_map/all_to_all | solution.py:121
  385.3 133.6 %reduce-scatter.13.cloned.1.call-start = ((), (), s32[]{:S(2)}) async-start(), calls=%async_computation.9 | async-start | bytes 331776
  385.4 5.0 collective-permute-start.7
  389.5 46.6 %copy-start.3 = (f32[2,16,64,64]{2,3,1,0:T(8,128)}, f32[2,16,64,64]{2,3,1,0:T(8,128)S(1)}, u32[]{:S(2)}) copy-start(f32[2,16,64,64]{2,3,1,0:T(8,128)S(1)} %fusion.46) | copy-start | bytes 1572868
  390.4 23.6 %collective-permute-start.2 = (bf16[48,1152]{1,0:T(8,128)(2,1)}, bf16[48,1152]{1,0:T(8,128)(2,1)S(1)}, u32[]{:S(2)}, u32[]{:S(2)}) collective-permute-start(bf16[48,1152]{1,0:T(8,128)(2,1)} %get-tuple-element.22), channel_id=1, source_target_pairs={{0,3},{1,4},{2,5},{3,6},{4,7},{5,8},{6,9},{7,10},{8,11},{9,12},{10... | collective-permute-start | bytes 331784
  395.4 22.5 %collective-permute-start.1 = (bf16[48,1152]{1,0:T(8,128)(2,1)}, bf16[48,1152]{1,0:T(8,128)(2,1)S(1)}, u32[]{:S(2)}, u32[]{:S(2)}) collective-permute-start(bf16[48,1152]{1,0:T(8,128)(2,1)} %get-tuple-element.22), channel_id=1, source_target_pairs={{0,2},{1,3},{2,4},{3,5},{4,6},{5,7},{6,8},{7,9},{8,10},{9,11},{10,... | collective-permute-start | bytes 331784
  400.2 25.8 %collective-permute-start = (bf16[48,1152]{1,0:T(8,128)(2,1)}, bf16[48,1152]{1,0:T(8,128)(2,1)S(1)}, u32[]{:S(2)}, u32[]{:S(2)}) collective-permute-start(bf16[48,1152]{1,0:T(8,128)(2,1)} %get-tuple-element.22), channel_id=1, source_target_pairs={{0,1},{1,2},{2,3},{3,4},{4,5},{5,6},{6,7},{7,8},{8,9},{9,10},{10,1... | collective-permute-start | bytes 331784
  402.1 25.3 %collective-permute-start.14 = (bf16[48,1152]{1,0:T(8,128)(2,1)S(1)}, bf16[48,1152]{1,0:T(8,128)(2,1)S(1)}, u32[]{:S(2)}, u32[]{:S(2)}) collective-permute-start(bf16[48,1152]{1,0:T(8,128)(2,1)S(1)} %copy-done.4), channel_id=1, source_target_pairs={{0,7},{1,8},{2,9},{3,10},{4,11},{5,12},{6,13},{7,14},{8,15},{9,16}... | collective-permute-start | bytes 331784
  408.4 23.4 %collective-permute-start.13 = (bf16[48,1152]{1,0:T(8,128)(2,1)S(1)}, bf16[48,1152]{1,0:T(8,128)(2,1)S(1)}, u32[]{:S(2)}, u32[]{:S(2)}) collective-permute-start(bf16[48,1152]{1,0:T(8,128)(2,1)S(1)} %copy-done.4), channel_id=1, source_target_pairs={{0,6},{1,7},{2,8},{3,9},{4,10},{5,11},{6,12},{7,13},{8,14},{9,15},... | collective-permute-start | bytes 331784
  414.0 32.9 %copy-start.5 = (bf16[48,1152]{1,0:T(8,128)(2,1)S(1)}, bf16[48,1152]{1,0:T(8,128)(2,1)}, u32[]{:S(2)}) copy-start(bf16[48,1152]{1,0:T(8,128)(2,1)} %get-tuple-element.23) | copy-start | bytes 331780
  414.0 32.1 %collective-permute-start.12 = (bf16[48,1152]{1,0:T(8,128)(2,1)S(1)}, bf16[48,1152]{1,0:T(8,128)(2,1)S(1)}, u32[]{:S(2)}, u32[]{:S(2)}) collective-permute-start(bf16[48,1152]{1,0:T(8,128)(2,1)S(1)} %copy-done.4), channel_id=1, source_target_pairs={{0,5},{1,6},{2,7},{3,8},{4,9},{5,10},{6,11},{7,12},{8,13},{9,14},{... | collective-permute-start | bytes 331784
  417.8 28.4 %collective-permute-start.11 = (bf16[48,1152]{1,0:T(8,128)(2,1)S(1)}, bf16[48,1152]{1,0:T(8,128)(2,1)S(1)}, u32[]{:S(2)}, u32[]{:S(2)}) collective-permute-start(bf16[48,1152]{1,0:T(8,128)(2,1)S(1)} %copy-done.4), channel_id=1, source_target_pairs={{0,4},{1,5},{2,6},{3,7},{4,8},{5,9},{6,10},{7,11},{8,12},{9,13},{1... | collective-permute-start | bytes 331784
  426.1 5.7 copy-start.19
  426.1 20.1 %collective-permute-start.10 = (bf16[48,1152]{1,0:T(8,128)(2,1)S(1)}, bf16[48,1152]{1,0:T(8,128)(2,1)S(1)}, u32[]{:S(2)}, u32[]{:S(2)}) collective-permute-start(bf16[48,1152]{1,0:T(8,128)(2,1)S(1)} %copy-done.4), channel_id=1, source_target_pairs={{0,3},{1,4},{2,5},{3,6},{4,7},{5,8},{6,9},{7,10},{8,11},{9,12},{10... | collective-permute-start | bytes 331784
  427.4 11.9 %copy-start.17 = (bf16[48,1152]{1,0:T(8,128)(2,1)}, bf16[48,1152]{1,0:T(8,128)(2,1)S(1)}, u32[]{:S(2)}) copy-start(bf16[48,1152]{1,0:T(8,128)(2,1)S(1)} %collective-permute-done.14) | copy-start | bytes 331780
  427.4 18.8 %collective-permute-start.9 = (bf16[48,1152]{1,0:T(8,128)(2,1)S(1)}, bf16[48,1152]{1,0:T(8,128)(2,1)}, u32[]{:S(2)}, u32[]{:S(2)}) collective-permute-start(bf16[48,1152]{1,0:T(8,128)(2,1)S(1)} %copy-done.4), channel_id=1, source_target_pairs={{0,2},{1,3},{2,4},{3,5},{4,6},{5,7},{6,8},{7,9},{8,10},{9,11},{10,... | collective-permute-start | bytes 331784
  432.4 14.5 %collective-permute-start.8 = (bf16[48,1152]{1,0:T(8,128)(2,1)S(1)}, bf16[48,1152]{1,0:T(8,128)(2,1)}, u32[]{:S(2)}, u32[]{:S(2)}) collective-permute-start(bf16[48,1152]{1,0:T(8,128)(2,1)S(1)} %copy-done.4), channel_id=1, source_target_pairs={{0,1},{1,2},{2,3},{3,4},{4,5},{5,6},{6,7},{7,8},{8,9},{9,10},{10,1... | collective-permute-start | bytes 331784
  436.2 3.1 copy-start.20
  439.3 18.8 %copy-start.8 = (bf16[2,64,1,16,72]{4,3,2,1,0:T(8,128)(2,1)S(1)}, bf16[2,64,1,16,72]{4,3,2,1,0:T(8,128)(2,1)}, u32[]{:S(2)}) copy-start(bf16[2,64,1,16,72]{4,3,2,1,0:T(8,128)(2,1)} %copy-done.7) | copy-start | bytes 884740
  457.7 3.2 copy-start.12
  457.7 3.2 copy-start.13
  457.7 95.7 %reduce-scatter.11.cloned.1.call-start = ((), (), s32[]{:S(2)}) async-start(), calls=%async_computation.8 | async-start | bytes 331776
  (4 other events, 2.6 us)
Sparse Core Ops, SparseCore 0:
  10.6 84.6 all-gather.6
  97.9 77.5 all-gather.8
  457.8 61.0 reduce-scatter.12
  521.4 31.9 reduce-scatter.10
where the time goes:
time: 583 us; the launch traced here: 580 us
  waiting for transfers between devices  190 us (33%)
  blocking collectives  176 us (30%)
  starting transfers between devices  90.4 us (16%)
  local copies, waits for them, and re-layouts  67.3 us (12%)
  matrix products  37 us (6%)
  between operations  16.9 us (3%)
    unnamed x1, blocking collectives  85.9 us
    all_gather x1, waiting for transfers between devices, per_device(): lax.all_gather(temporal_proj, 'seq', axis=0, tiled=True)  75.2 us
    unnamed x22, waiting for transfers between devices  72.6 us
    unnamed x18, starting transfers between devices  61 us
    psum x1, blocking collectives, pseudo_huber(): totals = lax.psum(partial_sums, 'seq')  58.7 us
    unnamed x70, local copies, waits for them, and re-layouts  38.6 us
    all_to_all x1, waiting for transfers between devices, per_device(): lax.all_to_all(temporal_qkv, 'seq', split_axis=2, concat_axis=1, tiled=True)  20.9 us
    all_gather x1, blocking collectives, per_device(): lax.all_gather(space_piece.astype(jnp.bfloat16), 'dp', axis=1, tiled=True)  15.6 us
  transfers between devices with their start and end apart: 24, of which 7 were waited for; matrix products, arithmetic and copies ran while one was open for 29% of the time, Pallas kernels for 0%

commit v1 on v0

v1 whole, which is shorter than its diff:
```python
import functools

import jax
import jax.numpy as jnp
from jax import lax
from jax.experimental import pallas as pl
from jax.experimental.pallas import tpu as pltpu
from jax.sharding import Mesh, PartitionSpec as P

HEADS = 16
D = 1152
E = D // HEADS
TOKENS = 128
LANES = 128
SEQ = ("x", "z")
DP = ("y", "core")
HUBER_DELTA = 0.03
CELLS = 64 * 64 * D
SCALING = E ** (-0.5)
BF16 = jnp.bfloat16
F32 = jnp.float32
VMEM_BYTES = 48 * 1024 * 1024

NN = (((1,), (0,)), ((), ()))
NT = (((1,), (1,)), ((), ()))
TN = (((0,), (0,)), ((), ()))


def mul(left, right, dims):
    return lax.dot_general(left, right, dims, preferred_element_type=F32)


def window(head):
    low = E * head // LANES
    high = (E * head + E - 1) // LANES + 1
    return low * LANES, high * LANES


def head_mask(head, low, high):
    lane = lax.broadcasted_iota(jnp.int32, (TOKENS, high - low), 1) + low
    return jnp.where((lane >= E * head) & (lane < E * head + E), 1.0, 0.0).astype(BF16)


def same_sequence(temporal):
    row = lax.broadcasted_iota(jnp.int32, (TOKENS, TOKENS), 0)
    col = lax.broadcasted_iota(jnp.int32, (TOKENS, TOKENS), 1)
    if temporal:
        return (row & 1) == (col & 1)
    return (row >> 6) == (col >> 6)


def natural_from_sent():
    nat = lax.broadcasted_iota(jnp.int32, (TOKENS, TOKENS), 0)
    sent = lax.broadcasted_iota(jnp.int32, (TOKENS, TOKENS), 1)
    goes = ((sent >> 1) & 1) * 64 + (sent >> 2) * 2 + (sent & 1)
    return jnp.where(nat == goes, 1.0, 0.0).astype(BF16)


class Tiles:
    def __init__(self, ref, offset, scale=None):
        self.ref, self.offset, self.scale, self.pending = ref, offset, scale, None

    def add(self, head, value):
        low, high = window(head)
        for tile in range(low, high, LANES):
            part = value[:, tile - low : tile - low + LANES]
            if E * head > tile:
                part = self.pending + part
            if E * head + E >= tile + LANES:
                if self.scale is not None:
                    part = part * self.scale
                at = self.offset + tile
                self.ref[:, at : at + LANES] = part.astype(self.ref.dtype)
            else:
                self.pending = part


def attend_kernel(temporal, x_ref, mix_ref, probs_ref):
    same = same_sequence(temporal)
    out = Tiles(mix_ref, 0)
    for head in range(HEADS):
        low, high = window(head)
        mask = head_mask(head, low, high)
        queries = x_ref[:, low:high]
        keys = x_ref[:, D + low : D + high] * mask
        values = x_ref[:, 2 * D + low : 2 * D + high] * mask
        scores = jnp.where(same, mul(queries, keys, NT) * SCALING, -1e30)
        powers = jnp.exp(scores - jnp.max(scores, axis=1, keepdims=True))
        probs = powers / jnp.sum(powers, axis=1, keepdims=True)
        probs_ref[head] = probs
        out.add(head, mul(probs.astype(BF16), values, NN))


def attend(x, temporal):
    return pl.pallas_call(
        functools.partial(attend_kernel, temporal),
        out_shape=(
            jax.ShapeDtypeStruct((TOKENS, D), BF16),
            jax.ShapeDtypeStruct((HEADS, TOKENS, TOKENS), F32),
        ),
        compiler_params=pltpu.CompilerParams(vmem_limit_bytes=VMEM_BYTES),
        name="attend_time" if temporal else "attend_space",
    )(x)


def attend_back_kernel(inv_ref, x_ref, probs_ref, grad_ref, out_ref):
    inv = inv_ref[0]
    query_out = Tiles(out_ref, 0)
    key_out = Tiles(out_ref, D)
    value_out = Tiles(out_ref, 2 * D, inv)
    for head in range(HEADS):
        low, high = window(head)
        mask = head_mask(head, low, high)
        queries = x_ref[:, low:high] * mask
        keys = x_ref[:, D + low : D + high] * mask
        values = x_ref[:, 2 * D + low : 2 * D + high]
        grads = grad_ref[:, low:high] * mask
        probs = probs_ref[head]
        value_out.add(head, mul(probs.astype(BF16), grads, TN))
        prob_grad = mul(grads, values, NT)
        inner = jnp.sum(prob_grad * probs, axis=1, keepdims=True)
        score_grad = (probs * (prob_grad - inner) * (SCALING * inv)).astype(BF16)
        query_out.add(head, mul(score_grad, keys, NN))
        key_out.add(head, mul(score_grad, queries, TN))


def attend_back(inv, x, probs, grad, name):
    vmem = pl.BlockSpec(memory_space=pltpu.VMEM)
    return pl.pallas_call(
        attend_back_kernel,
        out_shape=jax.ShapeDtypeStruct((TOKENS, 3 * D), BF16),
        in_specs=[pl.BlockSpec(memory_space=pltpu.SMEM), vmem, vmem, vmem],
        compiler_params=pltpu.CompilerParams(vmem_limit_bytes=VMEM_BYTES),
        name=name,
    )(inv, x, probs, grad)


def project_kernel(place_ref, hidden_ref, target_ref, space_ref, time_ref, *rest):
    own_refs, other_refs = rest[0:4], rest[4:8]
    resid_ref, space_grad_ref, time_grad_ref, time_mix_ref = rest[8:12]
    weights, sems = rest[12:]
    at_x, at_core = place_ref[0], place_ref[1]
    copies = []
    for k in range(4):
        rows = pl.ds(pl.multiple_of(lax.rem(at_x + 4 - k, 4) * 288, 288), 288)
        for n, (refs, which) in enumerate(((own_refs, at_core), (other_refs, 1 - at_core))):
            copy = pltpu.make_async_copy(refs[k], weights.at[which, rows], sems.at[2 * k + n])
            copy.start()
            copies.append(copy)
    natural = natural_from_sent()
    time_mix = mul(natural, time_ref[...], NN).astype(BF16)
    time_mix_ref[...] = time_mix
    base = hidden_ref[...].astype(F32) - target_ref[...].astype(F32)
    for copy in copies:
        copy.wait()
    resid = (
        base
        + mul(space_ref[...], weights[0], NN)
        + mul(time_mix, weights[1], NN)
    )
    total = jnp.sum(resid * resid)
    out_grad = resid.astype(BF16)
    resid_ref[...] = out_grad
    time_grad = mul(out_grad, weights[1], NT).astype(BF16)
    time_grad_ref[:, :D] = mul(natural, time_grad, TN).astype(BF16)
    lane = lax.broadcasted_iota(jnp.int32, (TOKENS, LANES), 1)
    whole = jnp.full((TOKENS, LANES), total, F32)
    first = whole.astype(BF16).astype(F32)
    second = (whole - first).astype(BF16).astype(F32)
    third = whole - first - second
    parts = jnp.where(lane == 0, first, jnp.where(lane == 1, second, jnp.where(lane == 2, third, 0.0)))
    time_grad_ref[:, D:] = parts.astype(BF16)
    space_grad_ref[...] = mul(out_grad, weights[0], NT).astype(BF16)


def project(place, hidden, target, space_mix, time_mix, own, other):
    vmem = pl.BlockSpec(memory_space=pltpu.VMEM)
    rows = jax.ShapeDtypeStruct((TOKENS, D), BF16)
    return pl.pallas_call(
        project_kernel,
        out_shape=(rows, rows, jax.ShapeDtypeStruct((TOKENS, D + LANES), BF16), rows),
        in_specs=[pl.BlockSpec(memory_space=pltpu.SMEM)]
        + [vmem] * 4
        + [pl.BlockSpec(memory_space=pl.ANY)] * 8,
        scratch_shapes=[pltpu.VMEM((2, D, D), BF16), pltpu.SemaphoreType.DMA((8,))],
        compiler_params=pltpu.CompilerParams(vmem_limit_bytes=VMEM_BYTES),
        name="project",
    )(place, hidden, target, space_mix, time_mix, *own, *other)


def choose_kernel(space_ref, time_ref, out_ref):
    for part in range(4):
        col = lax.broadcasted_iota(jnp.int32, (D, 288), 0)
        to = lax.broadcasted_iota(jnp.int32, (D, 288), 1)
        block = (to * 7282) >> 16
        wanted = block * 36 + part * 9 + (to - block * 9)
        chosen = jnp.where(col == wanted, 1.0, 0.0).astype(BF16)
        out_ref[2 * part] = mul(space_ref[...], chosen, NN).astype(BF16)
        out_ref[2 * part + 1] = mul(time_ref[...], chosen, NN).astype(BF16)


def choose(space_mix, time_mix):
    return pl.pallas_call(
        choose_kernel,
        out_shape=jax.ShapeDtypeStruct((8, TOKENS, 288), BF16),
        compiler_params=pltpu.CompilerParams(vmem_limit_bytes=VMEM_BYTES),
        name="choose",
    )(space_mix, time_mix)


def weight_kernel(place_ref, inv_ref, mix_ref, own_ref, other_ref, out_ref, total):
    at_x, at_core, at_y = place_ref[0], place_ref[1], place_ref[2]
    for k in range(4):
        from_y = lax.rem(at_y + 4 - k, 4)
        for refs, which in ((own_ref, at_core), (other_ref, 1 - at_core)):
            clip = 2 * from_y + which
            out_grad = (refs[k].astype(F32) * inv_ref[clip]).astype(BF16)
            term = mul(mix_ref[clip], out_grad, TN)
            if k == 0 and refs is own_ref:
                total[...] = term
            else:
                total[...] += term
    for k in range(4):
        rows = pl.ds(pl.multiple_of(lax.rem(at_x + k, 4) * 72, 72), 72)
        out_ref[k] = total[rows, :].astype(BF16)


def weight_grad(place, inv, mixes, own, other):
    vmem = pl.BlockSpec(memory_space=pltpu.VMEM)
    smem = pl.BlockSpec(memory_space=pltpu.SMEM)
    return pl.pallas_call(
        weight_kernel,
        out_shape=jax.ShapeDtypeStruct((4, 72, D), BF16),
        in_specs=[smem, smem, vmem, vmem, vmem],
        scratch_shapes=[pltpu.VMEM((288, D), F32)],
        compiler_params=pltpu.CompilerParams(vmem_limit_bytes=VMEM_BYTES),
        name="weight_grad",
    )(place, inv, mixes, own, other)


def shift(value, axis, size, step):
    return lax.ppermute(value, axis, [(i, (i + step) % size) for i in range(size)])


def swap(value):
    return lax.ppermute(value, "core", [(0, 1), (1, 0)])


def exchange(value, axis):
    return lax.all_to_all(value, axis, split_axis=0, concat_axis=0, tiled=True)


def per_device(hidden_in, spatial_qkv, temporal_qkv, teacher_target, spatial_proj, temporal_proj):
    at_x, at_core, at_y = (lax.axis_index(a) for a in ("x", "core", "y"))
    place = jnp.stack([at_x, at_core, at_y]).astype(jnp.int32)

    sent = temporal_qkv.reshape(2, 32, 2, 3 * D).transpose(1, 0, 2, 3).reshape(32, 4, 3 * D)
    time_x = exchange(sent, SEQ).reshape(TOKENS, 3 * D)

    rows = jnp.where(at_core == 0, spatial_proj, temporal_proj)
    gathered = exchange(jnp.broadcast_to(rows[None], (8, 36, D)), "z").reshape(288, D)
    own = [gathered] + [shift(gathered, "x", 4, k) for k in (1, 2, 3)]
    other = [swap(block) for block in own]

    space_x = spatial_qkv.reshape(TOKENS, 3 * D)
    space_mix, space_probs = attend(space_x, False)
    time_mix_sent, time_probs = attend(time_x, True)
    time_mix = exchange(time_mix_sent.reshape(32, 4, D), SEQ).reshape(TOKENS, D)

    resid, space_grad, time_grad, time_mix = project(
        place,
        hidden_in.reshape(TOKENS, D),
        teacher_target.reshape(TOKENS, D),
        space_mix,
        time_mix,
        own,
        other,
    )
    time_back = exchange(time_grad.reshape(32, 4, D + LANES), SEQ)

    resids = jnp.stack([resid] + [shift(resid, "y", 4, k) for k in (1, 2, 3)])
    resids_other = swap(resids)
    mixes = exchange(choose(space_mix, time_mix), DP)

    total = jnp.sum(time_back[:, 0, D : D + 3].astype(F32))
    spread = jnp.sqrt(total / CELLS + HUBER_DELTA**2)
    clip_loss = (spread - HUBER_DELTA).reshape(1)
    inv = (1.0 / spread).reshape(1)
    invs = exchange(jnp.broadcast_to(inv, (8, 1, LANES)), DP)[:, 0, 0]

    time_out = attend_back(
        inv, time_x, time_probs, time_back.reshape(TOKENS, D + LANES), "attend_back_time"
    )
    time_out = exchange(time_out.reshape(32, 4, 3 * D), SEQ)
    temporal_qkv_grad = time_out.reshape(32, 2, 2, 3 * D).transpose(1, 0, 2, 3)

    spatial_qkv_grad = attend_back(inv, space_x, space_probs, space_grad, "attend_back_space")

    partial = weight_grad(place, invs, mixes, resids, resids_other)
    summed = sum(
        [partial[0].astype(F32)] + [shift(partial[k], "x", 4, k).astype(F32) for k in (1, 2, 3)]
    ).astype(BF16)
    pieces = exchange(summed.reshape(8, 9, D), "z")
    piece = jnp.sum(pieces.astype(F32), axis=0).astype(BF16)
    blocks = exchange(jnp.broadcast_to(piece[None], (8, 9, D)), DP)
    blocks = blocks.reshape(4, 2, 9, D).astype(F32)
    return (
        clip_loss,
        spatial_qkv_grad.reshape(1, 2, 64, 3 * D),
        temporal_qkv_grad.reshape(1, 2, 64, 3 * D),
        blocks[:, 0].reshape(36, D),
        blocks[:, 1].reshape(36, D),
    )


def solution(mesh):
    fine = Mesh(mesh.devices.reshape(4, 2, 4, 8), ("y", "core", "x", "z"))
    clips = P(DP, SEQ, None, None)
    weight = P(SEQ, None)
    return jax.shard_map(
        per_device,
        mesh=fine,
        in_specs=(clips, clips, clips, clips, weight, weight),
        out_specs=(P(DP), clips, clips, weight, weight),
        check_vma=False,
    )
```

time: 583 us -> 246 us (0.42)
  blocking collectives: 176 us -> 13.7 us
  waiting for transfers between devices: 190 us -> 89 us
  local copies, waits for them, and re-layouts: 67.3 us -> 29.3 us
  matrix products: 37 us -> 0 us
  Pallas kernels: 0 us -> 27.3 us
  between operations: 16.9 us -> 2.89 us
  starting transfers between devices: 90.4 us -> 77 us
    all_gather x2 -> x0, waiting for transfers between devices: 90 us -> none  [the longest x1 75.2 us: per_device(): lax.all_gather(temporal_proj, 'seq', axis=0, tiled=True)]
    unnamed x1 -> x0, blocking collectives: 85.9 us -> none
    unnamed x22 -> x0, waiting for transfers between devices: 72.6 us -> none
    unnamed x18 -> x0, starting transfers between devices: 61 us -> none
    psum x1 -> x0, blocking collectives: 58.7 us -> none  [pseudo_huber(): totals = lax.psum(partial_sums, 'seq')]
    ppermute x0 -> x14, waiting for transfers between devices: none -> 36.1 us  [the longest x9 36.1 us: shift(): lax.ppermute(value, axis, [(i, (i + step) % size) for i in range(size)])]
    dot_general x16 -> x0, matrix products: 33.5 us -> none  [the longest x2 6.2 us: attend_back(): jnp.einsum('nhqk,nqhe->nkhe', score_grad, queries, preferred_element_type...]
    all_gather x2 -> x0, blocking collectives: 31.2 us -> none  [the longest x1 15.6 us: per_device(): lax.all_gather(space_piece.astype(jnp.bfloat16), 'dp', axis=1, tiled=True)]
  transfers between devices with their start and end apart: 24 -> 22, of which waited for: 7 -> 10; matrix products, arithmetic and copies ran while one was open for 29% -> 7% of each run, Pallas kernels for 0% -> 8%
where the time goes in v1:
time: 246 us; the launch traced here: 243 us
  waiting for transfers between devices  89 us (36%)
  starting transfers between devices  77 us (31%)
  local copies, waits for them, and re-layouts  29.3 us (12%)
  Pallas kernels  27.3 us (11%)
  blocking collectives  13.7 us (6%)
  other arithmetic  3.93 us (2%)
  between operations  2.89 us (1%)
    all_to_all x8, waiting for transfers between devices, exchange(): return lax.all_to_all(value, axis, split_axis=0, concat_axis=0, tiled=True)  52.9 us
    all_to_all x8, starting transfers between devices, exchange(): return lax.all_to_all(value, axis, split_axis=0, concat_axis=0, tiled=True)  47.7 us
    ppermute x9, waiting for transfers between devices, shift(): lax.ppermute(value, axis, [(i, (i + step) % size) for i in range(size)])  36.1 us
    ppermute x5, starting transfers between devices, swap(): return lax.ppermute(value, 'core', [(0, 1), (1, 0)])  18.3 us
    all_to_all x1, blocking collectives, exchange(): return lax.all_to_all(value, axis, split_axis=0, concat_axis=0, tiled=True)  13.7 us
    ppermute x9, starting transfers between devices, shift(): lax.ppermute(value, axis, [(i, (i + step) % size) for i in range(size)])  11 us
    pallas_call x2, Pallas kernels, attend_back(): pl.pallas_call(attend_back_kernel, out_shape=jax.ShapeDtypeStruct((TOKENS...  10.2 us
    unnamed x32, local copies, waits for them, and re-layouts  9.05 us
  transfers between devices with their start and end apart: 22, of which 10 were waited for; matrix products, arithmetic and copies ran while one was open for 7% of the time, Pallas kernels for 8%

profile of v1, /device:TPU:1, one launch (start us, length us, event | category | flops | bytes accessed | tf_op | source)
XLA Modules:
  0.0 243.1 jit_solution(2696431587769534531)
XLA Ops:
  2.5 9.0 %all-to-all-start.2 = ((bf16[8,36,1152]{2,1,0:T(8,128)(2,1)}), bf16[8,36,1152]{2,1,0:T(8,128)(2,1)S(1)}, u32[]{:S(2)}, u32[]{:S(2)}) async-start(bf16[8,36,1152]{2,1,0:T(8,128)(2,1)} %broadcast_in_dim.6), calls=%async_computation.2 | async-start | bytes 1474560 | tf_op jit(solution)/shard_map/all_to_all | solution.py:250
  12.5 1.2 reshape.76
  13.7 20.3 %all-to-all-done.2 = bf16[8,36,1152]{2,1,0:T(8,128)(2,1)S(1)} async-done(((bf16[8,36,1152]{2,1,0:T(8,128)(2,1)}), bf16[8,36,1152]{2,1,0:T(8,128)(2,1)S(1)}, u32[]{:S(2)}, u32[]{:S(2)}) %all-to-all-start.2) | async-done | bytes 663584 | tf_op jit(solution)/shard_map/all_to_all | solution.py:250
  34.0 4.4 %all-to-all-start = ((bf16[32,4,3456]{2,1,0:T(4,128)(2,1)}), bf16[32,4,3456]{2,1,0:T(4,128)(2,1)S(1)}, u32[]{:S(2)}, u32[]{:S(2)}) async-start(bf16[32,4,3456]{2,1,0:T(4,128)(2,1)} %reshape.76), calls=%async_computation | async-start | bytes 1769472 | tf_op jit(solution)/shard_map/all_to_all | solution.py:250
  38.6 2.6 %collective-permute-start.2 = (bf16[288,1152]{1,0:T(8,128)(2,1)S(1)}, bf16[288,1152]{1,0:T(8,128)(2,1)}, u32[]{:S(2)}, u32[]{:S(2)}) collective-permute-start(bf16[288,1152]{1,0:T(8,128)(2,1)S(1)} %reshape.80.rest_0_), channel_id=1, source_target_pairs={{0,24},{8,0},{16,8},{24,16},{1,25},{9,1},{17,9},{25,17},{2,26},{10... | collective-permute-start | bytes 1990664 | tf_op jit(solution)/shard_map/ppermute | solution.py:242
  42.3 1.9 collective-permute-start.3
  44.2 20.1 %collective-permute-done.2.rest_3_ = bf16[288,1152]{1,0:T(8,128)(2,1)} collective-permute-done((bf16[288,1152]{1,0:T(8,128)(2,1)S(1)}, bf16[288,1152]{1,0:T(8,128)(2,1)}, u32[]{:S(2)}, u32[]{:S(2)}) %collective-permute-start.2) | collective-permute-done | bytes 663584 | tf_op jit(solution)/shard_map/ppermute | solution.py:242
  64.2 14.9 %collective-permute-start.6 = (bf16[288,1152]{1,0:T(8,128)(2,1)}, bf16[288,1152]{1,0:T(8,128)(2,1)}, u32[]{:S(2)}, u32[]{:S(2)}) collective-permute-start(bf16[288,1152]{1,0:T(8,128)(2,1)} %collective-permute-done.2.rest_3_), channel_id=1, source_target_pairs={{0,32},{32,0},{1,33},{33,1},{2,34},{34,2},{3,35},{35,3},{4,36},{36... | collective-permute-start | bytes 1990664 | tf_op jit(solution)/shard_map/ppermute | solution.py:246
  79.1 2.3 collective-permute-done.rest_1_
  82.2 3.1 %attend_time.1 = (bf16[128,1152]{1,0:T(8,128)(2,1)S(1)}, f32[16,128,128]{2,1,0:T(8,128)S(1)}) custom-call(bf16[128,3456]{1,0:T(8,128)(2,1)S(1)} %reshape.77.x_ref), custom_call_target="tpu_custom_call" | custom-call | tf_op jit(solution)/shard_map/attend_time/pallas_call | solution.py:95
  85.3 1.0 copy-done.5
  87.0 7.5 %all-to-all-start.1 = ((bf16[32,4,1152]{2,1,0:T(4,128)(2,1)}), bf16[32,4,1152]{2,1,0:T(4,128)(2,1)}, u32[]{:S(2)}, u32[]{:S(2)}) async-start(bf16[32,4,1152]{2,1,0:T(4,128)(2,1)} %reshape.78), calls=%async_computation.1 | async-start | bytes 589824 | tf_op jit(solution)/shard_map/all_to_all | solution.py:250
  94.5 3.1 %attend_space.1 = (bf16[128,1152]{1,0:T(8,128)(2,1)S(1)}, f32[16,128,128]{2,1,0:T(8,128)S(1)}) custom-call(bf16[128,3456]{1,0:T(8,128)(2,1)S(1)} %bitcast.36), custom_call_target="tpu_custom_call" | custom-call | tf_op jit(solution)/shard_map/attend_space/pallas_call | solution.py:95
  97.6 1.0 copy-done.3
  98.7 6.2 %all-to-all-done.1 = bf16[32,4,1152]{2,1,0:T(4,128)(2,1)} async-done(((bf16[32,4,1152]{2,1,0:T(4,128)(2,1)}), bf16[32,4,1152]{2,1,0:T(4,128)(2,1)}, u32[]{:S(2)}, u32[]{:S(2)}) %all-to-all-start.1) | async-done | bytes 294944 | tf_op jit(solution)/shard_map/all_to_all | solution.py:250
  104.9 1.0 reshape.79.time_ref
  106.0 1.0 copy-done.9
  106.9 6.0 %project.1 = (bf16[128,1152]{1,0:T(8,128)(2,1)}, bf16[128,1152]{1,0:T(8,128)(2,1)S(1)}, bf16[128,1280]{1,0:T(8,128)(2,1)S(1)}, bf16[128,1152]{1,0:T(8,128)(2,1)S(1)}) custom-call(s32[3]{0:T(128)S(1)} %pad_add_fusion.place_ref, bf16[128,1152]{1,0:T(8,128)(2,1)S(1)} %bitcast.38, bf16[128,1152]{1,0:T(8,128)(2,1)S(1)} %bitcast.39, ...), custom_call_target="tpu_custom_call" | custom-call | tf_op jit(solution)/shard_map/project/pallas_call | solution.py:179
  115.1 2.7 %collective-permute-start.9 = (bf16[128,1152]{1,0:T(8,128)(2,1)}, bf16[128,1152]{1,0:T(8,128)(2,1)S(1)}, u32[]{:S(2)}, u32[]{:S(2)}) collective-permute-start(bf16[128,1152]{1,0:T(8,128)(2,1)} %get-tuple-element.20), channel_id=1, source_target_pairs={{0,192},{64,0},{128,64},{192,128},{1,193},{65,1},{129,65},{193,129... | collective-permute-start | bytes 884744 | tf_op jit(solution)/shard_map/ppermute | solution.py:242
  118.9 1.8 reshape.81
  120.7 6.9 %all-to-all-start.3 = ((bf16[32,4,1280]{2,1,0:T(4,128)(2,1)}), bf16[32,4,1280]{2,1,0:T(4,128)(2,1)}, u32[]{:S(2)}, u32[]{:S(2)}) async-start(bf16[32,4,1280]{2,1,0:T(4,128)(2,1)} %reshape.81), calls=%async_computation.3 | async-start | bytes 655360 | tf_op jit(solution)/shard_map/all_to_all | solution.py:250
  127.6 6.8 %collective-permute-done.7 = bf16[128,1152]{1,0:T(8,128)(2,1)S(1)} collective-permute-done((bf16[128,1152]{1,0:T(8,128)(2,1)}, bf16[128,1152]{1,0:T(8,128)(2,1)S(1)}, u32[]{:S(2)}, u32[]{:S(2)}) %collective-permute-start.7) | collective-permute-done | bytes 294944 | tf_op jit(solution)/shard_map/ppermute | solution.py:242
  135.1 1.4 pad_maximum_fusion.own_ref
  136.5 1.0 collective-permute-start.10
  137.5 1.9 choose.1
  140.3 2.2 copy.33
  142.5 3.5 %all-to-all-start.6 = ((bf16[8,128,288]{1,2,0:T(8,128)(2,1)}), bf16[8,128,288]{1,2,0:T(8,128)(2,1)S(1)}, u32[]{:S(2)}, u32[]{:S(2)}) async-start(bf16[8,128,288]{1,2,0:T(8,128)(2,1)} %copy.33), calls=%async_computation.6 | async-start | bytes 1179648 | tf_op jit(solution)/shard_map/all_to_all | solution.py:250
  146.0 1.4 fusion.3
  148.2 8.0 %all-to-all-done.6 = bf16[8,128,288]{1,2,0:T(8,128)(2,1)S(1)} async-done(((bf16[8,128,288]{1,2,0:T(8,128)(2,1)}), bf16[8,128,288]{1,2,0:T(8,128)(2,1)S(1)}, u32[]{:S(2)}, u32[]{:S(2)}) %all-to-all-start.6) | async-done | bytes 589856 | tf_op jit(solution)/shard_map/all_to_all | solution.py:250
  156.8 4.1 %all-to-all-start.5 = ((f32[8,1,128]{2,1,0:T(1,128)}), f32[8,1,128]{2,1,0:T(1,128)S(1)}, u32[]{:S(2)}, u32[]{:S(2)}) async-start(f32[8,1,128]{2,1,0:T(1,128)} %broadcast_in_dim.7), calls=%async_computation.5 | async-start | bytes 8192 | tf_op jit(solution)/shard_map/all_to_all | solution.py:250
  160.9 1.2 copy.34.mix_ref
  162.0 3.4 %all-to-all-done.5 = f32[8,1,128]{2,1,0:T(1,128)S(1)} async-done(((f32[8,1,128]{2,1,0:T(1,128)}), f32[8,1,128]{2,1,0:T(1,128)S(1)}, u32[]{:S(2)}, u32[]{:S(2)}) %all-to-all-start.5) | async-done | bytes 4128 | tf_op jit(solution)/shard_map/all_to_all | solution.py:250
  165.5 1.1 copy-done.1
  166.7 3.0 %weight_grad.1 = bf16[4,72,1152]{2,1,0:T(8,128)(2,1)S(1)} custom-call(s32[3]{0:T(128)S(1)} %pad_add_fusion.place_ref, f32[8]{0:T(128)S(1)} %slice_reduce_fusion.inv_ref, bf16[8,128,288]{2,1,0:T(8,128)(2,1)S(1)} %copy-done.1, bf16[4,128,1152]{2,1,0:T(8,128)(2,1)S(1)} %pad_maximum_fusion.own_ref, bf16[4,128,1152]{2,1,0:T(8,128)(2,1)} %collective-permute-done.10.other_ref), custom_call_target="tpu_custom_call" | custom-call | tf_op jit(solution)/shard_map/weight_grad/pallas_call | solution.py:231
  170.4 2.1 collective-permute-start.13
  173.4 2.8 %collective-permute-done.11 = bf16[72,1152]{1,0:T(8,128)(2,1)S(1)} collective-permute-done((bf16[72,1152]{1,0:T(8,128)(2,1)S(1)}, bf16[72,1152]{1,0:T(8,128)(2,1)S(1)}, u32[]{:S(2)}, u32[]{:S(2)}) %collective-permute-start.11) | collective-permute-done | bytes 165920 | tf_op jit(solution)/shard_map/ppermute | solution.py:242
  176.1 4.1 %collective-permute-done.12 = bf16[72,1152]{1,0:T(8,128)(2,1)S(1)} collective-permute-done((bf16[72,1152]{1,0:T(8,128)(2,1)S(1)}, bf16[72,1152]{1,0:T(8,128)(2,1)S(1)}, u32[]{:S(2)}, u32[]{:S(2)}) %collective-permute-start.12) | collective-permute-done | bytes 165920 | tf_op jit(solution)/shard_map/ppermute | solution.py:242
  180.4 13.7 %all_to_all.45 = bf16[8,9,1152]{2,1,0:T(8,128)(2,1)S(1)} all-to-all(bf16[8,9,1152]{2,1,0:T(8,128)(2,1)S(1)} %reshape.89), channel_id=1, replica_groups=mesh['y'=4,'core'=2,'x'=4,'z'=8] {'z'}, dimensions={0} | all-to-all | bytes 331776 | tf_op jit(solution)/shard_map/all_to_all | solution.py:250
  194.9 7.2 %all-to-all-start.8 = ((bf16[8,9,1152]{2,1,0:T(8,128)(2,1)}), bf16[8,9,1152]{2,1,0:T(8,128)(2,1)S(1)}, u32[]{:S(2)}, u32[]{:S(2)}) async-start(bf16[8,9,1152]{2,1,0:T(8,128)(2,1)} %broadcast_in_dim.8), calls=%async_computation.8 | async-start | bytes 589824 | tf_op jit(solution)/shard_map/all_to_all | solution.py:250
  202.1 1.1 reshape.85.grad_ref
  203.2 1.2 copy-done.6
  204.4 4.6 %attend_back_time.1 = bf16[128,3456]{1,0:T(8,128)(2,1)S(1)} custom-call(f32[1]{0:T(128)} %bitcast.8.inv_ref, bf16[128,3456]{1,0:T(8,128)(2,1)S(1)} %reshape.77.x_ref, f32[16,128,128]{2,1,0:T(8,128)S(1)} %copy-done.6, bf16[128,1280]{1,0:T(8,128)(2,1)S(1)} %reshape.85.grad_ref), custom_call_target="tpu_custom_call" | custom-call | tf_op jit(solution)/shard_map/attend_back_time/pallas_call | solution.py:129
  209.1 1.1 reshape.86
  210.2 5.0 %all-to-all-start.4 = ((bf16[32,4,3456]{2,1,0:T(4,128)(2,1)}), bf16[32,4,3456]{2,1,0:T(4,128)(2,1)}, u32[]{:S(2)}, u32[]{:S(2)}) async-start(bf16[32,4,3456]{2,1,0:T(4,128)(2,1)} %reshape.86), calls=%async_computation.4 | async-start | bytes 1769472 | tf_op jit(solution)/shard_map/all_to_all | solution.py:250
  215.3 5.6 %attend_back_space.1 = bf16[128,3456]{1,0:T(8,128)(2,1)} custom-call(f32[1]{0:T(128)} %bitcast.8.inv_ref, bf16[128,3456]{1,0:T(8,128)(2,1)S(1)} %bitcast.37, f32[16,128,128]{2,1,0:T(8,128)S(1)} %copy-done.4, bf16[128,1152]{1,0:T(8,128)(2,1)S(1)} %copy-done.11), custom_call_target="tpu_custom_call" | custom-call | tf_op jit(solution)/shard_map/attend_back_space/pallas_call | solution.py:129
  222.8 15.0 %all-to-all-done.4 = bf16[32,4,3456]{2,1,0:T(4,128)(2,1)} async-done(((bf16[32,4,3456]{2,1,0:T(4,128)(2,1)}), bf16[32,4,3456]{2,1,0:T(4,128)(2,1)}, u32[]{:S(2)}, u32[]{:S(2)}) %all-to-all-start.4) | async-done | bytes 884768 | tf_op jit(solution)/shard_map/all_to_all | solution.py:250
  237.8 2.3 reshape.87
  240.7 1.2 reshape.88
  (70 shorter events, 16.2 us)
Async XLA Ops:
  1.6 9.9 %copy-start.14 = (bf16[1,2,64,3456]{3,2,1,0:T(8,128)(2,1)S(1)}, bf16[1,2,64,3456]{3,2,1,0:T(8,128)(2,1)}, u32[]{:S(2)}) copy-start(bf16[1,2,64,3456]{3,2,1,0:T(8,128)(2,1)} %param.8) | copy-start | bytes 2654212
  2.5 31.5 %all-to-all-start.2 = ((bf16[8,36,1152]{2,1,0:T(8,128)(2,1)}), bf16[8,36,1152]{2,1,0:T(8,128)(2,1)S(1)}, u32[]{:S(2)}, u32[]{:S(2)}) async-start(bf16[8,36,1152]{2,1,0:T(8,128)(2,1)} %broadcast_in_dim.6), calls=%async_computation.2 | async-start | bytes 1474560 | tf_op jit(solution)/shard_map/all_to_all | solution.py:250
  34.0 47.9 %all-to-all-start = ((bf16[32,4,3456]{2,1,0:T(4,128)(2,1)}), bf16[32,4,3456]{2,1,0:T(4,128)(2,1)S(1)}, u32[]{:S(2)}, u32[]{:S(2)}) async-start(bf16[32,4,3456]{2,1,0:T(4,128)(2,1)} %reshape.76), calls=%async_computation | async-start | bytes 1769472 | tf_op jit(solution)/shard_map/all_to_all | solution.py:250
  38.6 25.6 %collective-permute-start.2 = (bf16[288,1152]{1,0:T(8,128)(2,1)S(1)}, bf16[288,1152]{1,0:T(8,128)(2,1)}, u32[]{:S(2)}, u32[]{:S(2)}) collective-permute-start(bf16[288,1152]{1,0:T(8,128)(2,1)S(1)} %reshape.80.rest_0_), channel_id=1, source_target_pairs={{0,24},{8,0},{16,8},{24,16},{1,25},{9,1},{17,9},{25,17},{2,26},{10... | collective-permute-start | bytes 1990664 | tf_op jit(solution)/shard_map/ppermute | solution.py:242
  41.1 38.0 %collective-permute-start.1 = (bf16[288,1152]{1,0:T(8,128)(2,1)S(1)}, bf16[288,1152]{1,0:T(8,128)(2,1)}, u32[]{:S(2)}, u32[]{:S(2)}) collective-permute-start(bf16[288,1152]{1,0:T(8,128)(2,1)S(1)} %reshape.80.rest_0_), channel_id=1, source_target_pairs={{0,16},{8,24},{16,0},{24,8},{1,17},{9,25},{17,1},{25,9},{2,18},{10... | collective-permute-start | bytes 1990664 | tf_op jit(solution)/shard_map/ppermute | solution.py:242
  41.7 39.8 %collective-permute-start = (bf16[288,1152]{1,0:T(8,128)(2,1)S(1)}, bf16[288,1152]{1,0:T(8,128)(2,1)}, u32[]{:S(2)}, u32[]{:S(2)}) collective-permute-start(bf16[288,1152]{1,0:T(8,128)(2,1)S(1)} %reshape.80.rest_0_), channel_id=1, source_target_pairs={{0,8},{8,16},{16,24},{24,0},{1,9},{9,17},{17,25},{25,1},{2,10},{10... | collective-permute-start | bytes 1990664 | tf_op jit(solution)/shard_map/ppermute | solution.py:242
  42.3 63.6 %collective-permute-start.3 = (bf16[288,1152]{1,0:T(8,128)(2,1)S(1)}, bf16[288,1152]{1,0:T(8,128)(2,1)}, u32[]{:S(2)}, u32[]{:S(2)}) collective-permute-start(bf16[288,1152]{1,0:T(8,128)(2,1)S(1)} %reshape.80.rest_0_), channel_id=1, source_target_pairs={{0,32},{32,0},{1,33},{33,1},{2,34},{34,2},{3,35},{35,3},{4,36},{36... | collective-permute-start | bytes 1990664 | tf_op jit(solution)/shard_map/ppermute | solution.py:246
  64.2 41.7 %collective-permute-start.6 = (bf16[288,1152]{1,0:T(8,128)(2,1)}, bf16[288,1152]{1,0:T(8,128)(2,1)}, u32[]{:S(2)}, u32[]{:S(2)}) collective-permute-start(bf16[288,1152]{1,0:T(8,128)(2,1)} %collective-permute-done.2.rest_3_), channel_id=1, source_target_pairs={{0,32},{32,0},{1,33},{33,1},{2,34},{34,2},{3,35},{35,3},{4,36},{36... | collective-permute-start | bytes 1990664 | tf_op jit(solution)/shard_map/ppermute | solution.py:246
  79.1 26.8 %collective-permute-start.5 = (bf16[288,1152]{1,0:T(8,128)(2,1)}, bf16[288,1152]{1,0:T(8,128)(2,1)}, u32[]{:S(2)}, u32[]{:S(2)}) collective-permute-start(bf16[288,1152]{1,0:T(8,128)(2,1)} %collective-permute-done.1.rest_2_), channel_id=1, source_target_pairs={{0,32},{32,0},{1,33},{33,1},{2,34},{34,2},{3,35},{35,3},{4,36},{36... | collective-permute-start | bytes 1990664 | tf_op jit(solution)/shard_map/ppermute | solution.py:246
  81.5 24.5 %collective-permute-start.4 = (bf16[288,1152]{1,0:T(8,128)(2,1)}, bf16[288,1152]{1,0:T(8,128)(2,1)}, u32[]{:S(2)}, u32[]{:S(2)}) collective-permute-start(bf16[288,1152]{1,0:T(8,128)(2,1)} %collective-permute-done.rest_1_), channel_id=1, source_target_pairs={{0,32},{32,0},{1,33},{33,1},{2,34},{34,2},{3,35},{35,3},{4,36},{36... | collective-permute-start | bytes 1990664 | tf_op jit(solution)/shard_map/ppermute | solution.py:246
  82.2 12.4 %copy-start = (bf16[1,2,64,3456]{3,2,1,0:T(8,128)(2,1)S(1)}, bf16[1,2,64,3456]{3,2,1,0:T(8,128)(2,1)}, u32[]{:S(2)}) copy-start(bf16[1,2,64,3456]{3,2,1,0:T(8,128)(2,1)} %param.7) | copy-start | bytes 2654212
  85.3 1.0 copy-start.5
  87.0 18.9 %copy-start.8 = (bf16[1,2,64,1152]{3,2,1,0:T(8,128)(2,1)S(1)}, bf16[1,2,64,1152]{3,2,1,0:T(8,128)(2,1)}, u32[]{:S(2)}) copy-start(bf16[1,2,64,1152]{3,2,1,0:T(8,128)(2,1)} %param.6) | copy-start | bytes 884740
  87.0 17.8 %all-to-all-start.1 = ((bf16[32,4,1152]{2,1,0:T(4,128)(2,1)}), bf16[32,4,1152]{2,1,0:T(4,128)(2,1)}, u32[]{:S(2)}, u32[]{:S(2)}) async-start(bf16[32,4,1152]{2,1,0:T(4,128)(2,1)} %reshape.78), calls=%async_computation.1 | async-start | bytes 589824 | tf_op jit(solution)/shard_map/all_to_all | solution.py:250
  97.6 1.0 copy-start.3
  106.0 1.0 copy-start.9
  112.9 0.7 copy-start.7
  113.7 0.7 copy-start.10
  114.4 0.7 copy-start.12
  115.1 12.5 %collective-permute-start.9 = (bf16[128,1152]{1,0:T(8,128)(2,1)}, bf16[128,1152]{1,0:T(8,128)(2,1)S(1)}, u32[]{:S(2)}, u32[]{:S(2)}) collective-permute-start(bf16[128,1152]{1,0:T(8,128)(2,1)} %get-tuple-element.20), channel_id=1, source_target_pairs={{0,192},{64,0},{128,64},{192,128},{1,193},{65,1},{129,65},{193,129... | collective-permute-start | bytes 884744 | tf_op jit(solution)/shard_map/ppermute | solution.py:242
  117.9 9.8 %collective-permute-start.8 = (bf16[128,1152]{1,0:T(8,128)(2,1)}, bf16[128,1152]{1,0:T(8,128)(2,1)}, u32[]{:S(2)}, u32[]{:S(2)}) collective-permute-start(bf16[128,1152]{1,0:T(8,128)(2,1)} %get-tuple-element.20), channel_id=1, source_target_pairs={{0,128},{64,192},{128,0},{192,64},{1,129},{65,193},{129,1},{193,65... | collective-permute-start | bytes 884744 | tf_op jit(solution)/shard_map/ppermute | solution.py:242
  118.2 16.2 %collective-permute-start.7 = (bf16[128,1152]{1,0:T(8,128)(2,1)}, bf16[128,1152]{1,0:T(8,128)(2,1)S(1)}, u32[]{:S(2)}, u32[]{:S(2)}) collective-permute-start(bf16[128,1152]{1,0:T(8,128)(2,1)} %get-tuple-element.20), channel_id=1, source_target_pairs={{0,64},{64,128},{128,192},{192,0},{1,65},{65,129},{129,193},{193,1... | collective-permute-start | bytes 884744 | tf_op jit(solution)/shard_map/ppermute | solution.py:242
  120.7 21.9 %all-to-all-start.3 = ((bf16[32,4,1280]{2,1,0:T(4,128)(2,1)}), bf16[32,4,1280]{2,1,0:T(4,128)(2,1)}, u32[]{:S(2)}, u32[]{:S(2)}) async-start(bf16[32,4,1280]{2,1,0:T(4,128)(2,1)} %reshape.81), calls=%async_computation.3 | async-start | bytes 655360 | tf_op jit(solution)/shard_map/all_to_all | solution.py:250
  134.4 0.7 copy-start.15
  135.1 2.4 copy-start.13
  136.5 29.0 %collective-permute-start.10 = (bf16[4,128,1152]{2,1,0:T(8,128)(2,1)S(1)}, bf16[4,128,1152]{2,1,0:T(8,128)(2,1)}, u32[]{:S(2)}, u32[]{:S(2)}) collective-permute-start(bf16[4,128,1152]{2,1,0:T(8,128)(2,1)S(1)} %pad_maximum_fusion.own_ref), channel_id=1, source_target_pairs={{0,32},{32,0},{1,33},{33,1},{2,34},{34,2},{3,35},{35,3},{4,36},{36... | collective-permute-start | bytes 3538952 | tf_op jit(solution)/shard_map/ppermute | solution.py:246
  139.4 0.9 copy-start.2
  142.5 13.7 %all-to-all-start.6 = ((bf16[8,128,288]{1,2,0:T(8,128)(2,1)}), bf16[8,128,288]{1,2,0:T(8,128)(2,1)S(1)}, u32[]{:S(2)}, u32[]{:S(2)}) async-start(bf16[8,128,288]{1,2,0:T(8,128)(2,1)} %copy.33), calls=%async_computation.6 | async-start | bytes 1179648 | tf_op jit(solution)/shard_map/all_to_all | solution.py:250
  156.8 8.6 %all-to-all-start.5 = ((f32[8,1,128]{2,1,0:T(1,128)}), f32[8,1,128]{2,1,0:T(1,128)S(1)}, u32[]{:S(2)}, u32[]{:S(2)}) async-start(f32[8,1,128]{2,1,0:T(1,128)} %broadcast_in_dim.7), calls=%async_computation.5 | async-start | bytes 8192 | tf_op jit(solution)/shard_map/all_to_all | solution.py:250
  165.5 1.1 copy-start.1
  169.8 6.4 %collective-permute-start.11 = (bf16[72,1152]{1,0:T(8,128)(2,1)S(1)}, bf16[72,1152]{1,0:T(8,128)(2,1)S(1)}, u32[]{:S(2)}, u32[]{:S(2)}) collective-permute-start(bf16[72,1152]{1,0:T(8,128)(2,1)S(1)} %get-tuple-element.21), channel_id=1, source_target_pairs={{0,8},{8,16},{16,24},{24,0},{1,9},{9,17},{17,25},{25,1},{2,10},{10... | collective-permute-start | bytes 497672 | tf_op jit(solution)/shard_map/ppermute | solution.py:242
  170.4 5.7 %collective-permute-start.13 = (bf16[72,1152]{1,0:T(8,128)(2,1)S(1)}, bf16[72,1152]{1,0:T(8,128)(2,1)S(1)}, u32[]{:S(2)}, u32[]{:S(2)}) collective-permute-start(bf16[72,1152]{1,0:T(8,128)(2,1)S(1)} %get-tuple-element.22), channel_id=1, source_target_pairs={{0,24},{8,0},{16,8},{24,16},{1,25},{9,1},{17,9},{25,17},{2,26},{10... | collective-permute-start | bytes 497672 | tf_op jit(solution)/shard_map/ppermute | solution.py:242
  172.5 7.7 %collective-permute-start.12 = (bf16[72,1152]{1,0:T(8,128)(2,1)S(1)}, bf16[72,1152]{1,0:T(8,128)(2,1)S(1)}, u32[]{:S(2)}, u32[]{:S(2)}) collective-permute-start(bf16[72,1152]{1,0:T(8,128)(2,1)S(1)} %get-tuple-element.23), channel_id=1, source_target_pairs={{0,16},{8,24},{16,0},{24,8},{1,17},{9,25},{17,1},{25,9},{2,18},{10... | collective-permute-start | bytes 497672 | tf_op jit(solution)/shard_map/ppermute | solution.py:242
  194.9 15.3 %all-to-all-start.8 = ((bf16[8,9,1152]{2,1,0:T(8,128)(2,1)}), bf16[8,9,1152]{2,1,0:T(8,128)(2,1)S(1)}, u32[]{:S(2)}, u32[]{:S(2)}) async-start(bf16[8,9,1152]{2,1,0:T(8,128)(2,1)} %broadcast_in_dim.8), calls=%async_computation.8 | async-start | bytes 589824 | tf_op jit(solution)/shard_map/all_to_all | solution.py:250
  203.2 1.2 copy-start.6
  210.2 5.1 %copy-start.4 = (f32[16,128,128]{2,1,0:T(8,128)S(1)}, f32[16,128,128]{2,1,0:T(8,128)}, u32[]{:S(2)}) copy-start(f32[16,128,128]{2,1,0:T(8,128)} %copy-done.3) | copy-start | bytes 3145732
  210.2 5.1 %copy-start.11 = (bf16[128,1152]{1,0:T(8,128)(2,1)S(1)}, bf16[128,1152]{1,0:T(8,128)(2,1)}, u32[]{:S(2)}) copy-start(bf16[128,1152]{1,0:T(8,128)(2,1)} %copy-done.10) | copy-start | bytes 884740
  210.2 27.6 %all-to-all-start.4 = ((bf16[32,4,3456]{2,1,0:T(4,128)(2,1)}), bf16[32,4,3456]{2,1,0:T(4,128)(2,1)}, u32[]{:S(2)}, u32[]{:S(2)}) async-start(bf16[32,4,3456]{2,1,0:T(4,128)(2,1)} %reshape.86), calls=%async_computation.4 | async-start | bytes 1769472 | tf_op jit(solution)/shard_map/all_to_all | solution.py:250

commit v2 on v1

v2 whole, which is shorter than its diff:
```python
import functools

import jax
import jax.numpy as jnp
from jax import lax
from jax.experimental import pallas as pl
from jax.experimental.pallas import tpu as pltpu
from jax.sharding import Mesh, PartitionSpec as P

HEADS = 16
D = 1152
E = D // HEADS
TOKENS = 128
LANES = 128
SEQ = ("x", "z")
DP = ("y", "core")
HUBER_DELTA = 0.03
CELLS = 64 * 64 * D
SCALING = E ** (-0.5)
BF16 = jnp.bfloat16
F32 = jnp.float32
VMEM_BYTES = 63 * 1024 * 1024

NN = (((1,), (0,)), ((), ()))
NT = (((1,), (1,)), ((), ()))
TN = (((0,), (0,)), ((), ()))


def mul(left, right, dims):
    return lax.dot_general(left, right, dims, preferred_element_type=F32)


def window(head):
    low = E * head // LANES
    high = (E * head + E - 1) // LANES + 1
    return low * LANES, high * LANES


def head_mask(head, low, high):
    lane = lax.broadcasted_iota(jnp.int32, (TOKENS, high - low), 1) + low
    return jnp.where((lane >= E * head) & (lane < E * head + E), 1.0, 0.0).astype(BF16)


def same_sequence(temporal):
    row = lax.broadcasted_iota(jnp.int32, (TOKENS, TOKENS), 0)
    col = lax.broadcasted_iota(jnp.int32, (TOKENS, TOKENS), 1)
    if temporal:
        return (row & 1) == (col & 1)
    return (row >> 6) == (col >> 6)


def natural_from_sent():
    nat = lax.broadcasted_iota(jnp.int32, (TOKENS, TOKENS), 0)
    sent = lax.broadcasted_iota(jnp.int32, (TOKENS, TOKENS), 1)
    goes = ((sent >> 1) & 1) * 64 + (sent >> 2) * 2 + (sent & 1)
    return jnp.where(nat == goes, 1.0, 0.0).astype(BF16)


class Tiles:
    def __init__(self, ref, offset, scale=None):
        self.ref, self.offset, self.scale, self.pending = ref, offset, scale, None

    def add(self, head, value):
        low, high = window(head)
        for tile in range(low, high, LANES):
            part = value[:, tile - low : tile - low + LANES]
            if E * head > tile:
                part = self.pending + part
            if E * head + E >= tile + LANES:
                if self.scale is not None:
                    part = part * self.scale
                at = self.offset + tile
                self.ref[:, at : at + LANES] = part.astype(self.ref.dtype)
            else:
                self.pending = part


def attend_heads(temporal, x_ref, mix_ref, probs_ref):
    same = same_sequence(temporal)
    out = Tiles(mix_ref, 0)
    for head in range(HEADS):
        low, high = window(head)
        mask = head_mask(head, low, high)
        queries = x_ref[:, low:high]
        keys = x_ref[:, D + low : D + high] * mask
        values = x_ref[:, 2 * D + low : 2 * D + high] * mask
        scores = jnp.where(same, mul(queries, keys, NT) * SCALING, -1e30)
        powers = jnp.exp(scores - jnp.max(scores, axis=1, keepdims=True))
        probs = powers / jnp.sum(powers, axis=1, keepdims=True)
        probs_ref[head] = probs
        out.add(head, mul(probs.astype(BF16), values, NN))


def attend_space_kernel(place_ref, x_ref, mix_ref, probs_ref, order_ref, mix):
    at_x, at_y, at_z = place_ref[0], place_ref[2], place_ref[3]
    column = lax.broadcasted_iota(jnp.int32, (D, LANES), 0)
    for tile in range(0, D, LANES):
        lane = lax.broadcasted_iota(jnp.int32, (1, LANES), 1) + tile
        block = (lane * 1821) >> 16
        from_z = (at_z + 2 * (((block >> 1) + at_y) & 3) + (block & 1)) & 7
        from_x = ((block >> 3) + at_x) & 3
        source = (from_x * 8 + from_z) * 36 + (lane - block * 36)
        order_ref[:, tile : tile + LANES] = jnp.where(column == source, 1.0, 0.0).astype(BF16)
    attend_heads(False, x_ref, mix, probs_ref)
    mix_ref[...] = mul(mix[...], order_ref[...], NN).astype(BF16)


ROWS = jax.ShapeDtypeStruct((TOKENS, D), BF16)
PROBS = jax.ShapeDtypeStruct((HEADS, TOKENS, TOKENS), F32)


def sent_rows(width):
    return jax.ShapeDtypeStruct((32, 4, width), BF16)


def specs(**places):
    kinds = {"smem": pltpu.SMEM, "vmem": pltpu.VMEM, "any": pl.ANY}
    return [pl.BlockSpec(memory_space=kinds[k]) for k, n in places.items() for _ in range(n)]


def call(kernel, out_shape, in_specs, scratch, name, micros=3, out_specs=None):
    return pl.pallas_call(
        kernel,
        out_shape=out_shape,
        in_specs=in_specs,
        **({} if out_specs is None else {"out_specs": out_specs}),
        scratch_shapes=scratch,
        cost_estimate=pl.CostEstimate(flops=micros * 10**9, bytes_accessed=1, transcendentals=0),
        compiler_params=pltpu.CompilerParams(vmem_limit_bytes=VMEM_BYTES),
        name=name,
    )


def attend_space(place, x):
    order = jax.ShapeDtypeStruct((D, D), BF16)
    return call(
        attend_space_kernel,
        (ROWS, PROBS, order),
        specs(smem=1, vmem=1),
        [pltpu.VMEM((TOKENS, D), BF16)],
        "attend_space",
    )(place, x)


def attend_time_kernel(x_ref, mix_ref, probs_ref, x, mix):
    x[...] = x_ref[...].reshape(TOKENS, 3 * D)
    attend_heads(True, x, mix, probs_ref)
    mix_ref[...] = mix[...].reshape(32, 4, D)


def attend_time(x):
    scratch = [pltpu.VMEM((TOKENS, 3 * D), BF16), pltpu.VMEM((TOKENS, D), BF16)]
    return call(attend_time_kernel, (sent_rows(D), PROBS), specs(vmem=1), scratch, "attend_time")(x)


def send_kernel(x_ref, out_ref):
    out_ref[...] = mul(natural_from_sent(), x_ref[...], TN).astype(BF16).reshape(32, 4, 3 * D)


def send(x):
    return call(send_kernel, sent_rows(3 * D), specs(vmem=1), [], "send_order")(x)


def receive_kernel(x_ref, out_ref):
    x = x_ref[...].reshape(TOKENS, 3 * D)
    out_ref[...] = mul(natural_from_sent(), x, NN).astype(BF16)


def receive(x):
    out = jax.ShapeDtypeStruct((TOKENS, 3 * D), BF16)
    return call(receive_kernel, out, specs(vmem=1), [], "natural_order")(x)


def attend_back_heads(inv, x_ref, probs_ref, grad_ref, out_ref):
    query_out = Tiles(out_ref, 0)
    key_out = Tiles(out_ref, D)
    value_out = Tiles(out_ref, 2 * D, inv)
    for head in range(HEADS):
        low, high = window(head)
        mask = head_mask(head, low, high)
        queries = x_ref[:, low:high] * mask
        keys = x_ref[:, D + low : D + high] * mask
        values = x_ref[:, 2 * D + low : 2 * D + high]
        grads = grad_ref[:, low:high] * mask
        probs = probs_ref[head]
        value_out.add(head, mul(probs.astype(BF16), grads, TN))
        prob_grad = mul(grads, values, NT)
        inner = jnp.sum(prob_grad * probs, axis=1, keepdims=True)
        score_grad = (probs * (prob_grad - inner) * (SCALING * inv)).astype(BF16)
        query_out.add(head, mul(score_grad, keys, NN))
        key_out.add(head, mul(score_grad, queries, TN))


def spread_kernel(grad_ref, spread_ref):
    total = 0.25 * jnp.sum(grad_ref[:, :, D:].reshape(TOKENS, LANES).astype(F32))
    spread_ref[...] = jnp.sqrt(jnp.full((8, LANES), total, F32) / CELLS + HUBER_DELTA**2)


def spread_of(grad):
    out = jax.ShapeDtypeStruct((8, LANES), F32)
    return call(spread_kernel, out, specs(vmem=1), [], "spread", 1)(grad)


def attend_back_time_kernel(x_ref, probs_ref, grad_ref, spread_ref, out_ref, x, grad, out):
    x[...] = x_ref[...].reshape(TOKENS, 3 * D)
    grad[...] = grad_ref[:, :, :D].reshape(TOKENS, D)
    inv = 1.0 / spread_ref[0:1, 0:1]
    attend_back_heads(inv, x, probs_ref, grad, out)
    out_ref[...] = out[...].reshape(32, 4, 3 * D)


def attend_back_time(x, probs, grad, spread):
    wide = pltpu.VMEM((TOKENS, 3 * D), BF16)
    return call(
        attend_back_time_kernel,
        sent_rows(3 * D),
        specs(vmem=4),
        [wide, pltpu.VMEM((TOKENS, D), BF16), wide],
        "attend_back_time",
        5,
    )(x, probs, grad, spread)


def attend_back_space_kernel(x_ref, probs_ref, grad_ref, spread_ref, out_ref):
    attend_back_heads(1.0 / spread_ref[0:1, 0:1], x_ref, probs_ref, grad_ref, out_ref)


def attend_back_space(x, probs, grad, spread):
    return call(
        attend_back_space_kernel,
        jax.ShapeDtypeStruct((TOKENS, 3 * D), BF16),
        specs(vmem=4),
        [],
        "attend_back_space",
        1,
    )(x, probs, grad, spread)


def fetch_weights(refs, weight, sems):
    copies = []
    for a in range(4):
        copy = pltpu.make_async_copy(refs[a], weight.at[pl.ds(288 * a, 288)], sems.at[a])
        copy.start()
        copies.append(copy)
    return copies


def project_kernel(place_ref, time_ref, hidden_any, target_any, space_any, order_any, *rest):
    own_refs, other_refs = rest[0:4], rest[4:8]
    time_grad_ref, space_grad_ref, pack_refs = rest[8], rest[9], rest[10:14]
    weights, hidden_ref, target_ref, space_ref, order_ref, packs, sems = rest[14:]
    at_core = place_ref[1]
    loads = [
        pltpu.make_async_copy(source, place, sems.at[2, n])
        for n, (source, place) in enumerate(
            ((order_any, order_ref), (hidden_any, hidden_ref), (target_any, target_ref), (space_any, space_ref))
        )
    ]
    for copy in loads:
        copy.start()
    copies = fetch_weights(own_refs, weights.at[at_core], sems.at[0])
    copies += fetch_weights(other_refs, weights.at[1 - at_core], sems.at[1])
    natural = natural_from_sent()
    for copy in loads:
        copy.wait()
    time_mix = mul(natural, time_ref[...].reshape(TOKENS, D), NN).astype(BF16)
    time_mix = mul(time_mix, order_ref[...], NN).astype(BF16)
    base = hidden_ref[...].astype(F32) - target_ref[...].astype(F32)
    for copy in copies:
        copy.wait()
    resid = (
        base
        + mul(space_ref[...], weights[0], NN)
        + mul(time_mix, weights[1], NN)
    )
    total = jnp.sum(resid * resid)
    out_grad = resid.astype(BF16)
    time_grad = mul(out_grad, weights[1], NT).astype(BF16)
    time_grad = mul(time_grad, order_ref[...], NT).astype(BF16)
    time_grad = mul(natural, time_grad, TN).astype(BF16)
    lane = lax.broadcasted_iota(jnp.int32, (TOKENS, LANES), 1)
    whole = jnp.full((TOKENS, LANES), total, F32)
    first = whole.astype(BF16).astype(F32)
    second = (whole - first).astype(BF16).astype(F32)
    third = whole - first - second
    parts = jnp.where(lane == 0, first, jnp.where(lane == 1, second, jnp.where(lane == 2, third, 0.0)))
    time_grad_ref[:, :, :D] = time_grad.reshape(32, 4, D)
    time_grad_ref[:, :, D:] = parts.astype(BF16).reshape(32, 4, LANES)
    stores = []
    for a in range(4):
        packs[a, :, :D] = out_grad
        packs[a, :, D:] = jnp.concatenate(
            [space_ref[:, 288 * a : 288 * a + 288], time_mix[:, 288 * a : 288 * a + 288]], axis=1
        )
        stores.append(pltpu.make_async_copy(packs.at[a], pack_refs[a], sems.at[3, a]))
        stores[-1].start()
    space_grad = mul(out_grad, weights[0], NT).astype(BF16)
    space_grad_ref[...] = mul(space_grad, order_ref[...], NT).astype(BF16)
    for copy in stores:
        copy.wait()


def project(place, hidden, target, space_mix, time_mix, order, own, other):
    packed = jax.ShapeDtypeStruct((TOKENS, D + 576), BF16)
    return call(
        project_kernel,
        (sent_rows(D + LANES), ROWS) + (packed,) * 4,
        specs(smem=1, vmem=1, any=12),
        [pltpu.VMEM((2, D, D), BF16)]
        + [pltpu.VMEM((TOKENS, D), BF16)] * 3
        + [
            pltpu.VMEM((D, D), BF16),
            pltpu.VMEM((4, TOKENS, D + 576), BF16),
            pltpu.SemaphoreType.DMA((4, 4)),
        ],
        "project",
        8,
        specs(vmem=2, any=4),
    )(place, time_mix, hidden, target, space_mix, order, *own, *other)


def weight_kernel(place_ref, *rest):
    spread_refs, pack_refs = rest[0:2], rest[2:10]
    out_ref, total = rest[10:]
    first = place_ref[1] == 0
    for n, pack_ref in enumerate(pack_refs):
        inv = 1.0 / spread_refs[n // 4][0:1, 0:1]
        out_grad = (pack_ref[:, :D].astype(F32) * inv).astype(BF16)
        mix = jnp.where(first, pack_ref[:, D : D + 288], pack_ref[:, D + 288 :])
        term = mul(mix, out_grad, TN)
        if n == 0:
            total[...] = term
        else:
            total[...] += term
    out_ref[...] = total[...].astype(BF16)


def weight_grad(place, spreads, packs):
    return call(
        weight_kernel,
        jax.ShapeDtypeStruct((288, D), BF16),
        specs(smem=1, vmem=10),
        [pltpu.VMEM((288, D), F32)],
        "weight_grad",
    )(place, *spreads, *packs)


def finish_kernel(place_ref, own_ref, other_ref, space_ref, time_ref):
    own, other = own_ref[...].astype(F32), other_ref[...].astype(F32)
    first = place_ref[1] == 0
    space_ref[...] = jnp.where(first, own, other)
    time_ref[...] = jnp.where(first, other, own)


def finish(place, own, other):
    rows = jax.ShapeDtypeStruct((36, D), F32)
    return call(finish_kernel, (rows, rows), specs(smem=1, vmem=2), [], "finish")(place, own, other)


def shift_z(value, slope, extra):
    extra = extra if slope > 0 else -extra
    pairs = [(8 * y + z, 8 * y + (z + slope * y + extra) % 8) for y in range(4) for z in range(8)]
    return lax.ppermute(value, ("y", "z"), pairs)


def shift(value, axis, size, step):
    return lax.ppermute(value, axis, [(i, (i + step) % size) for i in range(size)])


def swap(value):
    return lax.ppermute(value, "core", [(0, 1), (1, 0)])


def after(*values):
    return lax.optimization_barrier(values)


def add(blocks):
    return sum(block.astype(F32) for block in blocks).astype(BF16)


def exchange(value, axis):
    return lax.all_to_all(value, axis, split_axis=0, concat_axis=0, tiled=True)


def per_device(hidden_in, spatial_qkv, temporal_qkv, teacher_target, spatial_proj, temporal_proj):
    at_x, at_core, at_y, at_z = (lax.axis_index(a) for a in ("x", "core", "y", "z"))
    place = jnp.stack([at_x, at_core, at_y, at_z]).astype(jnp.int32)

    rows = jnp.where(at_core == 0, spatial_proj, temporal_proj)
    by_z = jnp.concatenate([shift_z(rows, -2, 0), shift_z(rows, -2, 1)])
    by_z, temporal_qkv = after(by_z, temporal_qkv)
    time_x = exchange(send(temporal_qkv.reshape(TOKENS, 3 * D)), SEQ)
    by_y = jnp.concatenate([by_z] + [shift(by_z, "y", 4, 4 - a) for a in range(1, 4)])

    by_y, spatial_qkv = after(by_y, spatial_qkv)
    space_x = spatial_qkv.reshape(TOKENS, 3 * D)
    space_mix, space_probs, order = attend_space(place, space_x)
    time_x, space_mix, space_probs, order = after(time_x, space_mix, space_probs, order)
    time_mix, time_probs = attend_time(time_x)
    time_mix = exchange(time_mix, SEQ)
    own = [by_y] + [shift(by_y, "x", 4, 4 - b) for b in range(1, 4)]
    other = [swap(own[0])]
    time_mix, own[1], own[2], own[3] = after(time_mix, own[1], own[2], own[3])
    other += [swap(block) for block in own[1:]]

    time_grad, space_grad, *packs = project(
        place,
        hidden_in.reshape(TOKENS, D),
        teacher_target.reshape(TOKENS, D),
        space_mix,
        time_mix,
        order,
        own,
        other,
    )
    time_back = exchange(time_grad, SEQ)
    packs = [packs[0]] + [shift(packs[b], "x", 4, b) for b in range(1, 4)]
    spread = spread_of(time_back)
    clip_loss = spread[0, :1] - HUBER_DELTA
    spreads = [spread, swap(spread)]
    time_out = attend_back_time(time_x, time_probs, time_back, spread)
    time_out, spread, packs = after(time_out, spread, packs)
    time_out = exchange(time_out, SEQ)
    packs = packs + [swap(block) for block in packs]

    spatial_qkv_grad = attend_back_space(space_x, space_probs, space_grad, spread)

    partial = weight_grad(place, spreads, packs)
    partial = add([partial[:72]] + [shift(partial[72 * a : 72 * a + 72], "y", 4, a) for a in range(1, 4)])
    piece = add([shift_z(partial[:36], 2, 0), shift_z(partial[36:], 2, 1)])
    piece, time_out, spatial_qkv_grad = after(piece, time_out, spatial_qkv_grad)
    ends = [shift(piece, "y", 4, a).astype(F32) for a in range(1, 4)]
    final = ((piece.astype(F32) + ends[1]) + (ends[0] + ends[2])).astype(BF16)
    spatial_proj_grad, temporal_proj_grad = finish(place, final, swap(final))
    temporal_qkv_grad = receive(time_out)
    return (
        clip_loss,
        spatial_qkv_grad.reshape(1, 2, 64, 3 * D),
        temporal_qkv_grad.reshape(1, 2, 64, 3 * D),
        spatial_proj_grad,
        temporal_proj_grad,
    )


def solution(mesh):
    fine = Mesh(mesh.devices.reshape(4, 2, 4, 8), ("y", "core", "x", "z"))
    clips = P(DP, SEQ, None, None)
    weight = P(SEQ, None)
    return jax.shard_map(
        per_device,
        mesh=fine,
        in_specs=(clips, clips, clips, clips, weight, weight),
        out_specs=(P(DP), clips, clips, weight, weight),
        check_vma=False,
    )
```

time: 246 us -> 193 us (0.78)
  waiting for transfers between devices: 89 us -> 36 us
  local copies, waits for them, and re-layouts: 29.3 us -> 5.17 us
  Pallas kernels: 27.3 us -> 49.4 us
  starting transfers between devices: 77 us -> 93.9 us
  blocking collectives: 13.7 us -> 0 us
    all_to_all x8 -> x4, waiting for transfers between devices: 52.9 us -> 6.15 us  [exchange(): return lax.all_to_all(value, axis, split_axis=0, concat_axis=0, tiled=True)]
    ppermute x9 -> x15, starting transfers between devices: 11 us -> 40.6 us  [shift(): lax.ppermute(value, axis, [(i, (i + step) % size) for i in range(size)])]
    pallas_call x7 -> x10, Pallas kernels: 27.3 us -> 49.4 us  [the longest x1 10.5 us: project(): call(project_kernel, (sent_rows(D + LANES), ROWS) + (packed,) * 4, specs(...]
    all_to_all x8 -> x4, starting transfers between devices: 47.7 us -> 29.1 us  [exchange(): return lax.all_to_all(value, axis, split_axis=0, concat_axis=0, tiled=True)]
    all_to_all x1 -> x0, blocking collectives: 13.7 us -> none  [exchange(): return lax.all_to_all(value, axis, split_axis=0, concat_axis=0, tiled=True)]
    reshape x13 -> x0, local copies, waits for them, and re-layouts: 11.9 us -> none  [the longest x2 2.9 us: per_device(): temporal_qkv_grad = time_out.reshape(32, 2, 2, 3 * D).transpose(1, 0, 2, 3)]
    ppermute x9 -> x15, waiting for transfers between devices: 36.1 us -> 25.5 us  [shift(): lax.ppermute(value, axis, [(i, (i + step) % size) for i in range(size)])]
    ppermute x0 -> x4, starting transfers between devices: none -> 10.2 us  [shift_z(): return lax.ppermute(value, ('y', 'z'), pairs)]
  transfers between devices with their start and end apart: 22 -> 33, of which waited for: 10 -> 14; matrix products, arithmetic and copies ran while one was open for 7% -> 3% of each run, Pallas kernels for 8% -> 18%
where the time goes in v2:
time: 193 us; the launch traced here: 192 us
  starting transfers between devices  93.9 us (49%)
  Pallas kernels  49.4 us (26%)
  waiting for transfers between devices  36 us (19%)
  other arithmetic  5.2 us (3%)
  local copies, waits for them, and re-layouts  5.17 us (3%)
  between operations  2.62 us (1%)
    ppermute x15, starting transfers between devices, shift(): lax.ppermute(value, axis, [(i, (i + step) % size) for i in range(size)])  40.6 us
    all_to_all x4, starting transfers between devices, exchange(): return lax.all_to_all(value, axis, split_axis=0, concat_axis=0, tiled=True)  29.1 us
    ppermute x15, waiting for transfers between devices, shift(): lax.ppermute(value, axis, [(i, (i + step) % size) for i in range(size)])  25.5 us
    ppermute x10, starting transfers between devices, swap(): return lax.ppermute(value, 'core', [(0, 1), (1, 0)])  14 us
    pallas_call x1, Pallas kernels, project(): call(project_kernel, (sent_rows(D + LANES), ROWS) + (packed,) * 4, specs(...  10.5 us
    ppermute x4, starting transfers between devices, shift_z(): return lax.ppermute(value, ('y', 'z'), pairs)  10.2 us
    pallas_call x1, Pallas kernels, attend_back_time(): call(attend_back_time_kernel, sent_rows(3 * D), specs(vmem=4), [wide, plt...  7.26 us
    pallas_call x1, Pallas kernels, attend_back_space(): call(attend_back_space_kernel, jax.ShapeDtypeStruct((TOKENS, 3 * D), BF16...  7.11 us
  transfers between devices with their start and end apart: 33, of which 14 were waited for; matrix products, arithmetic and copies ran while one was open for 3% of the time, Pallas kernels for 18%

profile of v2, /device:TPU:1, one launch (start us, length us, event | category | flops | bytes accessed | tf_op | source)
XLA Modules:
  0.0 192.3 jit_solution(684475308758578954)
XLA Ops:
  1.6 6.5 %collective-permute-start.1 = (bf16[36,1152]{1,0:T(8,128)(2,1)S(1)}, bf16[36,1152]{1,0:T(8,128)(2,1)S(1)}, u32[]{:S(2)}, u32[]{:S(2)}) collective-permute-start(bf16[36,1152]{1,0:T(8,128)(2,1)S(1)} %broadcast_select_fusion), channel_id=1, source_target_pairs={{0,7},{1,0},{2,1},{3,2},{4,3},{5,4},{6,5},{7,6},{64,69},{65,70},{6... | collective-permute-start | bytes 248840 | tf_op jit(solution)/shard_map/ppermute | solution.py:363
  10.3 2.5 %send_order.1 = bf16[32,4,3456]{2,1,0:T(4,128)(2,1)} custom-call(bf16[128,3456]{1,0:T(8,128)(2,1)} %bitcast.11), custom_call_target="tpu_custom_call" | custom-call | flops 3000000000 | bytes 1 | tf_op jit(solution)/shard_map/send_order/pallas_call | solution.py:161
  12.9 7.4 %all-to-all-start = ((bf16[32,4,3456]{2,1,0:T(4,128)(2,1)}), bf16[32,4,3456]{2,1,0:T(4,128)(2,1)S(1)}, u32[]{:S(2)}, u32[]{:S(2)}) async-start(bf16[32,4,3456]{2,1,0:T(4,128)(2,1)} %send_order.1), calls=%async_computation | async-start | bytes 1769472 | tf_op jit(solution)/shard_map/all_to_all | solution.py:383
  20.3 11.6 %collective-permute-start.4 = (bf16[72,1152]{1,0:T(8,128)(2,1)S(1)}, bf16[72,1152]{1,0:T(8,128)(2,1)S(1)}, u32[]{:S(2)}, u32[]{:S(2)}) collective-permute-start(bf16[72,1152]{1,0:T(8,128)(2,1)S(1)} %copy-done.2), channel_id=1, source_target_pairs={{0,64},{64,128},{128,192},{192,0},{1,65},{65,129},{129,193},{193,1... | collective-permute-start | bytes 497672 | tf_op jit(solution)/shard_map/ppermute | solution.py:367
  31.9 1.7 collective-permute-start.3
  33.6 2.0 %collective-permute-start.2 = (bf16[72,1152]{1,0:T(8,128)(2,1)S(1)}, bf16[72,1152]{1,0:T(8,128)(2,1)S(1)}, u32[]{:S(2)}, u32[]{:S(2)}) collective-permute-start(bf16[72,1152]{1,0:T(8,128)(2,1)S(1)} %copy-done.2), channel_id=1, source_target_pairs={{0,192},{64,0},{128,64},{192,128},{1,193},{65,1},{129,65},{193,129... | collective-permute-start | bytes 497672 | tf_op jit(solution)/shard_map/ppermute | solution.py:367
  36.2 3.6 %collective-permute-done.3 = bf16[72,1152]{1,0:T(8,128)(2,1)S(1)} collective-permute-done((bf16[72,1152]{1,0:T(8,128)(2,1)S(1)}, bf16[72,1152]{1,0:T(8,128)(2,1)S(1)}, u32[]{:S(2)}, u32[]{:S(2)}) %collective-permute-start.3) | collective-permute-done | bytes 165920 | tf_op jit(solution)/shard_map/ppermute | solution.py:367
  40.8 1.0 collective-permute-start.7
  41.8 2.4 %collective-permute-start.6 = (bf16[288,1152]{1,0:T(8,128)(2,1)}, bf16[288,1152]{1,0:T(8,128)(2,1)}, u32[]{:S(2)}, u32[]{:S(2)}) collective-permute-start(bf16[288,1152]{1,0:T(8,128)(2,1)} %pad_maximum_fusion.rest_0_), channel_id=1, source_target_pairs={{0,16},{8,24},{16,0},{24,8},{1,17},{9,25},{17,1},{25,9},{2,18},{10... | collective-permute-start | bytes 1990664 | tf_op jit(solution)/shard_map/ppermute | solution.py:367
  44.2 1.1 collective-permute-start.5
  45.4 6.3 %attend_space.1 = (bf16[128,1152]{1,0:T(8,128)(2,1)}, f32[16,128,128]{2,1,0:T(8,128)}, bf16[1152,1152]{1,0:T(8,128)(2,1)}) custom-call(s32[4]{0:T(128)} %pad_add_fusion.place_ref, bf16[128,3456]{1,0:T(8,128)(2,1)} %bitcast.12), custom_call_target="tpu_custom_call" | custom-call | flops 3000000000 | bytes 1 | tf_op jit(solution)/shard_map/attend_space/pallas_call | solution.py:136
  52.6 5.2 %attend_time.1 = (bf16[32,4,1152]{2,1,0:T(4,128)(2,1)}, f32[16,128,128]{2,1,0:T(8,128)}) custom-call(bf16[32,4,3456]{2,1,0:T(4,128)(2,1)} %copy-done), custom_call_target="tpu_custom_call" | custom-call | flops 3000000000 | bytes 1 | tf_op jit(solution)/shard_map/attend_time/pallas_call | solution.py:153
  57.8 6.8 %all-to-all-start.1 = ((bf16[32,4,1152]{2,1,0:T(4,128)(2,1)}), bf16[32,4,1152]{2,1,0:T(4,128)(2,1)S(1)}, u32[]{:S(2)}, u32[]{:S(2)}) async-start(bf16[32,4,1152]{2,1,0:T(4,128)(2,1)} %get-tuple-element.46), calls=%async_computation.1 | async-start | bytes 589824 | tf_op jit(solution)/shard_map/all_to_all | solution.py:383
  64.7 3.8 %collective-permute-start.8 = (bf16[288,1152]{1,0:T(8,128)(2,1)}, bf16[288,1152]{1,0:T(8,128)(2,1)S(1)}, u32[]{:S(2)}, u32[]{:S(2)}) collective-permute-start(bf16[288,1152]{1,0:T(8,128)(2,1)} %pad_maximum_fusion.rest_0_), channel_id=1, source_target_pairs={{0,32},{32,0},{1,33},{33,1},{2,34},{34,2},{3,35},{35,3},{4,36},{36... | collective-permute-start | bytes 1990664 | tf_op jit(solution)/shard_map/ppermute | solution.py:371
  68.4 3.8 %collective-permute-done.6.rest_2_ = bf16[288,1152]{1,0:T(8,128)(2,1)} collective-permute-done((bf16[288,1152]{1,0:T(8,128)(2,1)}, bf16[288,1152]{1,0:T(8,128)(2,1)}, u32[]{:S(2)}, u32[]{:S(2)}) %collective-permute-start.6) | collective-permute-done | bytes 663584 | tf_op jit(solution)/shard_map/ppermute | solution.py:367
  72.3 2.9 %collective-permute-done.5.rest_1_ = bf16[288,1152]{1,0:T(8,128)(2,1)} collective-permute-done((bf16[288,1152]{1,0:T(8,128)(2,1)}, bf16[288,1152]{1,0:T(8,128)(2,1)}, u32[]{:S(2)}, u32[]{:S(2)}) %collective-permute-start.5) | collective-permute-done | bytes 663584 | tf_op jit(solution)/shard_map/ppermute | solution.py:367
  75.7 3.7 %collective-permute-start.9 = (bf16[288,1152]{1,0:T(8,128)(2,1)}, bf16[288,1152]{1,0:T(8,128)(2,1)}, u32[]{:S(2)}, u32[]{:S(2)}) collective-permute-start(bf16[288,1152]{1,0:T(8,128)(2,1)} %collective-permute-done.5.rest_1_), channel_id=1, source_target_pairs={{0,32},{32,0},{1,33},{33,1},{2,34},{34,2},{3,35},{35,3},{4,36},{36... | collective-permute-start | bytes 1990664 | tf_op jit(solution)/shard_map/ppermute | solution.py:371
  79.9 1.6 collective-permute-done.9.rest_5_
  81.5 0.9 collective-permute-done.10.rest_6_
  83.4 10.5 %project.1 = (bf16[32,4,1280]{2,1,0:T(4,128)(2,1)}, bf16[128,1152]{1,0:T(8,128)(2,1)}, bf16[128,1728]{1,0:T(8,128)(2,1)}, bf16[128,1728]{1,0:T(8,128)(2,1)}, bf1...) custom-call(s32[4]{0:T(128)} %pad_add_fusion.place_ref, bf16[32,4,1152]{2,1,0:T(4,128)(2,1)} %copy-done.4, ...), custom_call_target="tpu_custom_call" | custom-call | flops 8000000000 | bytes 1 | tf_op jit(solution)/shard_map/project/pallas_call | solution.py:305
  93.9 7.1 %all-to-all-start.2 = ((bf16[32,4,1280]{2,1,0:T(4,128)(2,1)}), bf16[32,4,1280]{2,1,0:T(4,128)(2,1)S(1)}, u32[]{:S(2)}, u32[]{:S(2)}) async-start(bf16[32,4,1280]{2,1,0:T(4,128)(2,1)} %get-tuple-element.54), calls=%async_computation.2 | async-start | bytes 655360 | tf_op jit(solution)/shard_map/all_to_all | solution.py:383
  100.9 1.3 collective-permute-start.13
  102.3 2.4 %collective-permute-start.14 = (bf16[128,1728]{1,0:T(8,128)(2,1)}, bf16[128,1728]{1,0:T(8,128)(2,1)}, u32[]{:S(2)}, u32[]{:S(2)}) collective-permute-start(bf16[128,1728]{1,0:T(8,128)(2,1)} %get-tuple-element.58), channel_id=1, source_target_pairs={{0,16},{8,24},{16,0},{24,8},{1,17},{9,25},{17,1},{25,9},{2,18},{10... | collective-permute-start | bytes 1327112 | tf_op jit(solution)/shard_map/ppermute | solution.py:367
  104.7 1.1 collective-permute-start.15
  105.8 5.6 %all-to-all-done.2.grad_ref = bf16[32,4,1280]{2,1,0:T(4,128)(2,1)S(1)} async-done(((bf16[32,4,1280]{2,1,0:T(4,128)(2,1)}), bf16[32,4,1280]{2,1,0:T(4,128)(2,1)S(1)}, u32[]{:S(2)}, u32[]{:S(2)}) %all-to-all-start.2) | async-done | bytes 327712 | tf_op jit(solution)/shard_map/all_to_all | solution.py:383
  112.2 1.7 spread.1.spread_ref.rest_0_
  113.9 7.3 %attend_back_time.1 = bf16[32,4,3456]{2,1,0:T(4,128)(2,1)} custom-call(bf16[32,4,3456]{2,1,0:T(4,128)(2,1)} %copy-done, f32[16,128,128]{2,1,0:T(8,128)} %get-tuple-element.55.probs_ref, bf16[32,4,1280]{2,1,0:T(4,128)(2,1)} %copy-done.3, f32[8,128]{1,0:T(8,128)} %spread.1.spread_ref.rest_0_), custom_call_target="tpu_custom_call" | custom-call | flops 5000000000 | bytes 1 | tf_op jit(solution)/shard_map/attend_back_time/pallas_call | solution.py:214
  121.1 7.3 %collective-permute-done.14.rest_4_ = bf16[128,1728]{1,0:T(8,128)(2,1)} collective-permute-done((bf16[128,1728]{1,0:T(8,128)(2,1)}, bf16[128,1728]{1,0:T(8,128)(2,1)}, u32[]{:S(2)}, u32[]{:S(2)}) %collective-permute-start.14) | collective-permute-done | bytes 442400 | tf_op jit(solution)/shard_map/ppermute | solution.py:367
  128.5 1.2 collective-permute-start.16
  130.6 7.8 %all-to-all-start.3 = ((bf16[32,4,3456]{2,1,0:T(4,128)(2,1)}), bf16[32,4,3456]{2,1,0:T(4,128)(2,1)S(1)}, u32[]{:S(2)}, u32[]{:S(2)}) async-start(bf16[32,4,3456]{2,1,0:T(4,128)(2,1)} %attend_back_time.1), calls=%async_computation.3 | async-start | bytes 1769472 | tf_op jit(solution)/shard_map/all_to_all | solution.py:383
  139.0 4.6 %weight_grad.1 = bf16[288,1152]{1,0:T(8,128)(2,1)} custom-call(s32[4]{0:T(128)} %pad_add_fusion.place_ref, f32[8,128]{1,0:T(8,128)} %spread.1.spread_ref.rest_0_, f32[8,128]{1,0:T(8,128)} %copy-done.8, bf16[128,1728]{1,0:T(8,128)(2,1)} %get-tuple-element.60.rest_2_, bf16[128,1728]{1,0:T(8,128)(2,1)} %collective-permute-done.13.rest_3_, ...), custom_call_target="tpu_custom_call" | custom-call | flops 3000000000 | bytes 1 | tf_op jit(solution)/shard_map/weight_grad/pallas_call | solution.py:339
  143.6 1.1 fusion
  144.8 4.0 %collective-permute-start.20 = (bf16[72,1152]{1,0:T(8,128)(2,1)S(1)}, bf16[72,1152]{1,0:T(8,128)(2,1)S(1)}, u32[]{:S(2)}, u32[]{:S(2)}) collective-permute-start(bf16[72,1152]{1,0:T(8,128)(2,1)S(1)} %get-tuple-element.73), channel_id=1, source_target_pairs={{0,64},{64,128},{128,192},{192,0},{1,65},{65,129},{129,193},{193,1... | collective-permute-start | bytes 497672 | tf_op jit(solution)/shard_map/ppermute | solution.py:367
  149.6 3.0 %collective-permute-start.21 = (bf16[72,1152]{1,0:T(8,128)(2,1)S(1)}, bf16[72,1152]{1,0:T(8,128)(2,1)S(1)}, u32[]{:S(2)}, u32[]{:S(2)}) collective-permute-start(bf16[72,1152]{1,0:T(8,128)(2,1)S(1)} %get-tuple-element.75), channel_id=1, source_target_pairs={{0,128},{64,192},{128,0},{192,64},{1,129},{65,193},{129,1},{193,65... | collective-permute-start | bytes 497672 | tf_op jit(solution)/shard_map/ppermute | solution.py:367
  152.5 1.4 collective-permute-done.20
  154.8 4.2 %collective-permute-done.21 = bf16[72,1152]{1,0:T(8,128)(2,1)S(1)} collective-permute-done((bf16[72,1152]{1,0:T(8,128)(2,1)S(1)}, bf16[72,1152]{1,0:T(8,128)(2,1)S(1)}, u32[]{:S(2)}, u32[]{:S(2)}) %collective-permute-start.21) | collective-permute-done | bytes 165920 | tf_op jit(solution)/shard_map/ppermute | solution.py:367
  159.0 1.0 add_convert_fusion
  160.7 2.1 %collective-permute-start.23 = (bf16[36,1152]{1,0:T(8,128)(2,1)}, bf16[36,1152]{1,0:T(8,128)(2,1)}, u32[]{:S(2)}, u32[]{:S(2)}) collective-permute-start(bf16[36,1152]{1,0:T(8,128)(2,1)} %get-tuple-element.76), channel_id=1, source_target_pairs={{0,0},{1,1},{2,2},{3,3},{4,4},{5,5},{6,6},{7,7},{64,66},{65,67},{6... | collective-permute-start | bytes 248840 | tf_op jit(solution)/shard_map/ppermute | solution.py:363
  163.7 7.1 %attend_back_space.1 = bf16[128,3456]{1,0:T(8,128)(2,1)} custom-call(bf16[128,3456]{1,0:T(8,128)(2,1)} %bitcast.13, f32[16,128,128]{2,1,0:T(8,128)} %get-tuple-element.65.probs_ref, bf16[128,1152]{1,0:T(8,128)(2,1)} %get-tuple-element.66.grad_ref, f32[8,128]{1,0:T(8,128)} %spread.1.spread_ref.rest_0_), custom_call_target="tpu_custom_call" | custom-call | flops 1000000000 | bytes 1 | tf_op jit(solution)/shard_map/attend_back_space/pallas_call | solution.py:229
  170.8 1.0 add_convert_fusion.2
  171.8 5.0 %collective-permute-start.27 = (bf16[36,1152]{1,0:T(8,128)(2,1)S(1)}, bf16[36,1152]{1,0:T(8,128)(2,1)S(1)}, u32[]{:S(2)}, u32[]{:S(2)}) collective-permute-start(bf16[36,1152]{1,0:T(8,128)(2,1)S(1)} %add_convert_fusion.2), channel_id=1, source_target_pairs={{0,192},{64,0},{128,64},{192,128},{1,193},{65,1},{129,65},{193,129... | collective-permute-start | bytes 248840 | tf_op jit(solution)/shard_map/ppermute | solution.py:367
  176.8 1.3 collective-permute-start.26
  178.1 1.7 collective-permute-start.25
  179.8 1.2 slice.21
  181.7 1.3 collective-permute-done.25
  183.1 3.9 %collective-permute-start.28 = (bf16[36,1152]{1,0:T(8,128)(2,1)S(1)}, bf16[36,1152]{1,0:T(8,128)(2,1)}, u32[]{:S(2)}, u32[]{:S(2)}) collective-permute-start(bf16[36,1152]{1,0:T(8,128)(2,1)S(1)} %add_convert_fusion.1.own_ref), channel_id=1, source_target_pairs={{0,32},{32,0},{1,33},{33,1},{2,34},{34,2},{3,35},{35,3},{4,36},{36... | collective-permute-start | bytes 248840 | tf_op jit(solution)/shard_map/ppermute | solution.py:371
  186.9 2.5 %natural_order.1 = bf16[128,3456]{1,0:T(8,128)(2,1)} custom-call(bf16[32,4,3456]{2,1,0:T(4,128)(2,1)} %copy-done.1), custom_call_target="tpu_custom_call" | custom-call | flops 3000000000 | bytes 1 | tf_op jit(solution)/shard_map/natural_order/pallas_call | solution.py:171
  189.4 1.7 finish.1
  (56 shorter events, 13.4 us)
Async XLA Ops:
  1.6 8.1 %collective-permute-start.1 = (bf16[36,1152]{1,0:T(8,128)(2,1)S(1)}, bf16[36,1152]{1,0:T(8,128)(2,1)S(1)}, u32[]{:S(2)}, u32[]{:S(2)}) collective-permute-start(bf16[36,1152]{1,0:T(8,128)(2,1)S(1)} %broadcast_select_fusion), channel_id=1, source_target_pairs={{0,7},{1,0},{2,1},{3,2},{4,3},{5,4},{6,5},{7,6},{64,69},{65,70},{6... | collective-permute-start | bytes 248840 | tf_op jit(solution)/shard_map/ppermute | solution.py:363
  8.0 1.6 collective-permute-start
  12.8 7.4 %copy-start.2 = (bf16[72,1152]{1,0:T(8,128)(2,1)S(1)}, bf16[72,1152]{1,0:T(8,128)(2,1)}, u32[]{:S(2)}) copy-start(bf16[72,1152]{1,0:T(8,128)(2,1)} %pad_maximum_fusion.1) | copy-start | bytes 497668
  12.9 38.9 %all-to-all-start = ((bf16[32,4,3456]{2,1,0:T(4,128)(2,1)}), bf16[32,4,3456]{2,1,0:T(4,128)(2,1)S(1)}, u32[]{:S(2)}, u32[]{:S(2)}) async-start(bf16[32,4,3456]{2,1,0:T(4,128)(2,1)} %send_order.1), calls=%async_computation | async-start | bytes 1769472 | tf_op jit(solution)/shard_map/all_to_all | solution.py:383
  20.3 16.0 %collective-permute-start.4 = (bf16[72,1152]{1,0:T(8,128)(2,1)S(1)}, bf16[72,1152]{1,0:T(8,128)(2,1)S(1)}, u32[]{:S(2)}, u32[]{:S(2)}) collective-permute-start(bf16[72,1152]{1,0:T(8,128)(2,1)S(1)} %copy-done.2), channel_id=1, source_target_pairs={{0,64},{64,128},{128,192},{192,0},{1,65},{65,129},{129,193},{193,1... | collective-permute-start | bytes 497672 | tf_op jit(solution)/shard_map/ppermute | solution.py:367
  31.9 7.9 %collective-permute-start.3 = (bf16[72,1152]{1,0:T(8,128)(2,1)S(1)}, bf16[72,1152]{1,0:T(8,128)(2,1)S(1)}, u32[]{:S(2)}, u32[]{:S(2)}) collective-permute-start(bf16[72,1152]{1,0:T(8,128)(2,1)S(1)} %copy-done.2), channel_id=1, source_target_pairs={{0,128},{64,192},{128,0},{192,64},{1,129},{65,193},{129,1},{193,65... | collective-permute-start | bytes 497672 | tf_op jit(solution)/shard_map/ppermute | solution.py:367
  33.6 6.3 %collective-permute-start.2 = (bf16[72,1152]{1,0:T(8,128)(2,1)S(1)}, bf16[72,1152]{1,0:T(8,128)(2,1)S(1)}, u32[]{:S(2)}, u32[]{:S(2)}) collective-permute-start(bf16[72,1152]{1,0:T(8,128)(2,1)S(1)} %copy-done.2), channel_id=1, source_target_pairs={{0,192},{64,0},{128,64},{192,128},{1,193},{65,1},{129,65},{193,129... | collective-permute-start | bytes 497672 | tf_op jit(solution)/shard_map/ppermute | solution.py:367
  40.8 27.7 %collective-permute-start.7 = (bf16[288,1152]{1,0:T(8,128)(2,1)}, bf16[288,1152]{1,0:T(8,128)(2,1)}, u32[]{:S(2)}, u32[]{:S(2)}) collective-permute-start(bf16[288,1152]{1,0:T(8,128)(2,1)} %pad_maximum_fusion.rest_0_), channel_id=1, source_target_pairs={{0,8},{8,16},{16,24},{24,0},{1,9},{9,17},{17,25},{25,1},{2,10},{10... | collective-permute-start | bytes 1990664 | tf_op jit(solution)/shard_map/ppermute | solution.py:367
  41.8 30.5 %collective-permute-start.6 = (bf16[288,1152]{1,0:T(8,128)(2,1)}, bf16[288,1152]{1,0:T(8,128)(2,1)}, u32[]{:S(2)}, u32[]{:S(2)}) collective-permute-start(bf16[288,1152]{1,0:T(8,128)(2,1)} %pad_maximum_fusion.rest_0_), channel_id=1, source_target_pairs={{0,16},{8,24},{16,0},{24,8},{1,17},{9,25},{17,1},{25,9},{2,18},{10... | collective-permute-start | bytes 1990664 | tf_op jit(solution)/shard_map/ppermute | solution.py:367
  44.2 30.9 %collective-permute-start.5 = (bf16[288,1152]{1,0:T(8,128)(2,1)}, bf16[288,1152]{1,0:T(8,128)(2,1)}, u32[]{:S(2)}, u32[]{:S(2)}) collective-permute-start(bf16[288,1152]{1,0:T(8,128)(2,1)} %pad_maximum_fusion.rest_0_), channel_id=1, source_target_pairs={{0,24},{8,0},{16,8},{24,16},{1,25},{9,1},{17,9},{25,17},{2,26},{10... | collective-permute-start | bytes 1990664 | tf_op jit(solution)/shard_map/ppermute | solution.py:367
  51.7 0.9 copy-start
  57.8 17.9 %all-to-all-start.1 = ((bf16[32,4,1152]{2,1,0:T(4,128)(2,1)}), bf16[32,4,1152]{2,1,0:T(4,128)(2,1)S(1)}, u32[]{:S(2)}, u32[]{:S(2)}) async-start(bf16[32,4,1152]{2,1,0:T(4,128)(2,1)} %get-tuple-element.46), calls=%async_computation.1 | async-start | bytes 589824 | tf_op jit(solution)/shard_map/all_to_all | solution.py:383
  64.7 15.2 %collective-permute-start.8 = (bf16[288,1152]{1,0:T(8,128)(2,1)}, bf16[288,1152]{1,0:T(8,128)(2,1)S(1)}, u32[]{:S(2)}, u32[]{:S(2)}) collective-permute-start(bf16[288,1152]{1,0:T(8,128)(2,1)} %pad_maximum_fusion.rest_0_), channel_id=1, source_target_pairs={{0,32},{32,0},{1,33},{33,1},{2,34},{34,2},{3,35},{35,3},{4,36},{36... | collective-permute-start | bytes 1990664 | tf_op jit(solution)/shard_map/ppermute | solution.py:371
  75.7 7.7 %copy-start.4 = (bf16[32,4,1152]{2,1,0:T(4,128)(2,1)}, bf16[32,4,1152]{2,1,0:T(4,128)(2,1)S(1)}, u32[]{:S(2)}) copy-start(bf16[32,4,1152]{2,1,0:T(4,128)(2,1)S(1)} %all-to-all-done.1.time_ref) | copy-start | bytes 884740
  75.7 5.8 %collective-permute-start.9 = (bf16[288,1152]{1,0:T(8,128)(2,1)}, bf16[288,1152]{1,0:T(8,128)(2,1)}, u32[]{:S(2)}, u32[]{:S(2)}) collective-permute-start(bf16[288,1152]{1,0:T(8,128)(2,1)} %collective-permute-done.5.rest_1_), channel_id=1, source_target_pairs={{0,32},{32,0},{1,33},{33,1},{2,34},{34,2},{3,35},{35,3},{4,36},{36... | collective-permute-start | bytes 1990664 | tf_op jit(solution)/shard_map/ppermute | solution.py:371
  79.4 3.0 %collective-permute-start.10 = (bf16[288,1152]{1,0:T(8,128)(2,1)}, bf16[288,1152]{1,0:T(8,128)(2,1)}, u32[]{:S(2)}, u32[]{:S(2)}) collective-permute-start(bf16[288,1152]{1,0:T(8,128)(2,1)} %collective-permute-done.6.rest_2_), channel_id=1, source_target_pairs={{0,32},{32,0},{1,33},{33,1},{2,34},{34,2},{3,35},{35,3},{4,36},{36... | collective-permute-start | bytes 1990664 | tf_op jit(solution)/shard_map/ppermute | solution.py:371
  79.4 4.0 %collective-permute-start.11 = (bf16[288,1152]{1,0:T(8,128)(2,1)}, bf16[288,1152]{1,0:T(8,128)(2,1)}, u32[]{:S(2)}, u32[]{:S(2)}) collective-permute-start(bf16[288,1152]{1,0:T(8,128)(2,1)} %collective-permute-done.7.rest_3_), channel_id=1, source_target_pairs={{0,32},{32,0},{1,33},{33,1},{2,34},{34,2},{3,35},{35,3},{4,36},{36... | collective-permute-start | bytes 1990664 | tf_op jit(solution)/shard_map/ppermute | solution.py:371
  79.9 3.5 %copy-start.6 = (bf16[288,1152]{1,0:T(8,128)(2,1)}, bf16[288,1152]{1,0:T(8,128)(2,1)S(1)}, u32[]{:S(2)}) copy-start(bf16[288,1152]{1,0:T(8,128)(2,1)S(1)} %collective-permute-done.8.rest_4_) | copy-start | bytes 1990660
  93.9 17.6 %all-to-all-start.2 = ((bf16[32,4,1280]{2,1,0:T(4,128)(2,1)}), bf16[32,4,1280]{2,1,0:T(4,128)(2,1)S(1)}, u32[]{:S(2)}, u32[]{:S(2)}) async-start(bf16[32,4,1280]{2,1,0:T(4,128)(2,1)} %get-tuple-element.54), calls=%async_computation.2 | async-start | bytes 655360 | tf_op jit(solution)/shard_map/all_to_all | solution.py:383
  100.9 20.2 %collective-permute-start.13 = (bf16[128,1728]{1,0:T(8,128)(2,1)}, bf16[128,1728]{1,0:T(8,128)(2,1)}, u32[]{:S(2)}, u32[]{:S(2)}) collective-permute-start(bf16[128,1728]{1,0:T(8,128)(2,1)} %get-tuple-element.57), channel_id=1, source_target_pairs={{0,8},{8,16},{16,24},{24,0},{1,9},{9,17},{17,25},{25,1},{2,10},{10... | collective-permute-start | bytes 1327112 | tf_op jit(solution)/shard_map/ppermute | solution.py:367
  102.3 26.2 %collective-permute-start.14 = (bf16[128,1728]{1,0:T(8,128)(2,1)}, bf16[128,1728]{1,0:T(8,128)(2,1)}, u32[]{:S(2)}, u32[]{:S(2)}) collective-permute-start(bf16[128,1728]{1,0:T(8,128)(2,1)} %get-tuple-element.58), channel_id=1, source_target_pairs={{0,16},{8,24},{16,0},{24,8},{1,17},{9,25},{17,1},{25,9},{2,18},{10... | collective-permute-start | bytes 1327112 | tf_op jit(solution)/shard_map/ppermute | solution.py:367
  104.7 23.8 %collective-permute-start.15 = (bf16[128,1728]{1,0:T(8,128)(2,1)}, bf16[128,1728]{1,0:T(8,128)(2,1)}, u32[]{:S(2)}, u32[]{:S(2)}) collective-permute-start(bf16[128,1728]{1,0:T(8,128)(2,1)} %get-tuple-element.59), channel_id=1, source_target_pairs={{0,24},{8,0},{16,8},{24,16},{1,25},{9,1},{17,9},{25,17},{2,26},{10... | collective-permute-start | bytes 1327112 | tf_op jit(solution)/shard_map/ppermute | solution.py:367
  111.4 0.7 copy-start.3
  113.9 16.3 %copy-start.7 = (f32[8,128]{1,0:T(8,128)S(1)}, f32[8,128]{1,0:T(8,128)}, u32[]{:S(2)}) copy-start(f32[8,128]{1,0:T(8,128)} %spread.1.spread_ref.rest_0_) | copy-start | bytes 12292
  128.5 10.0 %collective-permute-start.16 = (bf16[128,1728]{1,0:T(8,128)(2,1)}, bf16[128,1728]{1,0:T(8,128)(2,1)}, u32[]{:S(2)}, u32[]{:S(2)}) collective-permute-start(bf16[128,1728]{1,0:T(8,128)(2,1)} %get-tuple-element.60.rest_2_), channel_id=1, source_target_pairs={{0,32},{32,0},{1,33},{33,1},{2,34},{34,2},{3,35},{35,3},{4,36},{36... | collective-permute-start | bytes 1327112 | tf_op jit(solution)/shard_map/ppermute | solution.py:371
  129.6 8.9 %collective-permute-start.17 = (bf16[128,1728]{1,0:T(8,128)(2,1)}, bf16[128,1728]{1,0:T(8,128)(2,1)}, u32[]{:S(2)}, u32[]{:S(2)}) collective-permute-start(bf16[128,1728]{1,0:T(8,128)(2,1)} %collective-permute-done.13.rest_3_), channel_id=1, source_target_pairs={{0,32},{32,0},{1,33},{33,1},{2,34},{34,2},{3,35},{35,3},{4,36},{36... | collective-permute-start | bytes 1327112 | tf_op jit(solution)/shard_map/ppermute | solution.py:371
  129.6 8.9 %collective-permute-start.18 = (bf16[128,1728]{1,0:T(8,128)(2,1)}, bf16[128,1728]{1,0:T(8,128)(2,1)}, u32[]{:S(2)}, u32[]{:S(2)}) collective-permute-start(bf16[128,1728]{1,0:T(8,128)(2,1)} %collective-permute-done.14.rest_4_), channel_id=1, source_target_pairs={{0,32},{32,0},{1,33},{33,1},{2,34},{34,2},{3,35},{35,3},{4,36},{36... | collective-permute-start | bytes 1327112 | tf_op jit(solution)/shard_map/ppermute | solution.py:371
  130.1 8.4 %collective-permute-start.19 = (bf16[128,1728]{1,0:T(8,128)(2,1)}, bf16[128,1728]{1,0:T(8,128)(2,1)}, u32[]{:S(2)}, u32[]{:S(2)}) collective-permute-start(bf16[128,1728]{1,0:T(8,128)(2,1)} %collective-permute-done.15.rest_5_), channel_id=1, source_target_pairs={{0,32},{32,0},{1,33},{33,1},{2,34},{34,2},{3,35},{35,3},{4,36},{36... | collective-permute-start | bytes 1327112 | tf_op jit(solution)/shard_map/ppermute | solution.py:371
  130.1 8.3 %collective-permute-start.12 = (f32[8,128]{1,0:T(8,128)S(1)}, f32[8,128]{1,0:T(8,128)S(1)}, u32[]{:S(2)}, u32[]{:S(2)}) collective-permute-start(f32[8,128]{1,0:T(8,128)S(1)} %copy-done.7), channel_id=1, source_target_pairs={{0,32},{32,0},{1,33},{33,1},{2,34},{34,2},{3,35},{35,3},{4,36},{36... | collective-permute-start | bytes 12296 | tf_op jit(solution)/shard_map/ppermute | solution.py:371
  130.6 41.2 %all-to-all-start.3 = ((bf16[32,4,3456]{2,1,0:T(4,128)(2,1)}), bf16[32,4,3456]{2,1,0:T(4,128)(2,1)S(1)}, u32[]{:S(2)}, u32[]{:S(2)}) async-start(bf16[32,4,3456]{2,1,0:T(4,128)(2,1)} %attend_back_time.1), calls=%async_computation.3 | async-start | bytes 1769472 | tf_op jit(solution)/shard_map/all_to_all | solution.py:383
  138.5 0.6 copy-start.8
  144.8 9.1 %collective-permute-start.20 = (bf16[72,1152]{1,0:T(8,128)(2,1)S(1)}, bf16[72,1152]{1,0:T(8,128)(2,1)S(1)}, u32[]{:S(2)}, u32[]{:S(2)}) collective-permute-start(bf16[72,1152]{1,0:T(8,128)(2,1)S(1)} %get-tuple-element.73), channel_id=1, source_target_pairs={{0,64},{64,128},{128,192},{192,0},{1,65},{65,129},{129,193},{193,1... | collective-permute-start | bytes 497672 | tf_op jit(solution)/shard_map/ppermute | solution.py:367
  148.8 6.1 %collective-permute-start.22 = (bf16[72,1152]{1,0:T(8,128)(2,1)S(1)}, bf16[72,1152]{1,0:T(8,128)(2,1)S(1)}, u32[]{:S(2)}, u32[]{:S(2)}) collective-permute-start(bf16[72,1152]{1,0:T(8,128)(2,1)S(1)} %get-tuple-element.74), channel_id=1, source_target_pairs={{0,192},{64,0},{128,64},{192,128},{1,193},{65,1},{129,65},{193,129... | collective-permute-start | bytes 497672 | tf_op jit(solution)/shard_map/ppermute | solution.py:367
  149.6 9.4 %collective-permute-start.21 = (bf16[72,1152]{1,0:T(8,128)(2,1)S(1)}, bf16[72,1152]{1,0:T(8,128)(2,1)S(1)}, u32[]{:S(2)}, u32[]{:S(2)}) collective-permute-start(bf16[72,1152]{1,0:T(8,128)(2,1)S(1)} %get-tuple-element.75), channel_id=1, source_target_pairs={{0,128},{64,192},{128,0},{192,64},{1,129},{65,193},{129,1},{193,65... | collective-permute-start | bytes 497672 | tf_op jit(solution)/shard_map/ppermute | solution.py:367
  160.7 10.2 %collective-permute-start.23 = (bf16[36,1152]{1,0:T(8,128)(2,1)}, bf16[36,1152]{1,0:T(8,128)(2,1)}, u32[]{:S(2)}, u32[]{:S(2)}) collective-permute-start(bf16[36,1152]{1,0:T(8,128)(2,1)} %get-tuple-element.76), channel_id=1, source_target_pairs={{0,0},{1,1},{2,2},{3,3},{4,4},{5,5},{6,6},{7,7},{64,66},{65,67},{6... | collective-permute-start | bytes 248840 | tf_op jit(solution)/shard_map/ppermute | solution.py:363
  162.8 8.0 %collective-permute-start.24 = (bf16[36,1152]{1,0:T(8,128)(2,1)S(1)}, bf16[36,1152]{1,0:T(8,128)(2,1)}, u32[]{:S(2)}, u32[]{:S(2)}) collective-permute-start(bf16[36,1152]{1,0:T(8,128)(2,1)S(1)} %get-tuple-element.77), channel_id=1, source_target_pairs={{0,1},{1,2},{2,3},{3,4},{4,5},{5,6},{6,7},{7,0},{64,67},{65,68},{6... | collective-permute-start | bytes 248840 | tf_op jit(solution)/shard_map/ppermute | solution.py:363
  171.8 15.1 %copy-start.1 = (bf16[32,4,3456]{2,1,0:T(4,128)(2,1)}, bf16[32,4,3456]{2,1,0:T(4,128)(2,1)S(1)}, u32[]{:S(2)}) copy-start(bf16[32,4,3456]{2,1,0:T(4,128)(2,1)S(1)} %all-to-all-done.3.x_ref) | copy-start | bytes 2654212
  171.8 9.8 %collective-permute-start.27 = (bf16[36,1152]{1,0:T(8,128)(2,1)S(1)}, bf16[36,1152]{1,0:T(8,128)(2,1)S(1)}, u32[]{:S(2)}, u32[]{:S(2)}) collective-permute-start(bf16[36,1152]{1,0:T(8,128)(2,1)S(1)} %add_convert_fusion.2), channel_id=1, source_target_pairs={{0,192},{64,0},{128,64},{192,128},{1,193},{65,1},{129,65},{193,129... | collective-permute-start | bytes 248840 | tf_op jit(solution)/shard_map/ppermute | solution.py:367
  176.8 4.9 %collective-permute-start.26 = (bf16[36,1152]{1,0:T(8,128)(2,1)S(1)}, bf16[36,1152]{1,0:T(8,128)(2,1)S(1)}, u32[]{:S(2)}, u32[]{:S(2)}) collective-permute-start(bf16[36,1152]{1,0:T(8,128)(2,1)S(1)} %add_convert_fusion.2), channel_id=1, source_target_pairs={{0,64},{64,128},{128,192},{192,0},{1,65},{65,129},{129,193},{193,1... | collective-permute-start | bytes 248840 | tf_op jit(solution)/shard_map/ppermute | solution.py:367
  178.1 4.9 %collective-permute-start.25 = (bf16[36,1152]{1,0:T(8,128)(2,1)S(1)}, bf16[36,1152]{1,0:T(8,128)(2,1)S(1)}, u32[]{:S(2)}, u32[]{:S(2)}) collective-permute-start(bf16[36,1152]{1,0:T(8,128)(2,1)S(1)} %add_convert_fusion.2), channel_id=1, source_target_pairs={{0,128},{64,192},{128,0},{192,64},{1,129},{65,193},{129,1},{193,65... | collective-permute-start | bytes 248840 | tf_op jit(solution)/shard_map/ppermute | solution.py:367
  183.1 6.3 %copy-start.5 = (bf16[36,1152]{1,0:T(8,128)(2,1)}, bf16[36,1152]{1,0:T(8,128)(2,1)S(1)}, u32[]{:S(2)}) copy-start(bf16[36,1152]{1,0:T(8,128)(2,1)S(1)} %add_convert_fusion.1.own_ref) | copy-start | bytes 248836
  183.1 6.3 %collective-permute-start.28 = (bf16[36,1152]{1,0:T(8,128)(2,1)S(1)}, bf16[36,1152]{1,0:T(8,128)(2,1)}, u32[]{:S(2)}, u32[]{:S(2)}) collective-permute-start(bf16[36,1152]{1,0:T(8,128)(2,1)S(1)} %add_convert_fusion.1.own_ref), channel_id=1, source_target_pairs={{0,32},{32,0},{1,33},{33,1},{2,34},{34,2},{3,35},{35,3},{4,36},{36... | collective-permute-start | bytes 248840 | tf_op jit(solution)/shard_map/ppermute | solution.py:371

commit v3 on v2

--- a/solution.py
+++ b/solution.py
@@ -8,6 +8,7 @@
 from jax.sharding import Mesh, PartitionSpec as P
 
 HEADS = 16
+
 D = 1152
 E = D // HEADS
 TOKENS = 128
@@ -25,21 +26,17 @@
 NT = (((1,), (1,)), ((), ()))
 TN = (((0,), (0,)), ((), ()))
 
-
 def mul(left, right, dims):
     return lax.dot_general(left, right, dims, preferred_element_type=F32)
-
 
 def window(head):
     low = E * head // LANES
     high = (E * head + E - 1) // LANES + 1
     return low * LANES, high * LANES
 
-
 def head_mask(head, low, high):
     lane = lax.broadcasted_iota(jnp.int32, (TOKENS, high - low), 1) + low
     return jnp.where((lane >= E * head) & (lane < E * head + E), 1.0, 0.0).astype(BF16)
-
 
 def same_sequence(temporal):
     row = lax.broadcasted_iota(jnp.int32, (TOKENS, TOKENS), 0)
@@ -48,13 +45,11 @@
         return (row & 1) == (col & 1)
     return (row >> 6) == (col >> 6)
 
-
 def natural_from_sent():
     nat = lax.broadcasted_iota(jnp.int32, (TOKENS, TOKENS), 0)
     sent = lax.broadcasted_iota(jnp.int32, (TOKENS, TOKENS), 1)
     goes = ((sent >> 1) & 1) * 64 + (sent >> 2) * 2 + (sent & 1)
     return jnp.where(nat == goes, 1.0, 0.0).astype(BF16)
-
 
 class Tiles:
     def __init__(self, ref, offset, scale=None):
@@ -73,7 +68,6 @@
                 self.ref[:, at : at + LANES] = part.astype(self.ref.dtype)
             else:
                 self.pending = part
-
 
 def attend_heads(temporal, x_ref, mix_ref, probs_ref):
     same = same_sequence(temporal)
@@ -90,33 +84,28 @@
         probs_ref[head] = probs
         out.add(head, mul(probs.astype(BF16), values, NN))
 
-
 def attend_space_kernel(place_ref, x_ref, mix_ref, probs_ref, order_ref, mix):
     at_x, at_y, at_z = place_ref[0], place_ref[2], place_ref[3]
     column = lax.broadcasted_iota(jnp.int32, (D, LANES), 0)
     for tile in range(0, D, LANES):
         lane = lax.broadcasted_iota(jnp.int32, (1, LANES), 1) + tile
         block = (lane * 1821) >> 16
-        from_z = (at_z + 2 * (((block >> 1) + at_y) & 3) + (block & 1)) & 7
+        from_z = (at_z + (((block >> 1) + at_y) & 3) + 4 * (block & 1)) & 7
         from_x = ((block >> 3) + at_x) & 3
         source = (from_x * 8 + from_z) * 36 + (lane - block * 36)
         order_ref[:, tile : tile + LANES] = jnp.where(column == source, 1.0, 0.0).astype(BF16)
     attend_heads(False, x_ref, mix, probs_ref)
     mix_ref[...] = mul(mix[...], order_ref[...], NN).astype(BF16)
 
-
 ROWS = jax.ShapeDtypeStruct((TOKENS, D), BF16)
 PROBS = jax.ShapeDtypeStruct((HEADS, TOKENS, TOKENS), F32)
 
-
 def sent_rows(width):
     return jax.ShapeDtypeStruct((32, 4, width), BF16)
-
 
 def specs(**places):
     kinds = {"smem": pltpu.SMEM, "vmem": pltpu.VMEM, "any": pl.ANY}
     return [pl.BlockSpec(memory_space=kinds[k]) for k, n in places.items() for _ in range(n)]
-
 
 def call(kernel, out_shape, in_specs, scratch, name, micros=3, out_specs=None):
     return pl.pallas_call(
@@ -130,7 +119,6 @@
         name=name,
     )
 
-
 def attend_space(place, x):
     order = jax.ShapeDtypeStruct((D, D), BF16)
     return call(
@@ -139,37 +127,40 @@
         specs(smem=1, vmem=1),
         [pltpu.VMEM((TOKENS, D), BF16)],
         "attend_space",
+        14,
     )(place, x)
 
+def stack_kernel(*refs):
+    *block_refs, out_ref = refs
+    for a, ref in enumerate(block_refs):
+        out_ref[72 * a : 72 * a + 72] = ref[...]
+
+def stack(blocks):
+    out = jax.ShapeDtypeStruct((288, D), BF16)
+    return call(stack_kernel, out, specs(vmem=4), [], "stack", 1)(*blocks)
 
 def attend_time_kernel(x_ref, mix_ref, probs_ref, x, mix):
     x[...] = x_ref[...].reshape(TOKENS, 3 * D)
     attend_heads(True, x, mix, probs_ref)
     mix_ref[...] = mix[...].reshape(32, 4, D)
 
-
 def attend_time(x):
     scratch = [pltpu.VMEM((TOKENS, 3 * D), BF16), pltpu.VMEM((TOKENS, D), BF16)]
     return call(attend_time_kernel, (sent_rows(D), PROBS), specs(vmem=1), scratch, "attend_time")(x)
 
-
 def send_kernel(x_ref, out_ref):
     out_ref[...] = mul(natural_from_sent(), x_ref[...], TN).astype(BF16).reshape(32, 4, 3 * D)
 
-
 def send(x):
     return call(send_kernel, sent_rows(3 * D), specs(vmem=1), [], "send_order")(x)
-
 
 def receive_kernel(x_ref, out_ref):
     x = x_ref[...].reshape(TOKENS, 3 * D)
     out_ref[...] = mul(natural_from_sent(), x, NN).astype(BF16)
 
-
 def receive(x):
     out = jax.ShapeDtypeStruct((TOKENS, 3 * D), BF16)
     return call(receive_kernel, out, specs(vmem=1), [], "natural_order")(x)
-
 
 def attend_back_heads(inv, x_ref, probs_ref, grad_ref, out_ref):
     query_out = Tiles(out_ref, 0)
@@ -190,40 +181,29 @@
         query_out.add(head, mul(score_grad, keys, NN))
         key_out.add(head, mul(score_grad, queries, TN))
 
-
-def spread_kernel(grad_ref, spread_ref):
-    total = 0.25 * jnp.sum(grad_ref[:, :, D:].reshape(TOKENS, LANES).astype(F32))
-    spread_ref[...] = jnp.sqrt(jnp.full((8, LANES), total, F32) / CELLS + HUBER_DELTA**2)
-
-
-def spread_of(grad):
-    out = jax.ShapeDtypeStruct((8, LANES), F32)
-    return call(spread_kernel, out, specs(vmem=1), [], "spread", 1)(grad)
-
-
-def attend_back_time_kernel(x_ref, probs_ref, grad_ref, spread_ref, out_ref, x, grad, out):
+def attend_back_time_kernel(x_ref, probs_ref, grad_ref, out_ref, spread_ref, x, grad, out):
     x[...] = x_ref[...].reshape(TOKENS, 3 * D)
     grad[...] = grad_ref[:, :, :D].reshape(TOKENS, D)
-    inv = 1.0 / spread_ref[0:1, 0:1]
+    total = 0.25 * jnp.sum(grad_ref[:, :, D:].reshape(TOKENS, LANES).astype(F32))
+    spread = jnp.sqrt(jnp.full((8, LANES), total, F32) / CELLS + HUBER_DELTA**2)
+    spread_ref[...] = spread
+    inv = 1.0 / spread[0:1, 0:1]
     attend_back_heads(inv, x, probs_ref, grad, out)
     out_ref[...] = out[...].reshape(32, 4, 3 * D)
 
-
-def attend_back_time(x, probs, grad, spread):
+def attend_back_time(x, probs, grad):
     wide = pltpu.VMEM((TOKENS, 3 * D), BF16)
     return call(
         attend_back_time_kernel,
-        sent_rows(3 * D),
-        specs(vmem=4),
+        (sent_rows(3 * D), jax.ShapeDtypeStruct((8, LANES), F32)),
+        specs(vmem=3),
         [wide, pltpu.VMEM((TOKENS, D), BF16), wide],
         "attend_back_time",
         5,
-    )(x, probs, grad, spread)
-
+    )(x, probs, grad)
 
 def attend_back_space_kernel(x_ref, probs_ref, grad_ref, spread_ref, out_ref):
     attend_back_heads(1.0 / spread_ref[0:1, 0:1], x_ref, probs_ref, grad_ref, out_ref)
-
 
 def attend_back_space(x, probs, grad, spread):
     return call(
@@ -235,7 +215,6 @@
         1,
     )(x, probs, grad, spread)
 
-
 def fetch_weights(refs, weight, sems):
     copies = []
     for a in range(4):
@@ -244,11 +223,10 @@
         copies.append(copy)
     return copies
 
-
 def project_kernel(place_ref, time_ref, hidden_any, target_any, space_any, order_any, *rest):
     own_refs, other_refs = rest[0:4], rest[4:8]
-    time_grad_ref, space_grad_ref, pack_refs = rest[8], rest[9], rest[10:14]
-    weights, hidden_ref, target_ref, space_ref, order_ref, packs, sems = rest[14:]
+    time_grad_ref, pack_refs = rest[8], rest[9:13]
+    weights, hidden_ref, target_ref, space_ref, order_ref, packs, sems = rest[13:]
     at_core = place_ref[1]
     loads = [
         pltpu.make_async_copy(source, place, sems.at[2, n])
@@ -266,13 +244,14 @@
     time_mix = mul(natural, time_ref[...].reshape(TOKENS, D), NN).astype(BF16)
     time_mix = mul(time_mix, order_ref[...], NN).astype(BF16)
     base = hidden_ref[...].astype(F32) - target_ref[...].astype(F32)
-    for copy in copies:
+    first = at_core == 0
+    space_mix = space_ref[...]
+    for copy in copies[:4]:
         copy.wait()
-    resid = (
-        base
-        + mul(space_ref[...], weights[0], NN)
-        + mul(time_mix, weights[1], NN)
-    )
+    resid = base + mul(jnp.where(first, space_mix, time_mix), weights[at_core], NN)
+    for copy in copies[4:]:
+        copy.wait()
+    resid = resid + mul(jnp.where(first, time_mix, space_mix), weights[1 - at_core], NN)
     total = jnp.sum(resid * resid)
     out_grad = resid.astype(BF16)
     time_grad = mul(out_grad, weights[1], NT).astype(BF16)
@@ -294,17 +273,14 @@
         )
         stores.append(pltpu.make_async_copy(packs.at[a], pack_refs[a], sems.at[3, a]))
         stores[-1].start()
-    space_grad = mul(out_grad, weights[0], NT).astype(BF16)
-    space_grad_ref[...] = mul(space_grad, order_ref[...], NT).astype(BF16)
     for copy in stores:
         copy.wait()
 
-
 def project(place, hidden, target, space_mix, time_mix, order, own, other):
     packed = jax.ShapeDtypeStruct((TOKENS, D + 576), BF16)
     return call(
         project_kernel,
-        (sent_rows(D + LANES), ROWS) + (packed,) * 4,
+        (sent_rows(D + LANES),) + (packed,) * 4,
         specs(smem=1, vmem=1, any=12),
         [pltpu.VMEM((2, D, D), BF16)]
         + [pltpu.VMEM((TOKENS, D), BF16)] * 3
@@ -315,13 +291,36 @@
         ],
         "project",
         8,
-        specs(vmem=2, any=4),
+        specs(vmem=1, any=4),
     )(place, time_mix, hidden, target, space_mix, order, *own, *other)
 
+def space_back_kernel(place_ref, pack_ref, order_ref, *rest):
+    own_refs, other_refs = rest[0:4], rest[4:8]
+    out_ref, weight, sems = rest[8:]
+    first = place_ref[1] == 0
+
+    @pl.when(first)
+    def _():
+        for copy in fetch_weights(own_refs, weight, sems):
+            copy.wait()
+
+    @pl.when(jnp.logical_not(first))
+    def _():
+        for copy in fetch_weights(other_refs, weight, sems):
+            copy.wait()
+
+    mix_grad = mul(pack_ref[:, :D], weight[...], NT).astype(BF16)
+    out_ref[...] = mul(mix_grad, order_ref[...], NT).astype(BF16)
+
+def space_back(place, packed, order, own, other):
+    scratch = [pltpu.VMEM((D, D), BF16), pltpu.SemaphoreType.DMA((4,))]
+    return call(
+        space_back_kernel, ROWS, specs(smem=1, vmem=2, any=8), scratch, "space_back", 3
+    )(place, packed, order, *own, *other)
 
 def weight_kernel(place_ref, *rest):
     spread_refs, pack_refs = rest[0:2], rest[2:10]
-    out_ref, total = rest[10:]
+    out_refs, total = rest[10:14], rest[14]
     first = place_ref[1] == 0
     for n, pack_ref in enumerate(pack_refs):
         inv = 1.0 / spread_refs[n // 4][0:1, 0:1]
@@ -332,18 +331,28 @@
             total[...] = term
         else:
             total[...] += term
-    out_ref[...] = total[...].astype(BF16)
-
+    for a in range(4):
+        out_refs[a][...] = total[72 * a : 72 * a + 72].astype(BF16)
 
 def weight_grad(place, spreads, packs):
     return call(
         weight_kernel,
-        jax.ShapeDtypeStruct((288, D), BF16),
+        (jax.ShapeDtypeStruct((72, D), BF16),) * 4,
         specs(smem=1, vmem=10),
         [pltpu.VMEM((288, D), F32)],
         "weight_grad",
+        8,
     )(place, *spreads, *packs)
 
+def halves_kernel(*refs):
+    *block_refs, first_ref, second_ref = refs
+    total = sum(ref[...].astype(F32) for ref in block_refs)
+    first_ref[...] = total[:36].astype(BF16)
+    second_ref[...] = total[36:].astype(BF16)
+
+def halves(blocks):
+    out = jax.ShapeDtypeStruct((36, D), BF16)
+    return call(halves_kernel, (out, out), specs(vmem=4), [], "halves", 0)(*blocks)
 
 def finish_kernel(place_ref, own_ref, other_ref, space_ref, time_ref):
     own, other = own_ref[...].astype(F32), other_ref[...].astype(F32)
@@ -351,47 +360,38 @@
     space_ref[...] = jnp.where(first, own, other)
     time_ref[...] = jnp.where(first, other, own)
 
-
 def finish(place, own, other):
     rows = jax.ShapeDtypeStruct((36, D), F32)
     return call(finish_kernel, (rows, rows), specs(smem=1, vmem=2), [], "finish")(place, own, other)
-
 
 def shift_z(value, slope, extra):
     extra = extra if slope > 0 else -extra
     pairs = [(8 * y + z, 8 * y + (z + slope * y + extra) % 8) for y in range(4) for z in range(8)]
     return lax.ppermute(value, ("y", "z"), pairs)
 
-
 def shift(value, axis, size, step):
     return lax.ppermute(value, axis, [(i, (i + step) % size) for i in range(size)])
 
-
 def swap(value):
     return lax.ppermute(value, "core", [(0, 1), (1, 0)])
 
-
 def after(*values):
     return lax.optimization_barrier(values)
 
-
 def add(blocks):
     return sum(block.astype(F32) for block in blocks).astype(BF16)
 
-
 def exchange(value, axis):
     return lax.all_to_all(value, axis, split_axis=0, concat_axis=0, tiled=True)
-
 
 def per_device(hidden_in, spatial_qkv, temporal_qkv, teacher_target, spatial_proj, temporal_proj):
     at_x, at_core, at_y, at_z = (lax.axis_index(a) for a in ("x", "core", "y", "z"))
     place = jnp.stack([at_x, at_core, at_y, at_z]).astype(jnp.int32)
 
     rows = jnp.where(at_core == 0, spatial_proj, temporal_proj)
-    by_z = jnp.concatenate([shift_z(rows, -2, 0), shift_z(rows, -2, 1)])
-    by_z, temporal_qkv = after(by_z, temporal_qkv)
+    by_z = jnp.concatenate([shift_z(rows, -1, 0), shift_z(rows, -1, 4)])
     time_x = exchange(send(temporal_qkv.reshape(TOKENS, 3 * D)), SEQ)
-    by_y = jnp.concatenate([by_z] + [shift(by_z, "y", 4, 4 - a) for a in range(1, 4)])
+    by_y = stack([by_z] + [shift(by_z, "y", 4, 4 - a) for a in range(1, 4)])
 
     by_y, spatial_qkv = after(by_y, spatial_qkv)
     space_x = spatial_qkv.reshape(TOKENS, 3 * D)
@@ -404,7 +404,7 @@
     time_mix, own[1], own[2], own[3] = after(time_mix, own[1], own[2], own[3])
     other += [swap(block) for block in own[1:]]
 
-    time_grad, space_grad, *packs = project(
+    time_grad, *packs = project(
         place,
         hidden_in.reshape(TOKENS, D),
         teacher_target.reshape(TOKENS, D),
@@ -415,21 +415,22 @@
         other,
     )
     time_back = exchange(time_grad, SEQ)
+    space_grad = space_back(place, packs[0], order, own, other)
     packs = [packs[0]] + [shift(packs[b], "x", 4, b) for b in range(1, 4)]
-    spread = spread_of(time_back)
+    time_back, space_grad = after(time_back, space_grad)
+    time_out, spread = attend_back_time(time_x, time_probs, time_back)
     clip_loss = spread[0, :1] - HUBER_DELTA
+    _, spread, packs = after(time_out, spread, packs)
     spreads = [spread, swap(spread)]
-    time_out = attend_back_time(time_x, time_probs, time_back, spread)
-    time_out, spread, packs = after(time_out, spread, packs)
     time_out = exchange(time_out, SEQ)
     packs = packs + [swap(block) for block in packs]
 
     spatial_qkv_grad = attend_back_space(space_x, space_probs, space_grad, spread)
 
     partial = weight_grad(place, spreads, packs)
-    partial = add([partial[:72]] + [shift(partial[72 * a : 72 * a + 72], "y", 4, a) for a in range(1, 4)])
-    piece = add([shift_z(partial[:36], 2, 0), shift_z(partial[36:], 2, 1)])
-    piece, time_out, spatial_qkv_grad = after(piece, time_out, spatial_qkv_grad)
+    partial = halves([partial[0]] + [shift(partial[a], "y", 4, a) for a in range(1, 4)])
+    partial, time_out, spatial_qkv_grad = after(partial, time_out, spatial_qkv_grad)
+    piece = add([shift_z(partial[0], 1, 0), shift_z(partial[1], 1, 4)])
     ends = [shift(piece, "y", 4, a).astype(F32) for a in range(1, 4)]
     final = ((piece.astype(F32) + ends[1]) + (ends[0] + ends[2])).astype(BF16)
     spatial_proj_grad, temporal_proj_grad = finish(place, final, swap(final))
@@ -442,7 +443,6 @@
         temporal_proj_grad,
     )
 
-
 def solution(mesh):
     fine = Mesh(mesh.devices.reshape(4, 2, 4, 8), ("y", "core", "x", "z"))
     clips = P(DP, SEQ, None, None)

time: 193 us -> 175 us (0.907)
  waiting for transfers between devices: 36 us -> 23.4 us
  starting transfers between devices: 93.9 us -> 85.8 us
  Pallas kernels: 49.4 us -> 55.6 us
  other arithmetic: 5.2 us -> 2.61 us
    ppermute x15, starting transfers between devices: 40.6 us -> 28 us  [shift(): lax.ppermute(value, axis, [(i, (i + step) % size) for i in range(size)])]
    ppermute x15, waiting for transfers between devices: 25.5 us -> 14.1 us  [shift(): lax.ppermute(value, axis, [(i, (i + step) % size) for i in range(size)])]
    pallas_call x4 -> x6, Pallas kernels: 24.1 us -> 30.3 us  [the longest x1 8.46 us: project(): call(project_kernel, (sent_rows(D + LANES),) + (packed,) * 4, specs(smem=...]
    all_to_all x4, waiting for transfers between devices: 6.15 us -> 0.2 us  [exchange(): return lax.all_to_all(value, axis, split_axis=0, concat_axis=0, tiled=True)]
    ppermute x4, starting transfers between devices: 10.2 us -> 15.3 us  [shift_z(): return lax.ppermute(value, ('y', 'z'), pairs)]
    ppermute x10, waiting for transfers between devices: 3.48 us -> 6.2 us  [swap(): return lax.ppermute(value, 'core', [(0, 1), (1, 0)])]
    ppermute x4, waiting for transfers between devices: 0.93 us -> 2.91 us  [shift_z(): return lax.ppermute(value, ('y', 'z'), pairs)]
    convert_element_type x2 -> x1, other arithmetic: 1.97 us -> 0.03 us  [add(): return sum((block.astype(F32) for block in blocks)).astype(BF16)]
  transfers between devices with their start and end apart: 33 -> 33, of which waited for: 14 -> 14; matrix products, arithmetic and copies ran while one was open for 3% -> 2% of each run, Pallas kernels for 18% -> 26%
where the time goes in v3:
time: 175 us; the launch traced here: 174 us
  starting transfers between devices  85.8 us (49%)
  Pallas kernels  55.6 us (32%)
  waiting for transfers between devices  23.4 us (13%)
  local copies, waits for them, and re-layouts  3.52 us (2%)
  other arithmetic  2.61 us (1%)
  between operations  2.59 us (1%)
    ppermute x15, starting transfers between devices, shift(): lax.ppermute(value, axis, [(i, (i + step) % size) for i in range(size)])  28 us
    all_to_all x4, starting transfers between devices, exchange(): return lax.all_to_all(value, axis, split_axis=0, concat_axis=0, tiled=True)  27.3 us
    ppermute x4, starting transfers between devices, shift_z(): return lax.ppermute(value, ('y', 'z'), pairs)  15.3 us
    ppermute x10, starting transfers between devices, swap(): return lax.ppermute(value, 'core', [(0, 1), (1, 0)])  15.2 us
    ppermute x15, waiting for transfers between devices, shift(): lax.ppermute(value, axis, [(i, (i + step) % size) for i in range(size)])  14.1 us
    pallas_call x1, Pallas kernels, project(): call(project_kernel, (sent_rows(D + LANES),) + (packed,) * 4, specs(smem=...  8.46 us
    pallas_call x1, Pallas kernels, attend_back_time(): call(attend_back_time_kernel, (sent_rows(3 * D), jax.ShapeDtypeStruct((8,...  7.27 us
    pallas_call x1, Pallas kernels, attend_back_space(): call(attend_back_space_kernel, jax.ShapeDtypeStruct((TOKENS, 3 * D), BF16...  7.11 us
  transfers between devices with their start and end apart: 33, of which 14 were waited for; matrix products, arithmetic and copies ran while one was open for 2% of the time, Pallas kernels for 26%

profile of v3, /device:TPU:1, one launch (start us, length us, event | category | flops | bytes accessed | tf_op | source)
XLA Modules:
  0.0 173.6 jit_solution(4608588031406069824)
XLA Ops:
  1.6 7.8 %collective-permute-start.1 = (bf16[36,1152]{1,0:T(8,128)(2,1)S(1)}, bf16[36,1152]{1,0:T(8,128)(2,1)}, u32[]{:S(2)}, u32[]{:S(2)}) collective-permute-start(bf16[36,1152]{1,0:T(8,128)(2,1)S(1)} %broadcast_select_fusion), channel_id=1, source_target_pairs={{0,4},{1,5},{2,6},{3,7},{4,0},{5,1},{6,2},{7,3},{64,67},{65,68},{6... | collective-permute-start | bytes 248840 | tf_op jit(solution)/shard_map/ppermute | solution.py:370
  9.4 1.3 collective-permute-start
  10.7 2.5 %send_order.1 = bf16[32,4,3456]{2,1,0:T(4,128)(2,1)} custom-call(bf16[128,3456]{1,0:T(8,128)(2,1)} %bitcast.11), custom_call_target="tpu_custom_call" | custom-call | flops 3000000000 | bytes 1 | tf_op jit(solution)/shard_map/send_order/pallas_call | solution.py:155
  13.2 5.8 %all-to-all-start = ((bf16[32,4,3456]{2,1,0:T(4,128)(2,1)}), bf16[32,4,3456]{2,1,0:T(4,128)(2,1)S(1)}, u32[]{:S(2)}, u32[]{:S(2)}) async-start(bf16[32,4,3456]{2,1,0:T(4,128)(2,1)} %send_order.1), calls=%async_computation | async-start | bytes 1769472 | tf_op jit(solution)/shard_map/all_to_all | solution.py:385
  19.0 1.0 pad_maximum_fusion.refs_0_
  19.9 3.9 %collective-permute-start.4 = (bf16[72,1152]{1,0:T(8,128)(2,1)S(1)}, bf16[72,1152]{1,0:T(8,128)(2,1)S(1)}, u32[]{:S(2)}, u32[]{:S(2)}) collective-permute-start(bf16[72,1152]{1,0:T(8,128)(2,1)S(1)} %pad_maximum_fusion.refs_0_), channel_id=1, source_target_pairs={{0,64},{64,128},{128,192},{192,0},{1,65},{65,129},{129,193},{193,1... | collective-permute-start | bytes 497672 | tf_op jit(solution)/shard_map/ppermute | solution.py:373
  23.9 1.7 collective-permute-start.3
  25.6 2.0 %collective-permute-start.2 = (bf16[72,1152]{1,0:T(8,128)(2,1)S(1)}, bf16[72,1152]{1,0:T(8,128)(2,1)}, u32[]{:S(2)}, u32[]{:S(2)}) collective-permute-start(bf16[72,1152]{1,0:T(8,128)(2,1)S(1)} %pad_maximum_fusion.refs_0_), channel_id=1, source_target_pairs={{0,192},{64,0},{128,64},{192,128},{1,193},{65,1},{129,65},{193,129... | collective-permute-start | bytes 497672 | tf_op jit(solution)/shard_map/ppermute | solution.py:373
  28.2 3.4 %collective-permute-done.3.refs_2_ = bf16[72,1152]{1,0:T(8,128)(2,1)S(1)} collective-permute-done((bf16[72,1152]{1,0:T(8,128)(2,1)S(1)}, bf16[72,1152]{1,0:T(8,128)(2,1)S(1)}, u32[]{:S(2)}, u32[]{:S(2)}) %collective-permute-start.3) | collective-permute-done | bytes 165920 | tf_op jit(solution)/shard_map/ppermute | solution.py:373
  32.3 2.0 %stack.21.rest_0_ = bf16[288,1152]{1,0:T(8,128)(2,1)} custom-call(bf16[72,1152]{1,0:T(8,128)(2,1)} %copy-done.4, bf16[72,1152]{1,0:T(8,128)(2,1)} %collective-permute-done.2.refs_1_, bf16[72,1152]{1,0:T(8,128)(2,1)} %copy-done.8, bf16[72,1152]{1,0:T(8,128)(2,1)} %copy-done.7), custom_call_target="tpu_custom_call" | custom-call | flops 1000000000 | bytes 1 | tf_op jit(solution)/shard_map/stack/pallas_call | solution.py:140
  34.3 1.2 collective-permute-start.7
  35.6 2.4 %collective-permute-start.6 = (bf16[288,1152]{1,0:T(8,128)(2,1)}, bf16[288,1152]{1,0:T(8,128)(2,1)}, u32[]{:S(2)}, u32[]{:S(2)}) collective-permute-start(bf16[288,1152]{1,0:T(8,128)(2,1)} %stack.21.rest_0_), channel_id=1, source_target_pairs={{0,16},{8,24},{16,0},{24,8},{1,17},{9,25},{17,1},{25,9},{2,18},{10... | collective-permute-start | bytes 1990664 | tf_op jit(solution)/shard_map/ppermute | solution.py:373
  38.9 6.4 %attend_space.1 = (bf16[128,1152]{1,0:T(8,128)(2,1)}, f32[16,128,128]{2,1,0:T(8,128)}, bf16[1152,1152]{1,0:T(8,128)(2,1)}) custom-call(s32[4]{0:T(128)} %pad_add_fusion.place_ref, bf16[128,3456]{1,0:T(8,128)(2,1)} %bitcast.12), custom_call_target="tpu_custom_call" | custom-call | flops 14000000000 | bytes 1 | tf_op jit(solution)/shard_map/attend_space/pallas_call | solution.py:124
  46.1 5.2 %attend_time.1 = (bf16[32,4,1152]{2,1,0:T(4,128)(2,1)}, f32[16,128,128]{2,1,0:T(8,128)}) custom-call(bf16[32,4,3456]{2,1,0:T(4,128)(2,1)} %copy-done), custom_call_target="tpu_custom_call" | custom-call | flops 3000000000 | bytes 1 | tf_op jit(solution)/shard_map/attend_time/pallas_call | solution.py:149
  51.3 7.1 %all-to-all-start.1 = ((bf16[32,4,1152]{2,1,0:T(4,128)(2,1)}), bf16[32,4,1152]{2,1,0:T(4,128)(2,1)S(1)}, u32[]{:S(2)}, u32[]{:S(2)}) async-start(bf16[32,4,1152]{2,1,0:T(4,128)(2,1)} %get-tuple-element.52), calls=%async_computation.1 | async-start | bytes 589824 | tf_op jit(solution)/shard_map/all_to_all | solution.py:385
  58.5 3.9 %collective-permute-start.8 = (bf16[288,1152]{1,0:T(8,128)(2,1)}, bf16[288,1152]{1,0:T(8,128)(2,1)S(1)}, u32[]{:S(2)}, u32[]{:S(2)}) collective-permute-start(bf16[288,1152]{1,0:T(8,128)(2,1)} %stack.21.rest_0_), channel_id=1, source_target_pairs={{0,32},{32,0},{1,33},{33,1},{2,34},{34,2},{3,35},{35,3},{4,36},{36... | collective-permute-start | bytes 1990664 | tf_op jit(solution)/shard_map/ppermute | solution.py:376
  62.4 7.4 %collective-permute-done.6.rest_2_ = bf16[288,1152]{1,0:T(8,128)(2,1)} collective-permute-done((bf16[288,1152]{1,0:T(8,128)(2,1)}, bf16[288,1152]{1,0:T(8,128)(2,1)}, u32[]{:S(2)}, u32[]{:S(2)}) %collective-permute-start.6) | collective-permute-done | bytes 663584 | tf_op jit(solution)/shard_map/ppermute | solution.py:373
  70.3 3.1 %collective-permute-start.9 = (bf16[288,1152]{1,0:T(8,128)(2,1)}, bf16[288,1152]{1,0:T(8,128)(2,1)}, u32[]{:S(2)}, u32[]{:S(2)}) collective-permute-start(bf16[288,1152]{1,0:T(8,128)(2,1)} %collective-permute-done.5.rest_1_), channel_id=1, source_target_pairs={{0,32},{32,0},{1,33},{33,1},{2,34},{34,2},{3,35},{35,3},{4,36},{36... | collective-permute-start | bytes 1990664 | tf_op jit(solution)/shard_map/ppermute | solution.py:376
  73.9 1.6 collective-permute-done.9.rest_5_
  75.5 0.9 collective-permute-done.10.rest_6_
  76.4 0.9 collective-permute-done.11.rest_7_
  77.4 8.5 %project.1 = (bf16[32,4,1280]{2,1,0:T(4,128)(2,1)}, bf16[128,1728]{1,0:T(8,128)(2,1)}, bf16[128,1728]{1,0:T(8,128)(2,1)}, bf16[128,1728]{1,0:T(8,128)(2,1)}, bf16[128,1728]{1,0:T(8,128)(2,1)}) custom-call(s32[4]{0:T(128)} %pad_add_fusion.place_ref, bf16[32,4,1152]{2,1,0:T(4,128)(2,1)} %copy-done.3, bf16[128,1152]{1,0:T(8,128)(2,1)} %bitcast.14, ...), custom_call_target="tpu_custom_call" | custom-call | flops 8000000000 | bytes 1 | tf_op jit(solution)/shard_map/project/pallas_call | solution.py:281
  85.9 7.4 %all-to-all-start.2 = ((bf16[32,4,1280]{2,1,0:T(4,128)(2,1)}), bf16[32,4,1280]{2,1,0:T(4,128)(2,1)S(1)}, u32[]{:S(2)}, u32[]{:S(2)}) async-start(bf16[32,4,1280]{2,1,0:T(4,128)(2,1)} %get-tuple-element.60), calls=%async_computation.2 | async-start | bytes 655360 | tf_op jit(solution)/shard_map/all_to_all | solution.py:385
  93.2 1.3 collective-permute-start.12
  94.5 2.4 %collective-permute-start.13 = (bf16[128,1728]{1,0:T(8,128)(2,1)}, bf16[128,1728]{1,0:T(8,128)(2,1)}, u32[]{:S(2)}, u32[]{:S(2)}) collective-permute-start(bf16[128,1728]{1,0:T(8,128)(2,1)} %get-tuple-element.66), channel_id=1, source_target_pairs={{0,16},{8,24},{16,0},{24,8},{1,17},{9,25},{17,1},{25,9},{2,18},{10... | collective-permute-start | bytes 1327112 | tf_op jit(solution)/shard_map/ppermute | solution.py:373
  97.0 1.1 collective-permute-start.14
  98.1 6.0 %space_back.1.grad_ref = bf16[128,1152]{1,0:T(8,128)(2,1)} custom-call(s32[4]{0:T(128)} %pad_add_fusion.place_ref, bf16[128,1728]{1,0:T(8,128)(2,1)} %get-tuple-element.69.pack_ref.rest_2_, bf16[1152,1152]{1,0:T(8,128)(2,1)} %get-tuple-element.56.order_any.order_ref, bf16[288,1152]{1,0:T(8,128)(2,1)} %stack.21.rest_0_, ...), custom_call_target="tpu_custom_call" | custom-call | flops 3000000000 | bytes 1 | tf_op jit(solution)/shard_map/space_back/pallas_call | solution.py:317
  104.9 7.3 %attend_back_time.1 = (bf16[32,4,3456]{2,1,0:T(4,128)(2,1)}, f32[8,128]{1,0:T(8,128)}) custom-call(bf16[32,4,3456]{2,1,0:T(4,128)(2,1)} %copy-done, f32[16,128,128]{2,1,0:T(8,128)} %get-tuple-element.51.probs_ref, bf16[32,4,1280]{2,1,0:T(4,128)(2,1)} %copy-done.2), custom_call_target="tpu_custom_call" | custom-call | flops 5000000000 | bytes 1 | tf_op jit(solution)/shard_map/attend_back_time/pallas_call | solution.py:196
  112.2 7.0 %all-to-all-start.3 = ((bf16[32,4,3456]{2,1,0:T(4,128)(2,1)}), bf16[32,4,3456]{2,1,0:T(4,128)(2,1)S(1)}, u32[]{:S(2)}, u32[]{:S(2)}) async-start(bf16[32,4,3456]{2,1,0:T(4,128)(2,1)} %get-tuple-element.64), calls=%async_computation.3 | async-start | bytes 1769472 | tf_op jit(solution)/shard_map/all_to_all | solution.py:385
  119.2 1.5 collective-permute-done.13.rest_4_
  120.7 1.1 collective-permute-start.16
  122.9 1.3 collective-permute-done.15.rest_1_
  125.6 4.5 %weight_grad.1 = (bf16[72,1152]{1,0:T(8,128)(2,1)}, bf16[72,1152]{1,0:T(8,128)(2,1)}, bf16[72,1152]{1,0:T(8,128)(2,1)}, bf16[72,1152]{1,0:T(8,128)(2,1)}) custom-call(s32[4]{0:T(128)} %pad_add_fusion.place_ref, f32[8,128]{1,0:T(8,128)} %get-tuple-element.68.rest_0_.spread_ref, f32[8,128]{1,0:T(8,128)} %copy-done.9, ...), custom_call_target="tpu_custom_call" | custom-call | flops 8000000000 | bytes 1 | tf_op jit(solution)/shard_map/weight_grad/pallas_call | solution.py:338
  130.2 2.1 %collective-permute-start.20 = (bf16[72,1152]{1,0:T(8,128)(2,1)}, bf16[72,1152]{1,0:T(8,128)(2,1)}, u32[]{:S(2)}, u32[]{:S(2)}) collective-permute-start(bf16[72,1152]{1,0:T(8,128)(2,1)} %get-tuple-element.74), channel_id=1, source_target_pairs={{0,64},{64,128},{128,192},{192,0},{1,65},{65,129},{129,193},{193,1... | collective-permute-start | bytes 497672 | tf_op jit(solution)/shard_map/ppermute | solution.py:373
  132.3 3.1 %collective-permute-start.21 = (bf16[72,1152]{1,0:T(8,128)(2,1)}, bf16[72,1152]{1,0:T(8,128)(2,1)}, u32[]{:S(2)}, u32[]{:S(2)}) collective-permute-start(bf16[72,1152]{1,0:T(8,128)(2,1)} %get-tuple-element.75), channel_id=1, source_target_pairs={{0,128},{64,192},{128,0},{192,64},{1,129},{65,193},{129,1},{193,65... | collective-permute-start | bytes 497672 | tf_op jit(solution)/shard_map/ppermute | solution.py:373
  135.3 1.3 collective-permute-start.22
  136.7 7.1 %attend_back_space.1 = bf16[128,3456]{1,0:T(8,128)(2,1)} custom-call(bf16[128,3456]{1,0:T(8,128)(2,1)} %bitcast.13, f32[16,128,128]{2,1,0:T(8,128)} %get-tuple-element.79.probs_ref, bf16[128,1152]{1,0:T(8,128)(2,1)} %space_back.1.grad_ref, f32[8,128]{1,0:T(8,128)} %get-tuple-element.68.rest_0_.spread_ref), custom_call_target="tpu_custom_call" | custom-call | flops 1000000000 | bytes 1 | tf_op jit(solution)/shard_map/attend_back_space/pallas_call | solution.py:209
  143.8 1.9 %halves.1 = (bf16[36,1152]{1,0:T(8,128)(2,1)}, bf16[36,1152]{1,0:T(8,128)(2,1)}) custom-call(bf16[72,1152]{1,0:T(8,128)(2,1)} %get-tuple-element.73.refs_0_, bf16[72,1152]{1,0:T(8,128)(2,1)} %collective-permute-done.20.refs_1_, bf16[72,1152]{1,0:T(8,128)(2,1)} %collective-permute-done.21.refs_2_, bf16[72,1152]{1,0:T(8,128)(2,1)} %collective-permute-done.22.refs_3_), custom_call_target="tpu_custom_call" | custom-call | bytes 1 | tf_op jit(solution)/shard_map/halves/pallas_call | solution.py:355
  145.7 1.5 collective-permute-start.23
  147.2 4.7 %collective-permute-start.24 = (bf16[36,1152]{1,0:T(8,128)(2,1)}, bf16[36,1152]{1,0:T(8,128)(2,1)S(1)}, u32[]{:S(2)}, u32[]{:S(2)}) collective-permute-start(bf16[36,1152]{1,0:T(8,128)(2,1)} %get-tuple-element.84), channel_id=1, source_target_pairs={{0,4},{1,5},{2,6},{3,7},{4,0},{5,1},{6,2},{7,3},{64,69},{65,70},{6... | collective-permute-start | bytes 248840 | tf_op jit(solution)/shard_map/ppermute | solution.py:370
  151.9 2.9 %collective-permute-done.24 = bf16[36,1152]{1,0:T(8,128)(2,1)S(1)} collective-permute-done((bf16[36,1152]{1,0:T(8,128)(2,1)}, bf16[36,1152]{1,0:T(8,128)(2,1)S(1)}, u32[]{:S(2)}, u32[]{:S(2)}) %collective-permute-start.24) | collective-permute-done | bytes 82976 | tf_op jit(solution)/shard_map/ppermute | solution.py:370
  154.9 2.2 %collective-permute-start.27 = (bf16[36,1152]{1,0:T(8,128)(2,1)S(1)}, bf16[36,1152]{1,0:T(8,128)(2,1)S(1)}, u32[]{:S(2)}, u32[]{:S(2)}) collective-permute-start(bf16[36,1152]{1,0:T(8,128)(2,1)S(1)} %add_convert_fusion.1), channel_id=1, source_target_pairs={{0,192},{64,0},{128,64},{192,128},{1,193},{65,1},{129,65},{193,129... | collective-permute-start | bytes 248840 | tf_op jit(solution)/shard_map/ppermute | solution.py:373
  157.0 2.3 %collective-permute-start.25 = (bf16[36,1152]{1,0:T(8,128)(2,1)S(1)}, bf16[36,1152]{1,0:T(8,128)(2,1)S(1)}, u32[]{:S(2)}, u32[]{:S(2)}) collective-permute-start(bf16[36,1152]{1,0:T(8,128)(2,1)S(1)} %add_convert_fusion.1), channel_id=1, source_target_pairs={{0,128},{64,192},{128,0},{192,64},{1,129},{65,193},{129,1},{193,65... | collective-permute-start | bytes 248840 | tf_op jit(solution)/shard_map/ppermute | solution.py:373
  159.3 1.2 slice.3
  161.2 1.4 collective-permute-done.26
  162.7 5.5 %collective-permute-start.28 = (bf16[36,1152]{1,0:T(8,128)(2,1)S(1)}, bf16[36,1152]{1,0:T(8,128)(2,1)}, u32[]{:S(2)}, u32[]{:S(2)}) collective-permute-start(bf16[36,1152]{1,0:T(8,128)(2,1)S(1)} %add_convert_fusion.own_ref), channel_id=1, source_target_pairs={{0,32},{32,0},{1,33},{33,1},{2,34},{34,2},{3,35},{35,3},{4,36},{36... | collective-permute-start | bytes 248840 | tf_op jit(solution)/shard_map/ppermute | solution.py:376
  168.2 2.5 %natural_order.1 = bf16[128,3456]{1,0:T(8,128)(2,1)} custom-call(bf16[32,4,3456]{2,1,0:T(4,128)(2,1)} %copy-done.1), custom_call_target="tpu_custom_call" | custom-call | flops 3000000000 | bytes 1 | tf_op jit(solution)/shard_map/natural_order/pallas_call | solution.py:163
  170.7 1.7 finish.1
  (56 shorter events, 8.3 us)
Async XLA Ops:
  1.6 17.4 %collective-permute-start.1 = (bf16[36,1152]{1,0:T(8,128)(2,1)S(1)}, bf16[36,1152]{1,0:T(8,128)(2,1)}, u32[]{:S(2)}, u32[]{:S(2)}) collective-permute-start(bf16[36,1152]{1,0:T(8,128)(2,1)S(1)} %broadcast_select_fusion), channel_id=1, source_target_pairs={{0,4},{1,5},{2,6},{3,7},{4,0},{5,1},{6,2},{7,3},{64,67},{65,68},{6... | collective-permute-start | bytes 248840 | tf_op jit(solution)/shard_map/ppermute | solution.py:370
  9.4 9.6 %collective-permute-start = (bf16[36,1152]{1,0:T(8,128)(2,1)S(1)}, bf16[36,1152]{1,0:T(8,128)(2,1)}, u32[]{:S(2)}, u32[]{:S(2)}) collective-permute-start(bf16[36,1152]{1,0:T(8,128)(2,1)S(1)} %broadcast_select_fusion), channel_id=1, source_target_pairs={{0,0},{1,1},{2,2},{3,3},{4,4},{5,5},{6,6},{7,7},{64,71},{65,64},{6... | collective-permute-start | bytes 248840 | tf_op jit(solution)/shard_map/ppermute | solution.py:370
  13.2 32.1 %all-to-all-start = ((bf16[32,4,3456]{2,1,0:T(4,128)(2,1)}), bf16[32,4,3456]{2,1,0:T(4,128)(2,1)S(1)}, u32[]{:S(2)}, u32[]{:S(2)}) async-start(bf16[32,4,3456]{2,1,0:T(4,128)(2,1)} %send_order.1), calls=%async_computation | async-start | bytes 1769472 | tf_op jit(solution)/shard_map/all_to_all | solution.py:385
  19.9 5.7 %copy-start.4 = (bf16[72,1152]{1,0:T(8,128)(2,1)}, bf16[72,1152]{1,0:T(8,128)(2,1)S(1)}, u32[]{:S(2)}) copy-start(bf16[72,1152]{1,0:T(8,128)(2,1)S(1)} %pad_maximum_fusion.refs_0_) | copy-start | bytes 497668
  19.9 8.3 %collective-permute-start.4 = (bf16[72,1152]{1,0:T(8,128)(2,1)S(1)}, bf16[72,1152]{1,0:T(8,128)(2,1)S(1)}, u32[]{:S(2)}, u32[]{:S(2)}) collective-permute-start(bf16[72,1152]{1,0:T(8,128)(2,1)S(1)} %pad_maximum_fusion.refs_0_), channel_id=1, source_target_pairs={{0,64},{64,128},{128,192},{192,0},{1,65},{65,129},{129,193},{193,1... | collective-permute-start | bytes 497672 | tf_op jit(solution)/shard_map/ppermute | solution.py:373
  23.9 7.7 %collective-permute-start.3 = (bf16[72,1152]{1,0:T(8,128)(2,1)S(1)}, bf16[72,1152]{1,0:T(8,128)(2,1)S(1)}, u32[]{:S(2)}, u32[]{:S(2)}) collective-permute-start(bf16[72,1152]{1,0:T(8,128)(2,1)S(1)} %pad_maximum_fusion.refs_0_), channel_id=1, source_target_pairs={{0,128},{64,192},{128,0},{192,64},{1,129},{65,193},{129,1},{193,65... | collective-permute-start | bytes 497672 | tf_op jit(solution)/shard_map/ppermute | solution.py:373
  25.6 6.7 %collective-permute-start.2 = (bf16[72,1152]{1,0:T(8,128)(2,1)S(1)}, bf16[72,1152]{1,0:T(8,128)(2,1)}, u32[]{:S(2)}, u32[]{:S(2)}) collective-permute-start(bf16[72,1152]{1,0:T(8,128)(2,1)S(1)} %pad_maximum_fusion.refs_0_), channel_id=1, source_target_pairs={{0,192},{64,0},{128,64},{192,128},{1,193},{65,1},{129,65},{193,129... | collective-permute-start | bytes 497672 | tf_op jit(solution)/shard_map/ppermute | solution.py:373
  28.2 3.4 %copy-start.7 = (bf16[72,1152]{1,0:T(8,128)(2,1)}, bf16[72,1152]{1,0:T(8,128)(2,1)S(1)}, u32[]{:S(2)}) copy-start(bf16[72,1152]{1,0:T(8,128)(2,1)S(1)} %collective-permute-done.4.refs_3_) | copy-start | bytes 497668
  31.6 0.7 copy-start.8
  34.3 28.1 %collective-permute-start.7 = (bf16[288,1152]{1,0:T(8,128)(2,1)}, bf16[288,1152]{1,0:T(8,128)(2,1)}, u32[]{:S(2)}, u32[]{:S(2)}) collective-permute-start(bf16[288,1152]{1,0:T(8,128)(2,1)} %stack.21.rest_0_), channel_id=1, source_target_pairs={{0,8},{8,16},{16,24},{24,0},{1,9},{9,17},{17,25},{25,1},{2,10},{10... | collective-permute-start | bytes 1990664 | tf_op jit(solution)/shard_map/ppermute | solution.py:373
  35.6 34.3 %collective-permute-start.6 = (bf16[288,1152]{1,0:T(8,128)(2,1)}, bf16[288,1152]{1,0:T(8,128)(2,1)}, u32[]{:S(2)}, u32[]{:S(2)}) collective-permute-start(bf16[288,1152]{1,0:T(8,128)(2,1)} %stack.21.rest_0_), channel_id=1, source_target_pairs={{0,16},{8,24},{16,0},{24,8},{1,17},{9,25},{17,1},{25,9},{2,18},{10... | collective-permute-start | bytes 1990664 | tf_op jit(solution)/shard_map/ppermute | solution.py:373
  38.0 32.1 %collective-permute-start.5 = (bf16[288,1152]{1,0:T(8,128)(2,1)}, bf16[288,1152]{1,0:T(8,128)(2,1)}, u32[]{:S(2)}, u32[]{:S(2)}) collective-permute-start(bf16[288,1152]{1,0:T(8,128)(2,1)} %stack.21.rest_0_), channel_id=1, source_target_pairs={{0,24},{8,0},{16,8},{24,16},{1,25},{9,1},{17,9},{25,17},{2,26},{10... | collective-permute-start | bytes 1990664 | tf_op jit(solution)/shard_map/ppermute | solution.py:373
  45.2 0.9 copy-start
  51.3 19.0 %all-to-all-start.1 = ((bf16[32,4,1152]{2,1,0:T(4,128)(2,1)}), bf16[32,4,1152]{2,1,0:T(4,128)(2,1)S(1)}, u32[]{:S(2)}, u32[]{:S(2)}) async-start(bf16[32,4,1152]{2,1,0:T(4,128)(2,1)} %get-tuple-element.52), calls=%async_computation.1 | async-start | bytes 589824 | tf_op jit(solution)/shard_map/all_to_all | solution.py:385
  58.5 15.4 %collective-permute-start.8 = (bf16[288,1152]{1,0:T(8,128)(2,1)}, bf16[288,1152]{1,0:T(8,128)(2,1)S(1)}, u32[]{:S(2)}, u32[]{:S(2)}) collective-permute-start(bf16[288,1152]{1,0:T(8,128)(2,1)} %stack.21.rest_0_), channel_id=1, source_target_pairs={{0,32},{32,0},{1,33},{33,1},{2,34},{34,2},{3,35},{35,3},{4,36},{36... | collective-permute-start | bytes 1990664 | tf_op jit(solution)/shard_map/ppermute | solution.py:376
  70.3 7.1 %copy-start.3 = (bf16[32,4,1152]{2,1,0:T(4,128)(2,1)}, bf16[32,4,1152]{2,1,0:T(4,128)(2,1)S(1)}, u32[]{:S(2)}) copy-start(bf16[32,4,1152]{2,1,0:T(4,128)(2,1)S(1)} %all-to-all-done.1.time_ref) | copy-start | bytes 884740
  70.3 5.2 %collective-permute-start.9 = (bf16[288,1152]{1,0:T(8,128)(2,1)}, bf16[288,1152]{1,0:T(8,128)(2,1)}, u32[]{:S(2)}, u32[]{:S(2)}) collective-permute-start(bf16[288,1152]{1,0:T(8,128)(2,1)} %collective-permute-done.5.rest_1_), channel_id=1, source_target_pairs={{0,32},{32,0},{1,33},{33,1},{2,34},{34,2},{3,35},{35,3},{4,36},{36... | collective-permute-start | bytes 1990664 | tf_op jit(solution)/shard_map/ppermute | solution.py:376
  73.4 3.0 %collective-permute-start.10 = (bf16[288,1152]{1,0:T(8,128)(2,1)}, bf16[288,1152]{1,0:T(8,128)(2,1)}, u32[]{:S(2)}, u32[]{:S(2)}) collective-permute-start(bf16[288,1152]{1,0:T(8,128)(2,1)} %collective-permute-done.6.rest_2_), channel_id=1, source_target_pairs={{0,32},{32,0},{1,33},{33,1},{2,34},{34,2},{3,35},{35,3},{4,36},{36... | collective-permute-start | bytes 1990664 | tf_op jit(solution)/shard_map/ppermute | solution.py:376
  73.5 3.9 %collective-permute-start.11 = (bf16[288,1152]{1,0:T(8,128)(2,1)}, bf16[288,1152]{1,0:T(8,128)(2,1)}, u32[]{:S(2)}, u32[]{:S(2)}) collective-permute-start(bf16[288,1152]{1,0:T(8,128)(2,1)} %collective-permute-done.7.rest_3_), channel_id=1, source_target_pairs={{0,32},{32,0},{1,33},{33,1},{2,34},{34,2},{3,35},{35,3},{4,36},{36... | collective-permute-start | bytes 1990664 | tf_op jit(solution)/shard_map/ppermute | solution.py:376
  73.9 3.5 %copy-start.6 = (bf16[288,1152]{1,0:T(8,128)(2,1)}, bf16[288,1152]{1,0:T(8,128)(2,1)S(1)}, u32[]{:S(2)}) copy-start(bf16[288,1152]{1,0:T(8,128)(2,1)S(1)} %collective-permute-done.8.rest_4_) | copy-start | bytes 1990660
  85.9 18.3 %all-to-all-start.2 = ((bf16[32,4,1280]{2,1,0:T(4,128)(2,1)}), bf16[32,4,1280]{2,1,0:T(4,128)(2,1)S(1)}, u32[]{:S(2)}, u32[]{:S(2)}) async-start(bf16[32,4,1280]{2,1,0:T(4,128)(2,1)} %get-tuple-element.60), calls=%async_computation.2 | async-start | bytes 655360 | tf_op jit(solution)/shard_map/all_to_all | solution.py:385
  93.2 26.0 %collective-permute-start.12 = (bf16[128,1728]{1,0:T(8,128)(2,1)}, bf16[128,1728]{1,0:T(8,128)(2,1)}, u32[]{:S(2)}, u32[]{:S(2)}) collective-permute-start(bf16[128,1728]{1,0:T(8,128)(2,1)} %get-tuple-element.65), channel_id=1, source_target_pairs={{0,8},{8,16},{16,24},{24,0},{1,9},{9,17},{17,25},{25,1},{2,10},{10... | collective-permute-start | bytes 1327112 | tf_op jit(solution)/shard_map/ppermute | solution.py:373
  94.5 26.2 %collective-permute-start.13 = (bf16[128,1728]{1,0:T(8,128)(2,1)}, bf16[128,1728]{1,0:T(8,128)(2,1)}, u32[]{:S(2)}, u32[]{:S(2)}) collective-permute-start(bf16[128,1728]{1,0:T(8,128)(2,1)} %get-tuple-element.66), channel_id=1, source_target_pairs={{0,16},{8,24},{16,0},{24,8},{1,17},{9,25},{17,1},{25,9},{2,18},{10... | collective-permute-start | bytes 1327112 | tf_op jit(solution)/shard_map/ppermute | solution.py:373
  97.0 23.8 %collective-permute-start.14 = (bf16[128,1728]{1,0:T(8,128)(2,1)}, bf16[128,1728]{1,0:T(8,128)(2,1)}, u32[]{:S(2)}, u32[]{:S(2)}) collective-permute-start(bf16[128,1728]{1,0:T(8,128)(2,1)} %get-tuple-element.67), channel_id=1, source_target_pairs={{0,24},{8,0},{16,8},{24,16},{1,25},{9,1},{17,9},{25,17},{2,26},{10... | collective-permute-start | bytes 1327112 | tf_op jit(solution)/shard_map/ppermute | solution.py:373
  104.2 0.7 copy-start.2
  112.2 33.5 %all-to-all-start.3 = ((bf16[32,4,3456]{2,1,0:T(4,128)(2,1)}), bf16[32,4,3456]{2,1,0:T(4,128)(2,1)S(1)}, u32[]{:S(2)}, u32[]{:S(2)}) async-start(bf16[32,4,3456]{2,1,0:T(4,128)(2,1)} %get-tuple-element.64), calls=%async_computation.3 | async-start | bytes 1769472 | tf_op jit(solution)/shard_map/all_to_all | solution.py:385
  120.7 3.5 %collective-permute-start.16 = (bf16[128,1728]{1,0:T(8,128)(2,1)}, bf16[128,1728]{1,0:T(8,128)(2,1)}, u32[]{:S(2)}, u32[]{:S(2)}) collective-permute-start(bf16[128,1728]{1,0:T(8,128)(2,1)} %get-tuple-element.69.pack_ref.rest_2_), channel_id=1, source_target_pairs={{0,32},{32,0},{1,33},{33,1},{2,34},{34,2},{3,35},{35,3},{4,36},{36... | collective-permute-start | bytes 1327112 | tf_op jit(solution)/shard_map/ppermute | solution.py:376
  121.9 2.4 %collective-permute-start.17 = (bf16[128,1728]{1,0:T(8,128)(2,1)}, bf16[128,1728]{1,0:T(8,128)(2,1)}, u32[]{:S(2)}, u32[]{:S(2)}) collective-permute-start(bf16[128,1728]{1,0:T(8,128)(2,1)} %collective-permute-done.12.rest_3_), channel_id=1, source_target_pairs={{0,32},{32,0},{1,33},{33,1},{2,34},{34,2},{3,35},{35,3},{4,36},{36... | collective-permute-start | bytes 1327112 | tf_op jit(solution)/shard_map/ppermute | solution.py:376
  121.9 3.1 %collective-permute-start.18 = (bf16[128,1728]{1,0:T(8,128)(2,1)}, bf16[128,1728]{1,0:T(8,128)(2,1)}, u32[]{:S(2)}, u32[]{:S(2)}) collective-permute-start(bf16[128,1728]{1,0:T(8,128)(2,1)} %collective-permute-done.13.rest_4_), channel_id=1, source_target_pairs={{0,32},{32,0},{1,33},{33,1},{2,34},{34,2},{3,35},{35,3},{4,36},{36... | collective-permute-start | bytes 1327112 | tf_op jit(solution)/shard_map/ppermute | solution.py:376
  122.4 3.2 %collective-permute-start.19 = (bf16[128,1728]{1,0:T(8,128)(2,1)}, bf16[128,1728]{1,0:T(8,128)(2,1)}, u32[]{:S(2)}, u32[]{:S(2)}) collective-permute-start(bf16[128,1728]{1,0:T(8,128)(2,1)} %collective-permute-done.14.rest_5_), channel_id=1, source_target_pairs={{0,32},{32,0},{1,33},{33,1},{2,34},{34,2},{3,35},{35,3},{4,36},{36... | collective-permute-start | bytes 1327112 | tf_op jit(solution)/shard_map/ppermute | solution.py:376
  122.4 1.8 %collective-permute-start.15 = (f32[8,128]{1,0:T(8,128)}, f32[8,128]{1,0:T(8,128)S(1)}, u32[]{:S(2)}, u32[]{:S(2)}) collective-permute-start(f32[8,128]{1,0:T(8,128)} %get-tuple-element.68.rest_0_.spread_ref), channel_id=1, source_target_pairs={{0,32},{32,0},{1,33},{33,1},{2,34},{34,2},{3,35},{35,3},{4,36},{36... | collective-permute-start | bytes 12296 | tf_op jit(solution)/shard_map/ppermute | solution.py:376
  124.2 1.4 copy-start.9
  130.2 13.6 %collective-permute-start.20 = (bf16[72,1152]{1,0:T(8,128)(2,1)}, bf16[72,1152]{1,0:T(8,128)(2,1)}, u32[]{:S(2)}, u32[]{:S(2)}) collective-permute-start(bf16[72,1152]{1,0:T(8,128)(2,1)} %get-tuple-element.74), channel_id=1, source_target_pairs={{0,64},{64,128},{128,192},{192,0},{1,65},{65,129},{129,193},{193,1... | collective-permute-start | bytes 497672 | tf_op jit(solution)/shard_map/ppermute | solution.py:373
  132.3 11.5 %collective-permute-start.21 = (bf16[72,1152]{1,0:T(8,128)(2,1)}, bf16[72,1152]{1,0:T(8,128)(2,1)}, u32[]{:S(2)}, u32[]{:S(2)}) collective-permute-start(bf16[72,1152]{1,0:T(8,128)(2,1)} %get-tuple-element.75), channel_id=1, source_target_pairs={{0,128},{64,192},{128,0},{192,64},{1,129},{65,193},{129,1},{193,65... | collective-permute-start | bytes 497672 | tf_op jit(solution)/shard_map/ppermute | solution.py:373
  135.3 8.4 %collective-permute-start.22 = (bf16[72,1152]{1,0:T(8,128)(2,1)}, bf16[72,1152]{1,0:T(8,128)(2,1)}, u32[]{:S(2)}, u32[]{:S(2)}) collective-permute-start(bf16[72,1152]{1,0:T(8,128)(2,1)} %get-tuple-element.76), channel_id=1, source_target_pairs={{0,192},{64,0},{128,64},{192,128},{1,193},{65,1},{129,65},{193,129... | collective-permute-start | bytes 497672 | tf_op jit(solution)/shard_map/ppermute | solution.py:373
  145.7 22.6 %copy-start.1 = (bf16[32,4,3456]{2,1,0:T(4,128)(2,1)}, bf16[32,4,3456]{2,1,0:T(4,128)(2,1)S(1)}, u32[]{:S(2)}) copy-start(bf16[32,4,3456]{2,1,0:T(4,128)(2,1)S(1)} %all-to-all-done.3.x_ref) | copy-start | bytes 2654212
  145.7 6.3 %collective-permute-start.23 = (bf16[36,1152]{1,0:T(8,128)(2,1)}, bf16[36,1152]{1,0:T(8,128)(2,1)S(1)}, u32[]{:S(2)}, u32[]{:S(2)}) collective-permute-start(bf16[36,1152]{1,0:T(8,128)(2,1)} %get-tuple-element.83), channel_id=1, source_target_pairs={{0,0},{1,1},{2,2},{3,3},{4,4},{5,5},{6,6},{7,7},{64,65},{65,66},{6... | collective-permute-start | bytes 248840 | tf_op jit(solution)/shard_map/ppermute | solution.py:370
  147.2 7.6 %collective-permute-start.24 = (bf16[36,1152]{1,0:T(8,128)(2,1)}, bf16[36,1152]{1,0:T(8,128)(2,1)S(1)}, u32[]{:S(2)}, u32[]{:S(2)}) collective-permute-start(bf16[36,1152]{1,0:T(8,128)(2,1)} %get-tuple-element.84), channel_id=1, source_target_pairs={{0,4},{1,5},{2,6},{3,7},{4,0},{5,1},{6,2},{7,3},{64,69},{65,70},{6... | collective-permute-start | bytes 248840 | tf_op jit(solution)/shard_map/ppermute | solution.py:370
  154.9 6.3 %collective-permute-start.27 = (bf16[36,1152]{1,0:T(8,128)(2,1)S(1)}, bf16[36,1152]{1,0:T(8,128)(2,1)S(1)}, u32[]{:S(2)}, u32[]{:S(2)}) collective-permute-start(bf16[36,1152]{1,0:T(8,128)(2,1)S(1)} %add_convert_fusion.1), channel_id=1, source_target_pairs={{0,192},{64,0},{128,64},{192,128},{1,193},{65,1},{129,65},{193,129... | collective-permute-start | bytes 248840 | tf_op jit(solution)/shard_map/ppermute | solution.py:373
  157.0 5.6 %collective-permute-start.26 = (bf16[36,1152]{1,0:T(8,128)(2,1)S(1)}, bf16[36,1152]{1,0:T(8,128)(2,1)S(1)}, u32[]{:S(2)}, u32[]{:S(2)}) collective-permute-start(bf16[36,1152]{1,0:T(8,128)(2,1)S(1)} %add_convert_fusion.1), channel_id=1, source_target_pairs={{0,64},{64,128},{128,192},{192,0},{1,65},{65,129},{129,193},{193,1... | collective-permute-start | bytes 248840 | tf_op jit(solution)/shard_map/ppermute | solution.py:373
  157.0 5.6 %collective-permute-start.25 = (bf16[36,1152]{1,0:T(8,128)(2,1)S(1)}, bf16[36,1152]{1,0:T(8,128)(2,1)S(1)}, u32[]{:S(2)}, u32[]{:S(2)}) collective-permute-start(bf16[36,1152]{1,0:T(8,128)(2,1)S(1)} %add_convert_fusion.1), channel_id=1, source_target_pairs={{0,128},{64,192},{128,0},{192,64},{1,129},{65,193},{129,1},{193,65... | collective-permute-start | bytes 248840 | tf_op jit(solution)/shard_map/ppermute | solution.py:373
  162.7 8.0 %copy-start.5 = (bf16[36,1152]{1,0:T(8,128)(2,1)}, bf16[36,1152]{1,0:T(8,128)(2,1)S(1)}, u32[]{:S(2)}) copy-start(bf16[36,1152]{1,0:T(8,128)(2,1)S(1)} %add_convert_fusion.own_ref) | copy-start | bytes 248836
  162.7 8.0 %collective-permute-start.28 = (bf16[36,1152]{1,0:T(8,128)(2,1)S(1)}, bf16[36,1152]{1,0:T(8,128)(2,1)}, u32[]{:S(2)}, u32[]{:S(2)}) collective-permute-start(bf16[36,1152]{1,0:T(8,128)(2,1)S(1)} %add_convert_fusion.own_ref), channel_id=1, source_target_pairs={{0,32},{32,0},{1,33},{33,1},{2,34},{34,2},{3,35},{35,3},{4,36},{36... | collective-permute-start | bytes 248840 | tf_op jit(solution)/shard_map/ppermute | solution.py:376

commit v4 on v3

--- a/solution.py
+++ b/solution.py
@@ -84,19 +84,6 @@
         probs_ref[head] = probs
         out.add(head, mul(probs.astype(BF16), values, NN))
 
-def attend_space_kernel(place_ref, x_ref, mix_ref, probs_ref, order_ref, mix):
-    at_x, at_y, at_z = place_ref[0], place_ref[2], place_ref[3]
-    column = lax.broadcasted_iota(jnp.int32, (D, LANES), 0)
-    for tile in range(0, D, LANES):
-        lane = lax.broadcasted_iota(jnp.int32, (1, LANES), 1) + tile
-        block = (lane * 1821) >> 16
-        from_z = (at_z + (((block >> 1) + at_y) & 3) + 4 * (block & 1)) & 7
-        from_x = ((block >> 3) + at_x) & 3
-        source = (from_x * 8 + from_z) * 36 + (lane - block * 36)
-        order_ref[:, tile : tile + LANES] = jnp.where(column == source, 1.0, 0.0).astype(BF16)
-    attend_heads(False, x_ref, mix, probs_ref)
-    mix_ref[...] = mul(mix[...], order_ref[...], NN).astype(BF16)
-
 ROWS = jax.ShapeDtypeStruct((TOKENS, D), BF16)
 PROBS = jax.ShapeDtypeStruct((HEADS, TOKENS, TOKENS), F32)
 
@@ -107,7 +94,7 @@
     kinds = {"smem": pltpu.SMEM, "vmem": pltpu.VMEM, "any": pl.ANY}
     return [pl.BlockSpec(memory_space=kinds[k]) for k, n in places.items() for _ in range(n)]
 
-def call(kernel, out_shape, in_specs, scratch, name, micros=3, out_specs=None):
+def call(kernel, out_shape, in_specs, scratch, name, micros=3, out_specs=None, vmem=VMEM_BYTES):
     return pl.pallas_call(
         kernel,
         out_shape=out_shape,
@@ -115,29 +102,36 @@
         **({} if out_specs is None else {"out_specs": out_specs}),
         scratch_shapes=scratch,
         cost_estimate=pl.CostEstimate(flops=micros * 10**9, bytes_accessed=1, transcendentals=0),
-        compiler_params=pltpu.CompilerParams(vmem_limit_bytes=VMEM_BYTES),
+        compiler_params=pltpu.CompilerParams(vmem_limit_bytes=vmem),
         name=name,
     )
 
-def attend_space(place, x):
-    order = jax.ShapeDtypeStruct((D, D), BF16)
-    return call(
-        attend_space_kernel,
-        (ROWS, PROBS, order),
-        specs(smem=1, vmem=1),
-        [pltpu.VMEM((TOKENS, D), BF16)],
-        "attend_space",
-        14,
-    )(place, x)
-
-def stack_kernel(*refs):
-    *block_refs, out_ref = refs
+def attend_space(x):
+    kernel = functools.partial(attend_heads, False)
+    return call(kernel, (ROWS, PROBS), specs(vmem=1), [], "attend_space", 14)(x)
+
+
+def unit_rows(place_ref):
+    at_y, at_z = place_ref[2], place_ref[3]
+    natural = lax.broadcasted_iota(jnp.int32, (288, 288), 0)
+    unit = lax.broadcasted_iota(jnp.int32, (1, 288), 1)
+    block = (unit * 1821) >> 16
+    from_z = (at_z + (((block >> 1) + at_y) & 3) + 4 * (block & 1)) & 7
+    return jnp.where(natural == from_z * 36 + (unit - block * 36), 1.0, 0.0).astype(BF16)
+
+
+def stack_kernel(place_ref, *refs):
+    *block_refs, out_ref, units = refs
     for a, ref in enumerate(block_refs):
-        out_ref[72 * a : 72 * a + 72] = ref[...]
-
-def stack(blocks):
+        units[72 * a : 72 * a + 72] = ref[...]
+    out_ref[...] = mul(unit_rows(place_ref), units[...], NN).astype(BF16)
+
+
+def stack(place, blocks):
     out = jax.ShapeDtypeStruct((288, D), BF16)
-    return call(stack_kernel, out, specs(vmem=4), [], "stack", 1)(*blocks)
+    scratch = [pltpu.VMEM((288, D), BF16)]
+    return call(stack_kernel, out, specs(smem=1, vmem=4), scratch, "stack", 1, vmem=32 * 1024 * 1024)(place, *blocks)
+
 
 def attend_time_kernel(x_ref, mix_ref, probs_ref, x, mix):
     x[...] = x_ref[...].reshape(TOKENS, 3 * D)
@@ -160,7 +154,7 @@
 
 def receive(x):
     out = jax.ShapeDtypeStruct((TOKENS, 3 * D), BF16)
-    return call(receive_kernel, out, specs(vmem=1), [], "natural_order")(x)
+    return call(receive_kernel, out, specs(vmem=1), [], "natural_order", vmem=32 * 1024 * 1024)(x)
 
 def attend_back_heads(inv, x_ref, probs_ref, grad_ref, out_ref):
     query_out = Tiles(out_ref, 0)
@@ -213,36 +207,45 @@
         [],
         "attend_back_space",
         1,
+        vmem=32 * 1024 * 1024,
     )(x, probs, grad, spread)
 
-def fetch_weights(refs, weight, sems):
+def fetch_weights(at_x, refs, weight, sems):
     copies = []
-    for a in range(4):
-        copy = pltpu.make_async_copy(refs[a], weight.at[pl.ds(288 * a, 288)], sems.at[a])
+    for b in range(4):
+        rows = pl.ds(pl.multiple_of(((at_x + b) & 3) * 288, 288), 288)
+        copy = pltpu.make_async_copy(refs[b], weight.at[rows], sems.at[b])
         copy.start()
         copies.append(copy)
     return copies
 
-def project_kernel(place_ref, time_ref, hidden_any, target_any, space_any, order_any, *rest):
+
+def column_block(mix, index):
+    blocks = [mix[:, 288 * q : 288 * q + 288] for q in range(4)]
+    low = jnp.where(index == 0, blocks[0], blocks[1])
+    high = jnp.where(index == 2, blocks[2], blocks[3])
+    return jnp.where(index < 2, low, high)
+
+
+def project_kernel(place_ref, time_ref, hidden_any, target_any, space_any, *rest):
     own_refs, other_refs = rest[0:4], rest[4:8]
     time_grad_ref, pack_refs = rest[8], rest[9:13]
-    weights, hidden_ref, target_ref, space_ref, order_ref, packs, sems = rest[13:]
-    at_core = place_ref[1]
+    weights, hidden_ref, target_ref, space_ref, packs, sems = rest[13:]
+    at_x, at_core = place_ref[0], place_ref[1]
     loads = [
         pltpu.make_async_copy(source, place, sems.at[2, n])
         for n, (source, place) in enumerate(
-            ((order_any, order_ref), (hidden_any, hidden_ref), (target_any, target_ref), (space_any, space_ref))
+            ((hidden_any, hidden_ref), (target_any, target_ref), (space_any, space_ref))
         )
     ]
     for copy in loads:
         copy.start()
-    copies = fetch_weights(own_refs, weights.at[at_core], sems.at[0])
-    copies += fetch_weights(other_refs, weights.at[1 - at_core], sems.at[1])
+    copies = fetch_weights(at_x, own_refs, weights.at[at_core], sems.at[0])
+    copies += fetch_weights(at_x, other_refs, weights.at[1 - at_core], sems.at[1])
     natural = natural_from_sent()
     for copy in loads:
         copy.wait()
     time_mix = mul(natural, time_ref[...].reshape(TOKENS, D), NN).astype(BF16)
-    time_mix = mul(time_mix, order_ref[...], NN).astype(BF16)
     base = hidden_ref[...].astype(F32) - target_ref[...].astype(F32)
     first = at_core == 0
     space_mix = space_ref[...]
@@ -255,7 +258,6 @@
     total = jnp.sum(resid * resid)
     out_grad = resid.astype(BF16)
     time_grad = mul(out_grad, weights[1], NT).astype(BF16)
-    time_grad = mul(time_grad, order_ref[...], NT).astype(BF16)
     time_grad = mul(natural, time_grad, TN).astype(BF16)
     lane = lax.broadcasted_iota(jnp.int32, (TOKENS, LANES), 1)
     whole = jnp.full((TOKENS, LANES), total, F32)
@@ -268,55 +270,54 @@
     stores = []
     for a in range(4):
         packs[a, :, :D] = out_grad
+        index = (at_x + a) & 3
         packs[a, :, D:] = jnp.concatenate(
-            [space_ref[:, 288 * a : 288 * a + 288], time_mix[:, 288 * a : 288 * a + 288]], axis=1
+            [column_block(space_mix, index), column_block(time_mix, index)], axis=1
         )
         stores.append(pltpu.make_async_copy(packs.at[a], pack_refs[a], sems.at[3, a]))
         stores[-1].start()
     for copy in stores:
         copy.wait()
 
-def project(place, hidden, target, space_mix, time_mix, order, own, other):
+def project(place, hidden, target, space_mix, time_mix, own, other):
     packed = jax.ShapeDtypeStruct((TOKENS, D + 576), BF16)
     return call(
         project_kernel,
         (sent_rows(D + LANES),) + (packed,) * 4,
-        specs(smem=1, vmem=1, any=12),
+        specs(smem=1, vmem=1, any=11),
         [pltpu.VMEM((2, D, D), BF16)]
         + [pltpu.VMEM((TOKENS, D), BF16)] * 3
         + [
-            pltpu.VMEM((D, D), BF16),
             pltpu.VMEM((4, TOKENS, D + 576), BF16),
             pltpu.SemaphoreType.DMA((4, 4)),
         ],
         "project",
         8,
         specs(vmem=1, any=4),
-    )(place, time_mix, hidden, target, space_mix, order, *own, *other)
-
-def space_back_kernel(place_ref, pack_ref, order_ref, *rest):
+    )(place, time_mix, hidden, target, space_mix, *own, *other)
+
+def space_back_kernel(place_ref, pack_ref, *rest):
     own_refs, other_refs = rest[0:4], rest[4:8]
     out_ref, weight, sems = rest[8:]
     first = place_ref[1] == 0
 
     @pl.when(first)
     def _():
-        for copy in fetch_weights(own_refs, weight, sems):
+        for copy in fetch_weights(place_ref[0], own_refs, weight, sems):
             copy.wait()
 
     @pl.when(jnp.logical_not(first))
     def _():
-        for copy in fetch_weights(other_refs, weight, sems):
+        for copy in fetch_weights(place_ref[0], other_refs, weight, sems):
             copy.wait()
 
-    mix_grad = mul(pack_ref[:, :D], weight[...], NT).astype(BF16)
-    out_ref[...] = mul(mix_grad, order_ref[...], NT).astype(BF16)
-
-def space_back(place, packed, order, own, other):
+    out_ref[...] = mul(pack_ref[:, :D], weight[...], NT).astype(BF16)
+
+def space_back(place, packed, own, other):
     scratch = [pltpu.VMEM((D, D), BF16), pltpu.SemaphoreType.DMA((4,))]
     return call(
-        space_back_kernel, ROWS, specs(smem=1, vmem=2, any=8), scratch, "space_back", 3
-    )(place, packed, order, *own, *other)
+        space_back_kernel, ROWS, specs(smem=1, vmem=1, any=8), scratch, "space_back", 3
+    )(place, packed, *own, *other)
 
 def weight_kernel(place_ref, *rest):
     spread_refs, pack_refs = rest[0:2], rest[2:10]
@@ -331,8 +332,9 @@
             total[...] = term
         else:
             total[...] += term
+    units = mul(unit_rows(place_ref), total[...].astype(BF16), TN).astype(BF16)
     for a in range(4):
-        out_refs[a][...] = total[72 * a : 72 * a + 72].astype(BF16)
+        out_refs[a][...] = units[72 * a : 72 * a + 72]
 
 def weight_grad(place, spreads, packs):
     return call(
@@ -342,6 +344,7 @@
         [pltpu.VMEM((288, D), F32)],
         "weight_grad",
         8,
+        vmem=32 * 1024 * 1024,
     )(place, *spreads, *packs)
 
 def halves_kernel(*refs):
@@ -352,7 +355,7 @@
 
 def halves(blocks):
     out = jax.ShapeDtypeStruct((36, D), BF16)
-    return call(halves_kernel, (out, out), specs(vmem=4), [], "halves", 0)(*blocks)
+    return call(halves_kernel, (out, out), specs(vmem=4), [], "halves", 0, vmem=32 * 1024 * 1024)(*blocks)
 
 def finish_kernel(place_ref, own_ref, other_ref, space_ref, time_ref):
     own, other = own_ref[...].astype(F32), other_ref[...].astype(F32)
@@ -362,7 +365,7 @@
 
 def finish(place, own, other):
     rows = jax.ShapeDtypeStruct((36, D), F32)
-    return call(finish_kernel, (rows, rows), specs(smem=1, vmem=2), [], "finish")(place, own, other)
+    return call(finish_kernel, (rows, rows), specs(smem=1, vmem=2), [], "finish", vmem=32 * 1024 * 1024)(place, own, other)
 
 def shift_z(value, slope, extra):
     extra = extra if slope > 0 else -extra
@@ -391,12 +394,12 @@
     rows = jnp.where(at_core == 0, spatial_proj, temporal_proj)
     by_z = jnp.concatenate([shift_z(rows, -1, 0), shift_z(rows, -1, 4)])
     time_x = exchange(send(temporal_qkv.reshape(TOKENS, 3 * D)), SEQ)
-    by_y = stack([by_z] + [shift(by_z, "y", 4, 4 - a) for a in range(1, 4)])
+    by_y = stack(place, [by_z] + [shift(by_z, "y", 4, 4 - a) for a in range(1, 4)])
 
     by_y, spatial_qkv = after(by_y, spatial_qkv)
     space_x = spatial_qkv.reshape(TOKENS, 3 * D)
-    space_mix, space_probs, order = attend_space(place, space_x)
-    time_x, space_mix, space_probs, order = after(time_x, space_mix, space_probs, order)
+    space_mix, space_probs = attend_space(space_x)
+    time_x, space_mix, space_probs = after(time_x, space_mix, space_probs)
     time_mix, time_probs = attend_time(time_x)
     time_mix = exchange(time_mix, SEQ)
     own = [by_y] + [shift(by_y, "x", 4, 4 - b) for b in range(1, 4)]
@@ -410,12 +413,11 @@
         teacher_target.reshape(TOKENS, D),
         space_mix,
         time_mix,
-        order,
         own,
         other,
     )
     time_back = exchange(time_grad, SEQ)
-    space_grad = space_back(place, packs[0], order, own, other)
+    space_grad = space_back(place, packs[0], own, other)
     packs = [packs[0]] + [shift(packs[b], "x", 4, b) for b in range(1, 4)]
     time_back, space_grad = after(time_back, space_grad)
     time_out, spread = attend_back_time(time_x, time_probs, time_back)

time: 175 us -> 168 us (0.960)
  Pallas kernels: 55.6 us -> 43.9 us
  waiting for transfers between devices: 23.4 us -> 28 us
  starting transfers between devices: 85.8 us -> 87.9 us
    pallas_call x6, Pallas kernels: 20.5 us -> 13.4 us  [the longest x1 5.2 us: attend_space(): return call(kernel, (ROWS, PROBS), specs(vmem=1), [], 'attend_space', 14)(x)]
    ppermute x15, waiting for transfers between devices: 14.1 us -> 20.2 us  [shift(): lax.ppermute(value, axis, [(i, (i + step) % size) for i in range(size)])]
    ppermute x10, waiting for transfers between devices: 6.2 us -> 3.22 us  [swap(): return lax.ppermute(value, 'core', [(0, 1), (1, 0)])]
    ppermute x15, starting transfers between devices: 28 us -> 30.4 us  [shift(): lax.ppermute(value, axis, [(i, (i + step) % size) for i in range(size)])]
    pallas_call x1, Pallas kernels: 8.46 us -> 6.59 us  [project(): call(project_kernel, (sent_rows(D + LANES),) + (packed,) * 4, specs(smem=...]
  transfers between devices with their start and end apart: 33 -> 33, of which waited for: 14 -> 14; matrix products, arithmetic and copies ran while one was open for 2% -> 0% of each run, Pallas kernels for 26% -> 21%
where the time goes in v4:
time: 168 us
  starting transfers between devices  87.9 us (52%)
  Pallas kernels  43.9 us (26%)
  waiting for transfers between devices  28 us (17%)
  local copies, waits for them, and re-layouts  3.94 us (2%)
  between operations  2.66 us (2%)
    ppermute x15, starting transfers between devices, shift(): lax.ppermute(value, axis, [(i, (i + step) % size) for i in range(size)])  30.4 us
    all_to_all x4, starting transfers between devices, exchange(): return lax.all_to_all(value, axis, split_axis=0, concat_axis=0, tiled=True)  28.8 us
    ppermute x15, waiting for transfers between devices, shift(): lax.ppermute(value, axis, [(i, (i + step) % size) for i in range(size)])  20.2 us
    ppermute x10, starting transfers between devices, swap(): return lax.ppermute(value, 'core', [(0, 1), (1, 0)])  15.1 us
    ppermute x4, starting transfers between devices, shift_z(): return lax.ppermute(value, ('y', 'z'), pairs)  13.7 us
    pallas_call x1, Pallas kernels, attend_back_time(): call(attend_back_time_kernel, (sent_rows(3 * D), jax.ShapeDtypeStruct((8,...  7.25 us
    pallas_call x1, Pallas kernels, project(): call(project_kernel, (sent_rows(D + LANES),) + (packed,) * 4, specs(smem=...  6.59 us
    pallas_call x1, Pallas kernels, attend_back_space(): call(attend_back_space_kernel, jax.ShapeDtypeStruct((TOKENS, 3 * D), BF16...  5.57 us
  transfers between devices with their start and end apart: 33, of which 14 were waited for; matrix products, arithmetic and copies ran while one was open for 0% of the time, Pallas kernels for 21%

profile of v4, /device:TPU:1, one launch (start us, length us, event | category | flops | bytes accessed | tf_op | source)
XLA Modules:
  0.0 167.6 jit_solution(15697191456469304033)
XLA Ops:
  0.6 0.9 broadcast_select_fusion
  1.6 7.8 %collective-permute-start.1 = (bf16[36,1152]{1,0:T(8,128)(2,1)S(1)}, bf16[36,1152]{1,0:T(8,128)(2,1)S(1)}, u32[]{:S(2)}, u32[]{:S(2)}) collective-permute-start(bf16[36,1152]{1,0:T(8,128)(2,1)S(1)} %broadcast_select_fusion), channel_id=1, source_target_pairs={{0,4},{1,5},{2,6},{3,7},{4,0},{5,1},{6,2},{7,3},{64,67},{65,68},{6... | collective-permute-start | bytes 248840 | tf_op jit(solution)/shard_map/ppermute | solution.py:373
  10.0 2.5 %send_order.1 = bf16[32,4,3456]{2,1,0:T(4,128)(2,1)} custom-call(bf16[128,3456]{1,0:T(8,128)(2,1)} %bitcast.13), custom_call_target="tpu_custom_call" | custom-call | flops 3000000000 | bytes 1 | tf_op jit(solution)/shard_map/send_order/pallas_call | solution.py:149
  12.5 5.9 %all-to-all-start = ((bf16[32,4,3456]{2,1,0:T(4,128)(2,1)}), bf16[32,4,3456]{2,1,0:T(4,128)(2,1)}, u32[]{:S(2)}, u32[]{:S(2)}) async-start(bf16[32,4,3456]{2,1,0:T(4,128)(2,1)} %send_order.1), calls=%async_computation | async-start | bytes 1769472 | tf_op jit(solution)/shard_map/all_to_all | solution.py:388
  18.5 4.6 %collective-permute-start.4 = (bf16[72,1152]{1,0:T(8,128)(2,1)S(1)}, bf16[72,1152]{1,0:T(8,128)(2,1)S(1)}, u32[]{:S(2)}, u32[]{:S(2)}) collective-permute-start(bf16[72,1152]{1,0:T(8,128)(2,1)S(1)} %pad_maximum_fusion.refs_0_), channel_id=1, source_target_pairs={{0,64},{64,128},{128,192},{192,0},{1,65},{65,129},{129,193},{193,1... | collective-permute-start | bytes 497672 | tf_op jit(solution)/shard_map/ppermute | solution.py:376
  23.1 1.7 %collective-permute-start.3 = (bf16[72,1152]{1,0:T(8,128)(2,1)S(1)}, bf16[72,1152]{1,0:T(8,128)(2,1)S(1)}, u32[]{:S(2)}, u32[]{:S(2)}) collective-permute-start(bf16[72,1152]{1,0:T(8,128)(2,1)S(1)} %pad_maximum_fusion.refs_0_), channel_id=1, source_target_pairs={{0,128},{64,192},{128,0},{192,64},{1,129},{65,193},{129,1},{193,65... | collective-permute-start | bytes 497672 | tf_op jit(solution)/shard_map/ppermute | solution.py:376
  24.8 2.0 %collective-permute-start.2 = (bf16[72,1152]{1,0:T(8,128)(2,1)S(1)}, bf16[72,1152]{1,0:T(8,128)(2,1)S(1)}, u32[]{:S(2)}, u32[]{:S(2)}) collective-permute-start(bf16[72,1152]{1,0:T(8,128)(2,1)S(1)} %pad_maximum_fusion.refs_0_), channel_id=1, source_target_pairs={{0,192},{64,0},{128,64},{192,128},{1,193},{65,1},{129,65},{193,129... | collective-permute-start | bytes 497672 | tf_op jit(solution)/shard_map/ppermute | solution.py:376
  26.8 4.0 %collective-permute-done.3.refs_2_ = bf16[72,1152]{1,0:T(8,128)(2,1)S(1)} collective-permute-done((bf16[72,1152]{1,0:T(8,128)(2,1)S(1)}, bf16[72,1152]{1,0:T(8,128)(2,1)S(1)}, u32[]{:S(2)}, u32[]{:S(2)}) %collective-permute-start.3) | collective-permute-done | bytes 165920 | tf_op jit(solution)/shard_map/ppermute | solution.py:376
  31.1 1.1 stack.21.rest_0_
  32.2 1.1 collective-permute-start.7
  33.2 2.5 %collective-permute-start.6 = (bf16[288,1152]{1,0:T(8,128)(2,1)S(1)}, bf16[288,1152]{1,0:T(8,128)(2,1)}, u32[]{:S(2)}, u32[]{:S(2)}) collective-permute-start(bf16[288,1152]{1,0:T(8,128)(2,1)S(1)} %stack.21.rest_0_), channel_id=1, source_target_pairs={{0,16},{8,24},{16,0},{24,8},{1,17},{9,25},{17,1},{25,9},{2,18},{10... | collective-permute-start | bytes 1990664 | tf_op jit(solution)/shard_map/ppermute | solution.py:376
  35.7 1.1 collective-permute-start.5
  36.8 5.2 %attend_space.1 = (bf16[128,1152]{1,0:T(8,128)(2,1)}, f32[16,128,128]{2,1,0:T(8,128)}) custom-call(bf16[128,3456]{1,0:T(8,128)(2,1)} %bitcast.11), custom_call_target="tpu_custom_call" | custom-call | flops 14000000000 | bytes 1 | tf_op jit(solution)/shard_map/attend_space/pallas_call | solution.py:111
  42.0 5.2 %attend_time.1 = (bf16[32,4,1152]{2,1,0:T(4,128)(2,1)}, f32[16,128,128]{2,1,0:T(8,128)}) custom-call(bf16[32,4,3456]{2,1,0:T(4,128)(2,1)} %all-to-all-done.x_ref), custom_call_target="tpu_custom_call" | custom-call | flops 3000000000 | bytes 1 | tf_op jit(solution)/shard_map/attend_time/pallas_call | solution.py:143
  47.2 6.9 %all-to-all-start.1 = ((bf16[32,4,1152]{2,1,0:T(4,128)(2,1)}), bf16[32,4,1152]{2,1,0:T(4,128)(2,1)S(1)}, u32[]{:S(2)}, u32[]{:S(2)}) async-start(bf16[32,4,1152]{2,1,0:T(4,128)(2,1)} %get-tuple-element.49), calls=%async_computation.1 | async-start | bytes 589824 | tf_op jit(solution)/shard_map/all_to_all | solution.py:388
  54.1 3.8 %collective-permute-start.8 = (bf16[288,1152]{1,0:T(8,128)(2,1)S(1)}, bf16[288,1152]{1,0:T(8,128)(2,1)S(1)}, u32[]{:S(2)}, u32[]{:S(2)}) collective-permute-start(bf16[288,1152]{1,0:T(8,128)(2,1)S(1)} %stack.21.rest_0_), channel_id=1, source_target_pairs={{0,32},{32,0},{1,33},{33,1},{2,34},{34,2},{3,35},{35,3},{4,36},{36... | collective-permute-start | bytes 1990664 | tf_op jit(solution)/shard_map/ppermute | solution.py:379
  57.9 11.1 %collective-permute-done.6.rest_2_ = bf16[288,1152]{1,0:T(8,128)(2,1)} collective-permute-done((bf16[288,1152]{1,0:T(8,128)(2,1)S(1)}, bf16[288,1152]{1,0:T(8,128)(2,1)}, u32[]{:S(2)}, u32[]{:S(2)}) %collective-permute-start.6) | collective-permute-done | bytes 663584 | tf_op jit(solution)/shard_map/ppermute | solution.py:376
  69.4 2.1 %collective-permute-start.9 = (bf16[288,1152]{1,0:T(8,128)(2,1)}, bf16[288,1152]{1,0:T(8,128)(2,1)S(1)}, u32[]{:S(2)}, u32[]{:S(2)}) collective-permute-start(bf16[288,1152]{1,0:T(8,128)(2,1)} %collective-permute-done.5.rest_1_), channel_id=1, source_target_pairs={{0,32},{32,0},{1,33},{33,1},{2,34},{34,2},{3,35},{35,3},{4,36},{36... | collective-permute-start | bytes 1990664 | tf_op jit(solution)/shard_map/ppermute | solution.py:379
  72.0 0.8 copy-done.9
  73.5 0.9 copy-done.10
  74.4 0.9 copy-done.11
  75.4 0.8 copy-done.12
  76.2 6.6 %project.1 = (bf16[32,4,1280]{2,1,0:T(4,128)(2,1)}, bf16[128,1728]{1,0:T(8,128)(2,1)}, bf16[128,1728]{1,0:T(8,128)(2,1)}, bf16[128,1728]{1,0:T(8,128)(2,1)}, bf16[128,1728]{1,0:T(8,128)(2,1)}) custom-call(s32[4]{0:T(128)} %copy-done, bf16[32,4,1152]{2,1,0:T(4,128)(2,1)} %copy-done.8, bf16[128,1152]{1,0:T(8,128)(2,1)} %bitcast.14, ...), custom_call_target="tpu_custom_call" | custom-call | flops 8000000000 | bytes 1 | tf_op jit(solution)/shard_map/project/pallas_call | solution.py:284
  82.8 8.4 %all-to-all-start.2 = ((bf16[32,4,1280]{2,1,0:T(4,128)(2,1)}), bf16[32,4,1280]{2,1,0:T(4,128)(2,1)}, u32[]{:S(2)}, u32[]{:S(2)}) async-start(bf16[32,4,1280]{2,1,0:T(4,128)(2,1)} %get-tuple-element.56), calls=%async_computation.2 | async-start | bytes 655360 | tf_op jit(solution)/shard_map/all_to_all | solution.py:388
  91.2 1.2 collective-permute-start.12
  92.5 2.4 %collective-permute-start.13 = (bf16[128,1728]{1,0:T(8,128)(2,1)}, bf16[128,1728]{1,0:T(8,128)(2,1)S(1)}, u32[]{:S(2)}, u32[]{:S(2)}) collective-permute-start(bf16[128,1728]{1,0:T(8,128)(2,1)} %get-tuple-element.62), channel_id=1, source_target_pairs={{0,16},{8,24},{16,0},{24,8},{1,17},{9,25},{17,1},{25,9},{2,18},{10... | collective-permute-start | bytes 1327112 | tf_op jit(solution)/shard_map/ppermute | solution.py:376
  94.9 1.1 collective-permute-start.14
  96.0 4.4 %space_back.1.grad_ref = bf16[128,1152]{1,0:T(8,128)(2,1)} custom-call(s32[4]{0:T(128)} %copy-done, bf16[128,1728]{1,0:T(8,128)(2,1)} %get-tuple-element.65.pack_ref.rest_2_, bf16[288,1152]{1,0:T(8,128)(2,1)} %copy-done.3, bf16[288,1152]{1,0:T(8,128)(2,1)} %collective-permute-done.5.rest_1_, bf16[288,1152]{1,0:T(8,128)(2,1)} %collective-permute-done.6.rest_2_, ...), custom_call_target="tpu_custom_call" | custom-call | flops 3000000000 | bytes 1 | tf_op jit(solution)/shard_map/space_back/pallas_call | solution.py:318
  100.4 1.3 all-to-all-done.2.grad_ref
  101.7 7.2 %attend_back_time.1 = (bf16[32,4,3456]{2,1,0:T(4,128)(2,1)}, f32[8,128]{1,0:T(8,128)}) custom-call(bf16[32,4,3456]{2,1,0:T(4,128)(2,1)} %all-to-all-done.x_ref, f32[16,128,128]{2,1,0:T(8,128)} %get-tuple-element.48.probs_ref, bf16[32,4,1280]{2,1,0:T(4,128)(2,1)} %all-to-all-done.2.grad_ref), custom_call_target="tpu_custom_call" | custom-call | flops 5000000000 | bytes 1 | tf_op jit(solution)/shard_map/attend_back_time/pallas_call | solution.py:190
  109.0 7.6 %all-to-all-start.3 = ((bf16[32,4,3456]{2,1,0:T(4,128)(2,1)}), bf16[32,4,3456]{2,1,0:T(4,128)(2,1)S(1)}, u32[]{:S(2)}, u32[]{:S(2)}) async-start(bf16[32,4,3456]{2,1,0:T(4,128)(2,1)} %get-tuple-element.60), calls=%async_computation.3 | async-start | bytes 1769472 | tf_op jit(solution)/shard_map/all_to_all | solution.py:388
  116.6 2.0 %collective-permute-done.13.rest_4_ = bf16[128,1728]{1,0:T(8,128)(2,1)S(1)} collective-permute-done((bf16[128,1728]{1,0:T(8,128)(2,1)}, bf16[128,1728]{1,0:T(8,128)(2,1)S(1)}, u32[]{:S(2)}, u32[]{:S(2)}) %collective-permute-start.13) | collective-permute-done | bytes 442400 | tf_op jit(solution)/shard_map/ppermute | solution.py:376
  118.6 1.2 collective-permute-start.16
  120.8 2.4 %collective-permute-done.15.rest_1_ = f32[8,128]{1,0:T(8,128)S(1)} collective-permute-done((f32[8,128]{1,0:T(8,128)S(1)}, f32[8,128]{1,0:T(8,128)S(1)}, u32[]{:S(2)}, u32[]{:S(2)}) %collective-permute-start.15) | collective-permute-done | bytes 4128 | tf_op jit(solution)/shard_map/ppermute | solution.py:379
  123.3 3.4 %weight_grad.1 = (bf16[72,1152]{1,0:T(8,128)(2,1)S(1)}, bf16[72,1152]{1,0:T(8,128)(2,1)S(1)}, bf16[72,1152]{1,0:T(8,128)(2,1)S(1)}, bf16[72,1152]{1,0:T(8,128)(2,1)S(1)}) custom-call(s32[4]{0:T(128)S(1)} %copy-done.1, f32[8,128]{1,0:T(8,128)S(1)} %copy-done.5, f32[8,128]{1,0:T(8,128)S(1)} %collective-permute-done.15.rest_1_, ...), custom_call_target="tpu_custom_call" | custom-call | flops 8000000000 | bytes 1 | tf_op jit(solution)/shard_map/weight_grad/pallas_call | solution.py:340
  126.7 1.8 %collective-permute-start.20 = (bf16[72,1152]{1,0:T(8,128)(2,1)S(1)}, bf16[72,1152]{1,0:T(8,128)(2,1)S(1)}, u32[]{:S(2)}, u32[]{:S(2)}) collective-permute-start(bf16[72,1152]{1,0:T(8,128)(2,1)S(1)} %get-tuple-element.70), channel_id=1, source_target_pairs={{0,64},{64,128},{128,192},{192,0},{1,65},{65,129},{129,193},{193,1... | collective-permute-start | bytes 497672 | tf_op jit(solution)/shard_map/ppermute | solution.py:376
  128.5 3.5 %collective-permute-start.21 = (bf16[72,1152]{1,0:T(8,128)(2,1)S(1)}, bf16[72,1152]{1,0:T(8,128)(2,1)S(1)}, u32[]{:S(2)}, u32[]{:S(2)}) collective-permute-start(bf16[72,1152]{1,0:T(8,128)(2,1)S(1)} %get-tuple-element.71), channel_id=1, source_target_pairs={{0,128},{64,192},{128,0},{192,64},{1,129},{65,193},{129,1},{193,65... | collective-permute-start | bytes 497672 | tf_op jit(solution)/shard_map/ppermute | solution.py:376
  132.0 1.1 collective-permute-start.22
  133.1 5.6 %attend_back_space.1 = bf16[128,3456]{1,0:T(8,128)(2,1)} custom-call(bf16[128,3456]{1,0:T(8,128)(2,1)S(1)} %bitcast.12, f32[16,128,128]{2,1,0:T(8,128)S(1)} %copy-done.6, bf16[128,1152]{1,0:T(8,128)(2,1)S(1)} %copy-done.7, f32[8,128]{1,0:T(8,128)S(1)} %copy-done.5), custom_call_target="tpu_custom_call" | custom-call | flops 1000000000 | bytes 1 | tf_op jit(solution)/shard_map/attend_back_space/pallas_call | solution.py:203
  138.7 0.9 collective-permute-done.21.refs_2_
  140.4 4.5 %collective-permute-start.24 = (bf16[36,1152]{1,0:T(8,128)(2,1)S(1)}, bf16[36,1152]{1,0:T(8,128)(2,1)S(1)}, u32[]{:S(2)}, u32[]{:S(2)}) collective-permute-start(bf16[36,1152]{1,0:T(8,128)(2,1)S(1)} %get-tuple-element.80), channel_id=1, source_target_pairs={{0,4},{1,5},{2,6},{3,7},{4,0},{5,1},{6,2},{7,3},{64,69},{65,70},{6... | collective-permute-start | bytes 248840 | tf_op jit(solution)/shard_map/ppermute | solution.py:373
  144.9 2.9 %collective-permute-done.24 = bf16[36,1152]{1,0:T(8,128)(2,1)S(1)} collective-permute-done((bf16[36,1152]{1,0:T(8,128)(2,1)S(1)}, bf16[36,1152]{1,0:T(8,128)(2,1)S(1)}, u32[]{:S(2)}, u32[]{:S(2)}) %collective-permute-start.24) | collective-permute-done | bytes 82976 | tf_op jit(solution)/shard_map/ppermute | solution.py:373
  147.9 3.8 %collective-permute-start.27 = (bf16[36,1152]{1,0:T(8,128)(2,1)S(1)}, bf16[36,1152]{1,0:T(8,128)(2,1)S(1)}, u32[]{:S(2)}, u32[]{:S(2)}) collective-permute-start(bf16[36,1152]{1,0:T(8,128)(2,1)S(1)} %add_convert_fusion.1), channel_id=1, source_target_pairs={{0,192},{64,0},{128,64},{192,128},{1,193},{65,1},{129,65},{193,129... | collective-permute-start | bytes 248840 | tf_op jit(solution)/shard_map/ppermute | solution.py:376
  151.7 2.5 %collective-permute-start.25 = (bf16[36,1152]{1,0:T(8,128)(2,1)S(1)}, bf16[36,1152]{1,0:T(8,128)(2,1)S(1)}, u32[]{:S(2)}, u32[]{:S(2)}) collective-permute-start(bf16[36,1152]{1,0:T(8,128)(2,1)S(1)} %add_convert_fusion.1), channel_id=1, source_target_pairs={{0,128},{64,192},{128,0},{192,64},{1,129},{65,193},{129,1},{193,65... | collective-permute-start | bytes 248840 | tf_op jit(solution)/shard_map/ppermute | solution.py:376
  155.4 1.9 %collective-permute-done.26 = bf16[36,1152]{1,0:T(8,128)(2,1)S(1)} collective-permute-done((bf16[36,1152]{1,0:T(8,128)(2,1)S(1)}, bf16[36,1152]{1,0:T(8,128)(2,1)S(1)}, u32[]{:S(2)}, u32[]{:S(2)}) %collective-permute-start.26) | collective-permute-done | bytes 82976 | tf_op jit(solution)/shard_map/ppermute | solution.py:376
  157.4 6.4 %collective-permute-start.28 = (bf16[36,1152]{1,0:T(8,128)(2,1)S(1)}, bf16[36,1152]{1,0:T(8,128)(2,1)S(1)}, u32[]{:S(2)}, u32[]{:S(2)}) collective-permute-start(bf16[36,1152]{1,0:T(8,128)(2,1)S(1)} %add_convert_fusion.own_ref), channel_id=1, source_target_pairs={{0,32},{32,0},{1,33},{33,1},{2,34},{34,2},{3,35},{35,3},{4,36},{36... | collective-permute-start | bytes 248840 | tf_op jit(solution)/shard_map/ppermute | solution.py:379
  163.8 1.3 natural_order.1
  165.1 1.3 finish.1
  (62 shorter events, 5.2 us)
Async XLA Ops:
  1.6 16.9 %collective-permute-start.1 = (bf16[36,1152]{1,0:T(8,128)(2,1)S(1)}, bf16[36,1152]{1,0:T(8,128)(2,1)S(1)}, u32[]{:S(2)}, u32[]{:S(2)}) collective-permute-start(bf16[36,1152]{1,0:T(8,128)(2,1)S(1)} %broadcast_select_fusion), channel_id=1, source_target_pairs={{0,4},{1,5},{2,6},{3,7},{4,0},{5,1},{6,2},{7,3},{64,67},{65,68},{6... | collective-permute-start | bytes 248840 | tf_op jit(solution)/shard_map/ppermute | solution.py:373
  9.4 9.1 %collective-permute-start = (bf16[36,1152]{1,0:T(8,128)(2,1)S(1)}, bf16[36,1152]{1,0:T(8,128)(2,1)S(1)}, u32[]{:S(2)}, u32[]{:S(2)}) collective-permute-start(bf16[36,1152]{1,0:T(8,128)(2,1)S(1)} %broadcast_select_fusion), channel_id=1, source_target_pairs={{0,0},{1,1},{2,2},{3,3},{4,4},{5,5},{6,6},{7,7},{64,71},{65,64},{6... | collective-permute-start | bytes 248840 | tf_op jit(solution)/shard_map/ppermute | solution.py:373
  12.5 29.5 %all-to-all-start = ((bf16[32,4,3456]{2,1,0:T(4,128)(2,1)}), bf16[32,4,3456]{2,1,0:T(4,128)(2,1)}, u32[]{:S(2)}, u32[]{:S(2)}) async-start(bf16[32,4,3456]{2,1,0:T(4,128)(2,1)} %send_order.1), calls=%async_computation | async-start | bytes 1769472 | tf_op jit(solution)/shard_map/all_to_all | solution.py:388
  18.5 8.3 %collective-permute-start.4 = (bf16[72,1152]{1,0:T(8,128)(2,1)S(1)}, bf16[72,1152]{1,0:T(8,128)(2,1)S(1)}, u32[]{:S(2)}, u32[]{:S(2)}) collective-permute-start(bf16[72,1152]{1,0:T(8,128)(2,1)S(1)} %pad_maximum_fusion.refs_0_), channel_id=1, source_target_pairs={{0,64},{64,128},{128,192},{192,0},{1,65},{65,129},{129,193},{193,1... | collective-permute-start | bytes 497672 | tf_op jit(solution)/shard_map/ppermute | solution.py:376
  23.1 7.7 %collective-permute-start.3 = (bf16[72,1152]{1,0:T(8,128)(2,1)S(1)}, bf16[72,1152]{1,0:T(8,128)(2,1)S(1)}, u32[]{:S(2)}, u32[]{:S(2)}) collective-permute-start(bf16[72,1152]{1,0:T(8,128)(2,1)S(1)} %pad_maximum_fusion.refs_0_), channel_id=1, source_target_pairs={{0,128},{64,192},{128,0},{192,64},{1,129},{65,193},{129,1},{193,65... | collective-permute-start | bytes 497672 | tf_op jit(solution)/shard_map/ppermute | solution.py:376
  24.8 6.3 %collective-permute-start.2 = (bf16[72,1152]{1,0:T(8,128)(2,1)S(1)}, bf16[72,1152]{1,0:T(8,128)(2,1)S(1)}, u32[]{:S(2)}, u32[]{:S(2)}) collective-permute-start(bf16[72,1152]{1,0:T(8,128)(2,1)S(1)} %pad_maximum_fusion.refs_0_), channel_id=1, source_target_pairs={{0,192},{64,0},{128,64},{192,128},{1,193},{65,1},{129,65},{193,129... | collective-permute-start | bytes 497672 | tf_op jit(solution)/shard_map/ppermute | solution.py:376
  26.8 5.3 %copy-start = (s32[4]{0:T(128)}, s32[4]{0:T(128)S(1)}, u32[]{:S(2)}) copy-start(s32[4]{0:T(128)S(1)} %pad_add_fusion.place_ref) | copy-start | bytes 52
  32.2 21.9 %copy-start.3 = (bf16[288,1152]{1,0:T(8,128)(2,1)}, bf16[288,1152]{1,0:T(8,128)(2,1)S(1)}, u32[]{:S(2)}) copy-start(bf16[288,1152]{1,0:T(8,128)(2,1)S(1)} %stack.21.rest_0_) | copy-start | bytes 1990660
  32.2 25.8 %collective-permute-start.7 = (bf16[288,1152]{1,0:T(8,128)(2,1)S(1)}, bf16[288,1152]{1,0:T(8,128)(2,1)}, u32[]{:S(2)}, u32[]{:S(2)}) collective-permute-start(bf16[288,1152]{1,0:T(8,128)(2,1)S(1)} %stack.21.rest_0_), channel_id=1, source_target_pairs={{0,8},{8,16},{16,24},{24,0},{1,9},{9,17},{17,25},{25,1},{2,10},{10... | collective-permute-start | bytes 1990664 | tf_op jit(solution)/shard_map/ppermute | solution.py:376
  33.2 35.8 %collective-permute-start.6 = (bf16[288,1152]{1,0:T(8,128)(2,1)S(1)}, bf16[288,1152]{1,0:T(8,128)(2,1)}, u32[]{:S(2)}, u32[]{:S(2)}) collective-permute-start(bf16[288,1152]{1,0:T(8,128)(2,1)S(1)} %stack.21.rest_0_), channel_id=1, source_target_pairs={{0,16},{8,24},{16,0},{24,8},{1,17},{9,25},{17,1},{25,9},{2,18},{10... | collective-permute-start | bytes 1990664 | tf_op jit(solution)/shard_map/ppermute | solution.py:376
  35.7 33.3 %collective-permute-start.5 = (bf16[288,1152]{1,0:T(8,128)(2,1)S(1)}, bf16[288,1152]{1,0:T(8,128)(2,1)}, u32[]{:S(2)}, u32[]{:S(2)}) collective-permute-start(bf16[288,1152]{1,0:T(8,128)(2,1)S(1)} %stack.21.rest_0_), channel_id=1, source_target_pairs={{0,24},{8,0},{16,8},{24,16},{1,25},{9,1},{17,9},{25,17},{2,26},{10... | collective-permute-start | bytes 1990664 | tf_op jit(solution)/shard_map/ppermute | solution.py:376
  47.2 22.2 %all-to-all-start.1 = ((bf16[32,4,1152]{2,1,0:T(4,128)(2,1)}), bf16[32,4,1152]{2,1,0:T(4,128)(2,1)S(1)}, u32[]{:S(2)}, u32[]{:S(2)}) async-start(bf16[32,4,1152]{2,1,0:T(4,128)(2,1)} %get-tuple-element.49), calls=%async_computation.1 | async-start | bytes 589824 | tf_op jit(solution)/shard_map/all_to_all | solution.py:388
  54.1 17.9 %collective-permute-start.8 = (bf16[288,1152]{1,0:T(8,128)(2,1)S(1)}, bf16[288,1152]{1,0:T(8,128)(2,1)S(1)}, u32[]{:S(2)}, u32[]{:S(2)}) collective-permute-start(bf16[288,1152]{1,0:T(8,128)(2,1)S(1)} %stack.21.rest_0_), channel_id=1, source_target_pairs={{0,32},{32,0},{1,33},{33,1},{2,34},{34,2},{3,35},{35,3},{4,36},{36... | collective-permute-start | bytes 1990664 | tf_op jit(solution)/shard_map/ppermute | solution.py:379
  69.4 6.8 %copy-start.8 = (bf16[32,4,1152]{2,1,0:T(4,128)(2,1)}, bf16[32,4,1152]{2,1,0:T(4,128)(2,1)S(1)}, u32[]{:S(2)}) copy-start(bf16[32,4,1152]{2,1,0:T(4,128)(2,1)S(1)} %all-to-all-done.1.time_ref) | copy-start | bytes 884740
  69.4 4.0 %collective-permute-start.9 = (bf16[288,1152]{1,0:T(8,128)(2,1)}, bf16[288,1152]{1,0:T(8,128)(2,1)S(1)}, u32[]{:S(2)}, u32[]{:S(2)}) collective-permute-start(bf16[288,1152]{1,0:T(8,128)(2,1)} %collective-permute-done.5.rest_1_), channel_id=1, source_target_pairs={{0,32},{32,0},{1,33},{33,1},{2,34},{34,2},{3,35},{35,3},{4,36},{36... | collective-permute-start | bytes 1990664 | tf_op jit(solution)/shard_map/ppermute | solution.py:379
  71.5 2.9 %collective-permute-start.10 = (bf16[288,1152]{1,0:T(8,128)(2,1)}, bf16[288,1152]{1,0:T(8,128)(2,1)S(1)}, u32[]{:S(2)}, u32[]{:S(2)}) collective-permute-start(bf16[288,1152]{1,0:T(8,128)(2,1)} %collective-permute-done.6.rest_2_), channel_id=1, source_target_pairs={{0,32},{32,0},{1,33},{33,1},{2,34},{34,2},{3,35},{35,3},{4,36},{36... | collective-permute-start | bytes 1990664 | tf_op jit(solution)/shard_map/ppermute | solution.py:379
  71.8 3.6 %collective-permute-start.11 = (bf16[288,1152]{1,0:T(8,128)(2,1)}, bf16[288,1152]{1,0:T(8,128)(2,1)S(1)}, u32[]{:S(2)}, u32[]{:S(2)}) collective-permute-start(bf16[288,1152]{1,0:T(8,128)(2,1)} %collective-permute-done.7.rest_3_), channel_id=1, source_target_pairs={{0,32},{32,0},{1,33},{33,1},{2,34},{34,2},{3,35},{35,3},{4,36},{36... | collective-permute-start | bytes 1990664 | tf_op jit(solution)/shard_map/ppermute | solution.py:379
  72.0 0.8 copy-start.9
  73.5 0.9 copy-start.10
  74.4 0.9 copy-start.11
  75.4 0.8 copy-start.12
  82.8 18.9 %all-to-all-start.2 = ((bf16[32,4,1280]{2,1,0:T(4,128)(2,1)}), bf16[32,4,1280]{2,1,0:T(4,128)(2,1)}, u32[]{:S(2)}, u32[]{:S(2)}) async-start(bf16[32,4,1280]{2,1,0:T(4,128)(2,1)} %get-tuple-element.56), calls=%async_computation.2 | async-start | bytes 655360 | tf_op jit(solution)/shard_map/all_to_all | solution.py:388
  91.2 25.4 %collective-permute-start.12 = (bf16[128,1728]{1,0:T(8,128)(2,1)}, bf16[128,1728]{1,0:T(8,128)(2,1)S(1)}, u32[]{:S(2)}, u32[]{:S(2)}) collective-permute-start(bf16[128,1728]{1,0:T(8,128)(2,1)} %get-tuple-element.61), channel_id=1, source_target_pairs={{0,8},{8,16},{16,24},{24,0},{1,9},{9,17},{17,25},{25,1},{2,10},{10... | collective-permute-start | bytes 1327112 | tf_op jit(solution)/shard_map/ppermute | solution.py:376
  92.5 26.1 %collective-permute-start.13 = (bf16[128,1728]{1,0:T(8,128)(2,1)}, bf16[128,1728]{1,0:T(8,128)(2,1)S(1)}, u32[]{:S(2)}, u32[]{:S(2)}) collective-permute-start(bf16[128,1728]{1,0:T(8,128)(2,1)} %get-tuple-element.62), channel_id=1, source_target_pairs={{0,16},{8,24},{16,0},{24,8},{1,17},{9,25},{17,1},{25,9},{2,18},{10... | collective-permute-start | bytes 1327112 | tf_op jit(solution)/shard_map/ppermute | solution.py:376
  94.9 23.7 %collective-permute-start.14 = (bf16[128,1728]{1,0:T(8,128)(2,1)}, bf16[128,1728]{1,0:T(8,128)(2,1)}, u32[]{:S(2)}, u32[]{:S(2)}) collective-permute-start(bf16[128,1728]{1,0:T(8,128)(2,1)} %get-tuple-element.63), channel_id=1, source_target_pairs={{0,24},{8,0},{16,8},{24,16},{1,25},{9,1},{17,9},{25,17},{2,26},{10... | collective-permute-start | bytes 1327112 | tf_op jit(solution)/shard_map/ppermute | solution.py:376
  109.0 9.6 %copy-start.4 = (bf16[128,1728]{1,0:T(8,128)(2,1)S(1)}, bf16[128,1728]{1,0:T(8,128)(2,1)}, u32[]{:S(2)}) copy-start(bf16[128,1728]{1,0:T(8,128)(2,1)} %get-tuple-element.65.pack_ref.rest_2_) | copy-start | bytes 1327108
  109.0 11.5 %copy-start.5 = (f32[8,128]{1,0:T(8,128)S(1)}, f32[8,128]{1,0:T(8,128)}, u32[]{:S(2)}) copy-start(f32[8,128]{1,0:T(8,128)} %get-tuple-element.64.rest_0_.spread_ref) | copy-start | bytes 12292
  109.0 30.8 %all-to-all-start.3 = ((bf16[32,4,3456]{2,1,0:T(4,128)(2,1)}), bf16[32,4,3456]{2,1,0:T(4,128)(2,1)S(1)}, u32[]{:S(2)}, u32[]{:S(2)}) async-start(bf16[32,4,3456]{2,1,0:T(4,128)(2,1)} %get-tuple-element.60), calls=%async_computation.3 | async-start | bytes 1769472 | tf_op jit(solution)/shard_map/all_to_all | solution.py:388
  116.6 6.7 %copy-start.1 = (s32[4]{0:T(128)S(1)}, s32[4]{0:T(128)}, u32[]{:S(2)}) copy-start(s32[4]{0:T(128)} %copy-done) | copy-start | bytes 52
  118.6 14.5 %copy-start.2 = (bf16[1,2,64,3456]{3,2,1,0:T(8,128)(2,1)S(1)}, bf16[1,2,64,3456]{3,2,1,0:T(8,128)(2,1)}, u32[]{:S(2)}) copy-start(bf16[1,2,64,3456]{3,2,1,0:T(8,128)(2,1)} %param.7) | copy-start | bytes 2654212
  118.6 14.5 %copy-start.6 = (f32[16,128,128]{2,1,0:T(8,128)S(1)}, f32[16,128,128]{2,1,0:T(8,128)}, u32[]{:S(2)}) copy-start(f32[16,128,128]{2,1,0:T(8,128)} %get-tuple-element.75.probs_ref) | copy-start | bytes 3145732
  118.6 14.5 %copy-start.7 = (bf16[128,1152]{1,0:T(8,128)(2,1)S(1)}, bf16[128,1152]{1,0:T(8,128)(2,1)}, u32[]{:S(2)}) copy-start(bf16[128,1152]{1,0:T(8,128)(2,1)} %space_back.1.grad_ref) | copy-start | bytes 884740
  118.6 4.6 %collective-permute-start.16 = (bf16[128,1728]{1,0:T(8,128)(2,1)S(1)}, bf16[128,1728]{1,0:T(8,128)(2,1)S(1)}, u32[]{:S(2)}, u32[]{:S(2)}) collective-permute-start(bf16[128,1728]{1,0:T(8,128)(2,1)S(1)} %copy-done.4), channel_id=1, source_target_pairs={{0,32},{32,0},{1,33},{33,1},{2,34},{34,2},{3,35},{35,3},{4,36},{36... | collective-permute-start | bytes 1327112 | tf_op jit(solution)/shard_map/ppermute | solution.py:379
  119.8 3.4 %collective-permute-start.17 = (bf16[128,1728]{1,0:T(8,128)(2,1)S(1)}, bf16[128,1728]{1,0:T(8,128)(2,1)S(1)}, u32[]{:S(2)}, u32[]{:S(2)}) collective-permute-start(bf16[128,1728]{1,0:T(8,128)(2,1)S(1)} %collective-permute-done.12.rest_3_), channel_id=1, source_target_pairs={{0,32},{32,0},{1,33},{33,1},{2,34},{34,2},{3,35},{35,3},{4,36},{36... | collective-permute-start | bytes 1327112 | tf_op jit(solution)/shard_map/ppermute | solution.py:379
  119.9 3.3 %collective-permute-start.18 = (bf16[128,1728]{1,0:T(8,128)(2,1)S(1)}, bf16[128,1728]{1,0:T(8,128)(2,1)S(1)}, u32[]{:S(2)}, u32[]{:S(2)}) collective-permute-start(bf16[128,1728]{1,0:T(8,128)(2,1)S(1)} %collective-permute-done.13.rest_4_), channel_id=1, source_target_pairs={{0,32},{32,0},{1,33},{33,1},{2,34},{34,2},{3,35},{35,3},{4,36},{36... | collective-permute-start | bytes 1327112 | tf_op jit(solution)/shard_map/ppermute | solution.py:379
  120.3 3.0 %collective-permute-start.19 = (bf16[128,1728]{1,0:T(8,128)(2,1)}, bf16[128,1728]{1,0:T(8,128)(2,1)S(1)}, u32[]{:S(2)}, u32[]{:S(2)}) collective-permute-start(bf16[128,1728]{1,0:T(8,128)(2,1)} %collective-permute-done.14.rest_5_), channel_id=1, source_target_pairs={{0,32},{32,0},{1,33},{33,1},{2,34},{34,2},{3,35},{35,3},{4,36},{36... | collective-permute-start | bytes 1327112 | tf_op jit(solution)/shard_map/ppermute | solution.py:379
  120.4 2.8 %collective-permute-start.15 = (f32[8,128]{1,0:T(8,128)S(1)}, f32[8,128]{1,0:T(8,128)S(1)}, u32[]{:S(2)}, u32[]{:S(2)}) collective-permute-start(f32[8,128]{1,0:T(8,128)S(1)} %copy-done.5), channel_id=1, source_target_pairs={{0,32},{32,0},{1,33},{33,1},{2,34},{34,2},{3,35},{35,3},{4,36},{36... | collective-permute-start | bytes 12296 | tf_op jit(solution)/shard_map/ppermute | solution.py:379
  126.7 12.0 %collective-permute-start.20 = (bf16[72,1152]{1,0:T(8,128)(2,1)S(1)}, bf16[72,1152]{1,0:T(8,128)(2,1)S(1)}, u32[]{:S(2)}, u32[]{:S(2)}) collective-permute-start(bf16[72,1152]{1,0:T(8,128)(2,1)S(1)} %get-tuple-element.70), channel_id=1, source_target_pairs={{0,64},{64,128},{128,192},{192,0},{1,65},{65,129},{129,193},{193,1... | collective-permute-start | bytes 497672 | tf_op jit(solution)/shard_map/ppermute | solution.py:376
  128.5 11.1 %collective-permute-start.21 = (bf16[72,1152]{1,0:T(8,128)(2,1)S(1)}, bf16[72,1152]{1,0:T(8,128)(2,1)S(1)}, u32[]{:S(2)}, u32[]{:S(2)}) collective-permute-start(bf16[72,1152]{1,0:T(8,128)(2,1)S(1)} %get-tuple-element.71), channel_id=1, source_target_pairs={{0,128},{64,192},{128,0},{192,64},{1,129},{65,193},{129,1},{193,65... | collective-permute-start | bytes 497672 | tf_op jit(solution)/shard_map/ppermute | solution.py:376
  132.0 7.6 %collective-permute-start.22 = (bf16[72,1152]{1,0:T(8,128)(2,1)S(1)}, bf16[72,1152]{1,0:T(8,128)(2,1)S(1)}, u32[]{:S(2)}, u32[]{:S(2)}) collective-permute-start(bf16[72,1152]{1,0:T(8,128)(2,1)S(1)} %get-tuple-element.72), channel_id=1, source_target_pairs={{0,192},{64,0},{128,64},{192,128},{1,193},{65,1},{129,65},{193,129... | collective-permute-start | bytes 497672 | tf_op jit(solution)/shard_map/ppermute | solution.py:376
  139.7 5.2 %collective-permute-start.23 = (bf16[36,1152]{1,0:T(8,128)(2,1)S(1)}, bf16[36,1152]{1,0:T(8,128)(2,1)S(1)}, u32[]{:S(2)}, u32[]{:S(2)}) collective-permute-start(bf16[36,1152]{1,0:T(8,128)(2,1)S(1)} %get-tuple-element.79), channel_id=1, source_target_pairs={{0,0},{1,1},{2,2},{3,3},{4,4},{5,5},{6,6},{7,7},{64,65},{65,66},{6... | collective-permute-start | bytes 248840 | tf_op jit(solution)/shard_map/ppermute | solution.py:373
  140.4 7.5 %collective-permute-start.24 = (bf16[36,1152]{1,0:T(8,128)(2,1)S(1)}, bf16[36,1152]{1,0:T(8,128)(2,1)S(1)}, u32[]{:S(2)}, u32[]{:S(2)}) collective-permute-start(bf16[36,1152]{1,0:T(8,128)(2,1)S(1)} %get-tuple-element.80), channel_id=1, source_target_pairs={{0,4},{1,5},{2,6},{3,7},{4,0},{5,1},{6,2},{7,3},{64,69},{65,70},{6... | collective-permute-start | bytes 248840 | tf_op jit(solution)/shard_map/ppermute | solution.py:373
  147.9 7.5 %collective-permute-start.27 = (bf16[36,1152]{1,0:T(8,128)(2,1)S(1)}, bf16[36,1152]{1,0:T(8,128)(2,1)S(1)}, u32[]{:S(2)}, u32[]{:S(2)}) collective-permute-start(bf16[36,1152]{1,0:T(8,128)(2,1)S(1)} %add_convert_fusion.1), channel_id=1, source_target_pairs={{0,192},{64,0},{128,64},{192,128},{1,193},{65,1},{129,65},{193,129... | collective-permute-start | bytes 248840 | tf_op jit(solution)/shard_map/ppermute | solution.py:376
  151.7 5.6 %collective-permute-start.26 = (bf16[36,1152]{1,0:T(8,128)(2,1)S(1)}, bf16[36,1152]{1,0:T(8,128)(2,1)S(1)}, u32[]{:S(2)}, u32[]{:S(2)}) collective-permute-start(bf16[36,1152]{1,0:T(8,128)(2,1)S(1)} %add_convert_fusion.1), channel_id=1, source_target_pairs={{0,64},{64,128},{128,192},{192,0},{1,65},{65,129},{129,193},{193,1... | collective-permute-start | bytes 248840 | tf_op jit(solution)/shard_map/ppermute | solution.py:376
  151.7 5.6 %collective-permute-start.25 = (bf16[36,1152]{1,0:T(8,128)(2,1)S(1)}, bf16[36,1152]{1,0:T(8,128)(2,1)S(1)}, u32[]{:S(2)}, u32[]{:S(2)}) collective-permute-start(bf16[36,1152]{1,0:T(8,128)(2,1)S(1)} %add_convert_fusion.1), channel_id=1, source_target_pairs={{0,128},{64,192},{128,0},{192,64},{1,129},{65,193},{129,1},{193,65... | collective-permute-start | bytes 248840 | tf_op jit(solution)/shard_map/ppermute | solution.py:376
  157.4 7.8 %collective-permute-start.28 = (bf16[36,1152]{1,0:T(8,128)(2,1)S(1)}, bf16[36,1152]{1,0:T(8,128)(2,1)S(1)}, u32[]{:S(2)}, u32[]{:S(2)}) collective-permute-start(bf16[36,1152]{1,0:T(8,128)(2,1)S(1)} %add_convert_fusion.own_ref), channel_id=1, source_target_pairs={{0,32},{32,0},{1,33},{33,1},{2,34},{34,2},{3,35},{35,3},{4,36},{36... | collective-permute-start | bytes 248840 | tf_op jit(solution)/shard_map/ppermute | solution.py:379

commit v5 on v4

--- a/solution.py
+++ b/solution.py
@@ -146,7 +146,7 @@
     out_ref[...] = mul(natural_from_sent(), x_ref[...], TN).astype(BF16).reshape(32, 4, 3 * D)
 
 def send(x):
-    return call(send_kernel, sent_rows(3 * D), specs(vmem=1), [], "send_order")(x)
+    return call(send_kernel, sent_rows(3 * D), specs(vmem=1), [], "send_order", vmem=32 * 1024 * 1024)(x)
 
 def receive_kernel(x_ref, out_ref):
     x = x_ref[...].reshape(TOKENS, 3 * D)

time: 168 us -> 168 us (level)
    unnamed x26 -> x28, local copies, waits for them, and re-layouts: 3.43 us -> 4.6 us
where the time goes in v5:
time: 168 us
  starting transfers between devices  87.9 us (52%)
  Pallas kernels  42.8 us (25%)
  waiting for transfers between devices  28 us (17%)
  local copies, waits for them, and re-layouts  5.11 us (3%)
  between operations  2.67 us (2%)
    ppermute x15, starting transfers between devices, shift(): lax.ppermute(value, axis, [(i, (i + step) % size) for i in range(size)])  30.4 us
    all_to_all x4, starting transfers between devices, exchange(): return lax.all_to_all(value, axis, split_axis=0, concat_axis=0, tiled=True)  28.8 us
    ppermute x15, waiting for transfers between devices, shift(): lax.ppermute(value, axis, [(i, (i + step) % size) for i in range(size)])  20.2 us
    ppermute x10, starting transfers between devices, swap(): return lax.ppermute(value, 'core', [(0, 1), (1, 0)])  15.1 us
    ppermute x4, starting transfers between devices, shift_z(): return lax.ppermute(value, ('y', 'z'), pairs)  13.7 us
    pallas_call x1, Pallas kernels, attend_back_time(): call(attend_back_time_kernel, (sent_rows(3 * D), jax.ShapeDtypeStruct((8,...  7.25 us
    pallas_call x1, Pallas kernels, project(): call(project_kernel, (sent_rows(D + LANES),) + (packed,) * 4, specs(smem=...  6.59 us
    pallas_call x1, Pallas kernels, attend_back_space(): call(attend_back_space_kernel, jax.ShapeDtypeStruct((TOKENS, 3 * D), BF16...  5.57 us
  transfers between devices with their start and end apart: 33, of which 14 were waited for; matrix products, arithmetic and copies ran while one was open for 0% of the time, Pallas kernels for 21%

profile of v5, /device:TPU:1, one launch (start us, length us, event | category | flops | bytes accessed | tf_op | source)
XLA Modules:
  0.0 167.6 jit_solution(7857127829618573936)
XLA Ops:
  0.6 0.9 broadcast_select_fusion
  1.6 7.8 %collective-permute-start.1 = (bf16[36,1152]{1,0:T(8,128)(2,1)S(1)}, bf16[36,1152]{1,0:T(8,128)(2,1)S(1)}, u32[]{:S(2)}, u32[]{:S(2)}) collective-permute-start(bf16[36,1152]{1,0:T(8,128)(2,1)S(1)} %broadcast_select_fusion), channel_id=1, source_target_pairs={{0,4},{1,5},{2,6},{3,7},{4,0},{5,1},{6,2},{7,3},{64,67},{65,68},{6... | collective-permute-start | bytes 248840 | tf_op jit(solution)/shard_map/ppermute | solution.py:373
  10.0 1.2 copy-done.2
  11.2 1.3 send_order.1
  12.6 5.9 %all-to-all-start = ((bf16[32,4,3456]{2,1,0:T(4,128)(2,1)}), bf16[32,4,3456]{2,1,0:T(4,128)(2,1)}, u32[]{:S(2)}, u32[]{:S(2)}) async-start(bf16[32,4,3456]{2,1,0:T(4,128)(2,1)} %send_order.1), calls=%async_computation | async-start | bytes 1769472 | tf_op jit(solution)/shard_map/all_to_all | solution.py:388
  18.5 4.5 %collective-permute-start.4 = (bf16[72,1152]{1,0:T(8,128)(2,1)S(1)}, bf16[72,1152]{1,0:T(8,128)(2,1)S(1)}, u32[]{:S(2)}, u32[]{:S(2)}) collective-permute-start(bf16[72,1152]{1,0:T(8,128)(2,1)S(1)} %pad_maximum_fusion.refs_0_), channel_id=1, source_target_pairs={{0,64},{64,128},{128,192},{192,0},{1,65},{65,129},{129,193},{193,1... | collective-permute-start | bytes 497672 | tf_op jit(solution)/shard_map/ppermute | solution.py:376
  23.1 1.7 %collective-permute-start.3 = (bf16[72,1152]{1,0:T(8,128)(2,1)S(1)}, bf16[72,1152]{1,0:T(8,128)(2,1)S(1)}, u32[]{:S(2)}, u32[]{:S(2)}) collective-permute-start(bf16[72,1152]{1,0:T(8,128)(2,1)S(1)} %pad_maximum_fusion.refs_0_), channel_id=1, source_target_pairs={{0,128},{64,192},{128,0},{192,64},{1,129},{65,193},{129,1},{193,65... | collective-permute-start | bytes 497672 | tf_op jit(solution)/shard_map/ppermute | solution.py:376
  24.8 2.0 %collective-permute-start.2 = (bf16[72,1152]{1,0:T(8,128)(2,1)S(1)}, bf16[72,1152]{1,0:T(8,128)(2,1)S(1)}, u32[]{:S(2)}, u32[]{:S(2)}) collective-permute-start(bf16[72,1152]{1,0:T(8,128)(2,1)S(1)} %pad_maximum_fusion.refs_0_), channel_id=1, source_target_pairs={{0,192},{64,0},{128,64},{192,128},{1,193},{65,1},{129,65},{193,129... | collective-permute-start | bytes 497672 | tf_op jit(solution)/shard_map/ppermute | solution.py:376
  26.8 4.0 %collective-permute-done.3.refs_2_ = bf16[72,1152]{1,0:T(8,128)(2,1)S(1)} collective-permute-done((bf16[72,1152]{1,0:T(8,128)(2,1)S(1)}, bf16[72,1152]{1,0:T(8,128)(2,1)S(1)}, u32[]{:S(2)}, u32[]{:S(2)}) %collective-permute-start.3) | collective-permute-done | bytes 165920 | tf_op jit(solution)/shard_map/ppermute | solution.py:376
  31.1 1.1 stack.21.rest_0_
  32.2 1.1 collective-permute-start.7
  33.2 2.5 %collective-permute-start.6 = (bf16[288,1152]{1,0:T(8,128)(2,1)S(1)}, bf16[288,1152]{1,0:T(8,128)(2,1)}, u32[]{:S(2)}, u32[]{:S(2)}) collective-permute-start(bf16[288,1152]{1,0:T(8,128)(2,1)S(1)} %stack.21.rest_0_), channel_id=1, source_target_pairs={{0,16},{8,24},{16,0},{24,8},{1,17},{9,25},{17,1},{25,9},{2,18},{10... | collective-permute-start | bytes 1990664 | tf_op jit(solution)/shard_map/ppermute | solution.py:376
  35.7 1.1 collective-permute-start.5
  36.8 5.2 %attend_space.1 = (bf16[128,1152]{1,0:T(8,128)(2,1)}, f32[16,128,128]{2,1,0:T(8,128)}) custom-call(bf16[128,3456]{1,0:T(8,128)(2,1)} %bitcast.12), custom_call_target="tpu_custom_call" | custom-call | flops 14000000000 | bytes 1 | tf_op jit(solution)/shard_map/attend_space/pallas_call | solution.py:111
  42.0 5.2 %attend_time.1 = (bf16[32,4,1152]{2,1,0:T(4,128)(2,1)}, f32[16,128,128]{2,1,0:T(8,128)}) custom-call(bf16[32,4,3456]{2,1,0:T(4,128)(2,1)} %all-to-all-done.x_ref), custom_call_target="tpu_custom_call" | custom-call | flops 3000000000 | bytes 1 | tf_op jit(solution)/shard_map/attend_time/pallas_call | solution.py:143
  47.2 6.9 %all-to-all-start.1 = ((bf16[32,4,1152]{2,1,0:T(4,128)(2,1)}), bf16[32,4,1152]{2,1,0:T(4,128)(2,1)S(1)}, u32[]{:S(2)}, u32[]{:S(2)}) async-start(bf16[32,4,1152]{2,1,0:T(4,128)(2,1)} %get-tuple-element.49), calls=%async_computation.1 | async-start | bytes 589824 | tf_op jit(solution)/shard_map/all_to_all | solution.py:388
  54.1 3.8 %collective-permute-start.8 = (bf16[288,1152]{1,0:T(8,128)(2,1)S(1)}, bf16[288,1152]{1,0:T(8,128)(2,1)S(1)}, u32[]{:S(2)}, u32[]{:S(2)}) collective-permute-start(bf16[288,1152]{1,0:T(8,128)(2,1)S(1)} %stack.21.rest_0_), channel_id=1, source_target_pairs={{0,32},{32,0},{1,33},{33,1},{2,34},{34,2},{3,35},{35,3},{4,36},{36... | collective-permute-start | bytes 1990664 | tf_op jit(solution)/shard_map/ppermute | solution.py:379
  57.9 11.1 %collective-permute-done.6.rest_2_ = bf16[288,1152]{1,0:T(8,128)(2,1)} collective-permute-done((bf16[288,1152]{1,0:T(8,128)(2,1)S(1)}, bf16[288,1152]{1,0:T(8,128)(2,1)}, u32[]{:S(2)}, u32[]{:S(2)}) %collective-permute-start.6) | collective-permute-done | bytes 663584 | tf_op jit(solution)/shard_map/ppermute | solution.py:376
  69.4 2.1 %collective-permute-start.9 = (bf16[288,1152]{1,0:T(8,128)(2,1)}, bf16[288,1152]{1,0:T(8,128)(2,1)S(1)}, u32[]{:S(2)}, u32[]{:S(2)}) collective-permute-start(bf16[288,1152]{1,0:T(8,128)(2,1)} %collective-permute-done.5.rest_1_), channel_id=1, source_target_pairs={{0,32},{32,0},{1,33},{33,1},{2,34},{34,2},{3,35},{35,3},{4,36},{36... | collective-permute-start | bytes 1990664 | tf_op jit(solution)/shard_map/ppermute | solution.py:379
  72.0 0.8 copy-done.10
  73.5 0.9 copy-done.11
  74.4 0.9 copy-done.12
  76.2 6.6 %project.1 = (bf16[32,4,1280]{2,1,0:T(4,128)(2,1)}, bf16[128,1728]{1,0:T(8,128)(2,1)}, bf16[128,1728]{1,0:T(8,128)(2,1)}, bf16[128,1728]{1,0:T(8,128)(2,1)}, bf16[128,1728]{1,0:T(8,128)(2,1)}) custom-call(s32[4]{0:T(128)} %copy-done, bf16[32,4,1152]{2,1,0:T(4,128)(2,1)} %copy-done.9, bf16[128,1152]{1,0:T(8,128)(2,1)} %bitcast.14, ...), custom_call_target="tpu_custom_call" | custom-call | flops 8000000000 | bytes 1 | tf_op jit(solution)/shard_map/project/pallas_call | solution.py:284
  82.8 8.4 %all-to-all-start.2 = ((bf16[32,4,1280]{2,1,0:T(4,128)(2,1)}), bf16[32,4,1280]{2,1,0:T(4,128)(2,1)}, u32[]{:S(2)}, u32[]{:S(2)}) async-start(bf16[32,4,1280]{2,1,0:T(4,128)(2,1)} %get-tuple-element.56), calls=%async_computation.2 | async-start | bytes 655360 | tf_op jit(solution)/shard_map/all_to_all | solution.py:388
  91.2 1.2 collective-permute-start.12
  92.5 2.4 %collective-permute-start.13 = (bf16[128,1728]{1,0:T(8,128)(2,1)}, bf16[128,1728]{1,0:T(8,128)(2,1)S(1)}, u32[]{:S(2)}, u32[]{:S(2)}) collective-permute-start(bf16[128,1728]{1,0:T(8,128)(2,1)} %get-tuple-element.62), channel_id=1, source_target_pairs={{0,16},{8,24},{16,0},{24,8},{1,17},{9,25},{17,1},{25,9},{2,18},{10... | collective-permute-start | bytes 1327112 | tf_op jit(solution)/shard_map/ppermute | solution.py:376
  94.9 1.1 collective-permute-start.14
  96.0 4.4 %space_back.1.grad_ref = bf16[128,1152]{1,0:T(8,128)(2,1)} custom-call(s32[4]{0:T(128)} %copy-done, bf16[128,1728]{1,0:T(8,128)(2,1)} %get-tuple-element.65.pack_ref.rest_2_, bf16[288,1152]{1,0:T(8,128)(2,1)} %copy-done.4, bf16[288,1152]{1,0:T(8,128)(2,1)} %collective-permute-done.5.rest_1_, bf16[288,1152]{1,0:T(8,128)(2,1)} %collective-permute-done.6.rest_2_, ...), custom_call_target="tpu_custom_call" | custom-call | flops 3000000000 | bytes 1 | tf_op jit(solution)/shard_map/space_back/pallas_call | solution.py:318
  100.5 1.2 all-to-all-done.2.grad_ref
  101.7 7.2 %attend_back_time.1 = (bf16[32,4,3456]{2,1,0:T(4,128)(2,1)}, f32[8,128]{1,0:T(8,128)}) custom-call(bf16[32,4,3456]{2,1,0:T(4,128)(2,1)} %all-to-all-done.x_ref, f32[16,128,128]{2,1,0:T(8,128)} %get-tuple-element.48.probs_ref, bf16[32,4,1280]{2,1,0:T(4,128)(2,1)} %all-to-all-done.2.grad_ref), custom_call_target="tpu_custom_call" | custom-call | flops 5000000000 | bytes 1 | tf_op jit(solution)/shard_map/attend_back_time/pallas_call | solution.py:190
  109.0 7.6 %all-to-all-start.3 = ((bf16[32,4,3456]{2,1,0:T(4,128)(2,1)}), bf16[32,4,3456]{2,1,0:T(4,128)(2,1)S(1)}, u32[]{:S(2)}, u32[]{:S(2)}) async-start(bf16[32,4,3456]{2,1,0:T(4,128)(2,1)} %get-tuple-element.60), calls=%async_computation.3 | async-start | bytes 1769472 | tf_op jit(solution)/shard_map/all_to_all | solution.py:388
  116.6 2.0 %collective-permute-done.13.rest_4_ = bf16[128,1728]{1,0:T(8,128)(2,1)S(1)} collective-permute-done((bf16[128,1728]{1,0:T(8,128)(2,1)}, bf16[128,1728]{1,0:T(8,128)(2,1)S(1)}, u32[]{:S(2)}, u32[]{:S(2)}) %collective-permute-start.13) | collective-permute-done | bytes 442400 | tf_op jit(solution)/shard_map/ppermute | solution.py:376
  118.6 1.2 collective-permute-start.16
  120.8 2.4 %collective-permute-done.15.rest_1_ = f32[8,128]{1,0:T(8,128)S(1)} collective-permute-done((f32[8,128]{1,0:T(8,128)S(1)}, f32[8,128]{1,0:T(8,128)S(1)}, u32[]{:S(2)}, u32[]{:S(2)}) %collective-permute-start.15) | collective-permute-done | bytes 4128 | tf_op jit(solution)/shard_map/ppermute | solution.py:379
  123.3 3.4 %weight_grad.1 = (bf16[72,1152]{1,0:T(8,128)(2,1)S(1)}, bf16[72,1152]{1,0:T(8,128)(2,1)S(1)}, bf16[72,1152]{1,0:T(8,128)(2,1)S(1)}, bf16[72,1152]{1,0:T(8,128)(2,1)S(1)}) custom-call(s32[4]{0:T(128)S(1)} %copy-done.1, f32[8,128]{1,0:T(8,128)S(1)} %copy-done.6, f32[8,128]{1,0:T(8,128)S(1)} %collective-permute-done.15.rest_1_, ...), custom_call_target="tpu_custom_call" | custom-call | flops 8000000000 | bytes 1 | tf_op jit(solution)/shard_map/weight_grad/pallas_call | solution.py:340
  126.7 1.8 %collective-permute-start.20 = (bf16[72,1152]{1,0:T(8,128)(2,1)S(1)}, bf16[72,1152]{1,0:T(8,128)(2,1)S(1)}, u32[]{:S(2)}, u32[]{:S(2)}) collective-permute-start(bf16[72,1152]{1,0:T(8,128)(2,1)S(1)} %get-tuple-element.70), channel_id=1, source_target_pairs={{0,64},{64,128},{128,192},{192,0},{1,65},{65,129},{129,193},{193,1... | collective-permute-start | bytes 497672 | tf_op jit(solution)/shard_map/ppermute | solution.py:376
  128.5 3.5 %collective-permute-start.21 = (bf16[72,1152]{1,0:T(8,128)(2,1)S(1)}, bf16[72,1152]{1,0:T(8,128)(2,1)S(1)}, u32[]{:S(2)}, u32[]{:S(2)}) collective-permute-start(bf16[72,1152]{1,0:T(8,128)(2,1)S(1)} %get-tuple-element.71), channel_id=1, source_target_pairs={{0,128},{64,192},{128,0},{192,64},{1,129},{65,193},{129,1},{193,65... | collective-permute-start | bytes 497672 | tf_op jit(solution)/shard_map/ppermute | solution.py:376
  132.0 1.0 collective-permute-start.22
  133.1 5.6 %attend_back_space.1 = bf16[128,3456]{1,0:T(8,128)(2,1)} custom-call(bf16[128,3456]{1,0:T(8,128)(2,1)S(1)} %bitcast.13, f32[16,128,128]{2,1,0:T(8,128)S(1)} %copy-done.7, bf16[128,1152]{1,0:T(8,128)(2,1)S(1)} %copy-done.8, f32[8,128]{1,0:T(8,128)S(1)} %copy-done.6), custom_call_target="tpu_custom_call" | custom-call | flops 1000000000 | bytes 1 | tf_op jit(solution)/shard_map/attend_back_space/pallas_call | solution.py:203
  138.6 1.0 collective-permute-done.21.refs_2_
  140.4 4.5 %collective-permute-start.24 = (bf16[36,1152]{1,0:T(8,128)(2,1)S(1)}, bf16[36,1152]{1,0:T(8,128)(2,1)S(1)}, u32[]{:S(2)}, u32[]{:S(2)}) collective-permute-start(bf16[36,1152]{1,0:T(8,128)(2,1)S(1)} %get-tuple-element.80), channel_id=1, source_target_pairs={{0,4},{1,5},{2,6},{3,7},{4,0},{5,1},{6,2},{7,3},{64,69},{65,70},{6... | collective-permute-start | bytes 248840 | tf_op jit(solution)/shard_map/ppermute | solution.py:373
  144.9 2.9 %collective-permute-done.24 = bf16[36,1152]{1,0:T(8,128)(2,1)S(1)} collective-permute-done((bf16[36,1152]{1,0:T(8,128)(2,1)S(1)}, bf16[36,1152]{1,0:T(8,128)(2,1)S(1)}, u32[]{:S(2)}, u32[]{:S(2)}) %collective-permute-start.24) | collective-permute-done | bytes 82976 | tf_op jit(solution)/shard_map/ppermute | solution.py:373
  147.9 3.8 %collective-permute-start.27 = (bf16[36,1152]{1,0:T(8,128)(2,1)S(1)}, bf16[36,1152]{1,0:T(8,128)(2,1)S(1)}, u32[]{:S(2)}, u32[]{:S(2)}) collective-permute-start(bf16[36,1152]{1,0:T(8,128)(2,1)S(1)} %add_convert_fusion.1), channel_id=1, source_target_pairs={{0,192},{64,0},{128,64},{192,128},{1,193},{65,1},{129,65},{193,129... | collective-permute-start | bytes 248840 | tf_op jit(solution)/shard_map/ppermute | solution.py:376
  151.7 2.5 %collective-permute-start.25 = (bf16[36,1152]{1,0:T(8,128)(2,1)S(1)}, bf16[36,1152]{1,0:T(8,128)(2,1)S(1)}, u32[]{:S(2)}, u32[]{:S(2)}) collective-permute-start(bf16[36,1152]{1,0:T(8,128)(2,1)S(1)} %add_convert_fusion.1), channel_id=1, source_target_pairs={{0,128},{64,192},{128,0},{192,64},{1,129},{65,193},{129,1},{193,65... | collective-permute-start | bytes 248840 | tf_op jit(solution)/shard_map/ppermute | solution.py:376
  155.4 1.9 %collective-permute-done.26 = bf16[36,1152]{1,0:T(8,128)(2,1)S(1)} collective-permute-done((bf16[36,1152]{1,0:T(8,128)(2,1)S(1)}, bf16[36,1152]{1,0:T(8,128)(2,1)S(1)}, u32[]{:S(2)}, u32[]{:S(2)}) %collective-permute-start.26) | collective-permute-done | bytes 82976 | tf_op jit(solution)/shard_map/ppermute | solution.py:376
  157.4 6.5 %collective-permute-start.28 = (bf16[36,1152]{1,0:T(8,128)(2,1)S(1)}, bf16[36,1152]{1,0:T(8,128)(2,1)S(1)}, u32[]{:S(2)}, u32[]{:S(2)}) collective-permute-start(bf16[36,1152]{1,0:T(8,128)(2,1)S(1)} %add_convert_fusion.own_ref), channel_id=1, source_target_pairs={{0,32},{32,0},{1,33},{33,1},{2,34},{34,2},{3,35},{35,3},{4,36},{36... | collective-permute-start | bytes 248840 | tf_op jit(solution)/shard_map/ppermute | solution.py:379
  163.8 1.3 natural_order.1
  165.1 1.3 finish.1
  (64 shorter events, 6.0 us)
Async XLA Ops:
  1.6 16.9 %collective-permute-start.1 = (bf16[36,1152]{1,0:T(8,128)(2,1)S(1)}, bf16[36,1152]{1,0:T(8,128)(2,1)S(1)}, u32[]{:S(2)}, u32[]{:S(2)}) collective-permute-start(bf16[36,1152]{1,0:T(8,128)(2,1)S(1)} %broadcast_select_fusion), channel_id=1, source_target_pairs={{0,4},{1,5},{2,6},{3,7},{4,0},{5,1},{6,2},{7,3},{64,67},{65,68},{6... | collective-permute-start | bytes 248840 | tf_op jit(solution)/shard_map/ppermute | solution.py:373
  9.4 9.1 %collective-permute-start = (bf16[36,1152]{1,0:T(8,128)(2,1)S(1)}, bf16[36,1152]{1,0:T(8,128)(2,1)S(1)}, u32[]{:S(2)}, u32[]{:S(2)}) collective-permute-start(bf16[36,1152]{1,0:T(8,128)(2,1)S(1)} %broadcast_select_fusion), channel_id=1, source_target_pairs={{0,0},{1,1},{2,2},{3,3},{4,4},{5,5},{6,6},{7,7},{64,71},{65,64},{6... | collective-permute-start | bytes 248840 | tf_op jit(solution)/shard_map/ppermute | solution.py:373
  10.0 1.2 copy-start.2
  12.6 29.5 %all-to-all-start = ((bf16[32,4,3456]{2,1,0:T(4,128)(2,1)}), bf16[32,4,3456]{2,1,0:T(4,128)(2,1)}, u32[]{:S(2)}, u32[]{:S(2)}) async-start(bf16[32,4,3456]{2,1,0:T(4,128)(2,1)} %send_order.1), calls=%async_computation | async-start | bytes 1769472 | tf_op jit(solution)/shard_map/all_to_all | solution.py:388
  18.5 8.3 %collective-permute-start.4 = (bf16[72,1152]{1,0:T(8,128)(2,1)S(1)}, bf16[72,1152]{1,0:T(8,128)(2,1)S(1)}, u32[]{:S(2)}, u32[]{:S(2)}) collective-permute-start(bf16[72,1152]{1,0:T(8,128)(2,1)S(1)} %pad_maximum_fusion.refs_0_), channel_id=1, source_target_pairs={{0,64},{64,128},{128,192},{192,0},{1,65},{65,129},{129,193},{193,1... | collective-permute-start | bytes 497672 | tf_op jit(solution)/shard_map/ppermute | solution.py:376
  23.1 7.8 %collective-permute-start.3 = (bf16[72,1152]{1,0:T(8,128)(2,1)S(1)}, bf16[72,1152]{1,0:T(8,128)(2,1)S(1)}, u32[]{:S(2)}, u32[]{:S(2)}) collective-permute-start(bf16[72,1152]{1,0:T(8,128)(2,1)S(1)} %pad_maximum_fusion.refs_0_), channel_id=1, source_target_pairs={{0,128},{64,192},{128,0},{192,64},{1,129},{65,193},{129,1},{193,65... | collective-permute-start | bytes 497672 | tf_op jit(solution)/shard_map/ppermute | solution.py:376
  24.8 6.3 %collective-permute-start.2 = (bf16[72,1152]{1,0:T(8,128)(2,1)S(1)}, bf16[72,1152]{1,0:T(8,128)(2,1)S(1)}, u32[]{:S(2)}, u32[]{:S(2)}) collective-permute-start(bf16[72,1152]{1,0:T(8,128)(2,1)S(1)} %pad_maximum_fusion.refs_0_), channel_id=1, source_target_pairs={{0,192},{64,0},{128,64},{192,128},{1,193},{65,1},{129,65},{193,129... | collective-permute-start | bytes 497672 | tf_op jit(solution)/shard_map/ppermute | solution.py:376
  26.8 5.3 %copy-start = (s32[4]{0:T(128)}, s32[4]{0:T(128)S(1)}, u32[]{:S(2)}) copy-start(s32[4]{0:T(128)S(1)} %pad_add_fusion.place_ref) | copy-start | bytes 52
  32.2 21.9 %copy-start.4 = (bf16[288,1152]{1,0:T(8,128)(2,1)}, bf16[288,1152]{1,0:T(8,128)(2,1)S(1)}, u32[]{:S(2)}) copy-start(bf16[288,1152]{1,0:T(8,128)(2,1)S(1)} %stack.21.rest_0_) | copy-start | bytes 1990660
  32.2 25.8 %collective-permute-start.7 = (bf16[288,1152]{1,0:T(8,128)(2,1)S(1)}, bf16[288,1152]{1,0:T(8,128)(2,1)}, u32[]{:S(2)}, u32[]{:S(2)}) collective-permute-start(bf16[288,1152]{1,0:T(8,128)(2,1)S(1)} %stack.21.rest_0_), channel_id=1, source_target_pairs={{0,8},{8,16},{16,24},{24,0},{1,9},{9,17},{17,25},{25,1},{2,10},{10... | collective-permute-start | bytes 1990664 | tf_op jit(solution)/shard_map/ppermute | solution.py:376
  33.2 35.8 %collective-permute-start.6 = (bf16[288,1152]{1,0:T(8,128)(2,1)S(1)}, bf16[288,1152]{1,0:T(8,128)(2,1)}, u32[]{:S(2)}, u32[]{:S(2)}) collective-permute-start(bf16[288,1152]{1,0:T(8,128)(2,1)S(1)} %stack.21.rest_0_), channel_id=1, source_target_pairs={{0,16},{8,24},{16,0},{24,8},{1,17},{9,25},{17,1},{25,9},{2,18},{10... | collective-permute-start | bytes 1990664 | tf_op jit(solution)/shard_map/ppermute | solution.py:376
  35.7 33.3 %collective-permute-start.5 = (bf16[288,1152]{1,0:T(8,128)(2,1)S(1)}, bf16[288,1152]{1,0:T(8,128)(2,1)}, u32[]{:S(2)}, u32[]{:S(2)}) collective-permute-start(bf16[288,1152]{1,0:T(8,128)(2,1)S(1)} %stack.21.rest_0_), channel_id=1, source_target_pairs={{0,24},{8,0},{16,8},{24,16},{1,25},{9,1},{17,9},{25,17},{2,26},{10... | collective-permute-start | bytes 1990664 | tf_op jit(solution)/shard_map/ppermute | solution.py:376
  47.2 22.2 %all-to-all-start.1 = ((bf16[32,4,1152]{2,1,0:T(4,128)(2,1)}), bf16[32,4,1152]{2,1,0:T(4,128)(2,1)S(1)}, u32[]{:S(2)}, u32[]{:S(2)}) async-start(bf16[32,4,1152]{2,1,0:T(4,128)(2,1)} %get-tuple-element.49), calls=%async_computation.1 | async-start | bytes 589824 | tf_op jit(solution)/shard_map/all_to_all | solution.py:388
  54.1 17.9 %collective-permute-start.8 = (bf16[288,1152]{1,0:T(8,128)(2,1)S(1)}, bf16[288,1152]{1,0:T(8,128)(2,1)S(1)}, u32[]{:S(2)}, u32[]{:S(2)}) collective-permute-start(bf16[288,1152]{1,0:T(8,128)(2,1)S(1)} %stack.21.rest_0_), channel_id=1, source_target_pairs={{0,32},{32,0},{1,33},{33,1},{2,34},{34,2},{3,35},{35,3},{4,36},{36... | collective-permute-start | bytes 1990664 | tf_op jit(solution)/shard_map/ppermute | solution.py:379
  69.4 6.8 %copy-start.9 = (bf16[32,4,1152]{2,1,0:T(4,128)(2,1)}, bf16[32,4,1152]{2,1,0:T(4,128)(2,1)S(1)}, u32[]{:S(2)}) copy-start(bf16[32,4,1152]{2,1,0:T(4,128)(2,1)S(1)} %all-to-all-done.1.time_ref) | copy-start | bytes 884740
  69.4 4.0 %collective-permute-start.9 = (bf16[288,1152]{1,0:T(8,128)(2,1)}, bf16[288,1152]{1,0:T(8,128)(2,1)S(1)}, u32[]{:S(2)}, u32[]{:S(2)}) collective-permute-start(bf16[288,1152]{1,0:T(8,128)(2,1)} %collective-permute-done.5.rest_1_), channel_id=1, source_target_pairs={{0,32},{32,0},{1,33},{33,1},{2,34},{34,2},{3,35},{35,3},{4,36},{36... | collective-permute-start | bytes 1990664 | tf_op jit(solution)/shard_map/ppermute | solution.py:379
  71.5 2.9 %collective-permute-start.10 = (bf16[288,1152]{1,0:T(8,128)(2,1)}, bf16[288,1152]{1,0:T(8,128)(2,1)S(1)}, u32[]{:S(2)}, u32[]{:S(2)}) collective-permute-start(bf16[288,1152]{1,0:T(8,128)(2,1)} %collective-permute-done.6.rest_2_), channel_id=1, source_target_pairs={{0,32},{32,0},{1,33},{33,1},{2,34},{34,2},{3,35},{35,3},{4,36},{36... | collective-permute-start | bytes 1990664 | tf_op jit(solution)/shard_map/ppermute | solution.py:379
  71.8 3.6 %collective-permute-start.11 = (bf16[288,1152]{1,0:T(8,128)(2,1)}, bf16[288,1152]{1,0:T(8,128)(2,1)S(1)}, u32[]{:S(2)}, u32[]{:S(2)}) collective-permute-start(bf16[288,1152]{1,0:T(8,128)(2,1)} %collective-permute-done.7.rest_3_), channel_id=1, source_target_pairs={{0,32},{32,0},{1,33},{33,1},{2,34},{34,2},{3,35},{35,3},{4,36},{36... | collective-permute-start | bytes 1990664 | tf_op jit(solution)/shard_map/ppermute | solution.py:379
  72.0 0.8 copy-start.10
  73.5 0.9 copy-start.11
  74.4 0.9 copy-start.12
  75.4 0.8 copy-start.13
  82.8 18.9 %all-to-all-start.2 = ((bf16[32,4,1280]{2,1,0:T(4,128)(2,1)}), bf16[32,4,1280]{2,1,0:T(4,128)(2,1)}, u32[]{:S(2)}, u32[]{:S(2)}) async-start(bf16[32,4,1280]{2,1,0:T(4,128)(2,1)} %get-tuple-element.56), calls=%async_computation.2 | async-start | bytes 655360 | tf_op jit(solution)/shard_map/all_to_all | solution.py:388
  91.2 25.4 %collective-permute-start.12 = (bf16[128,1728]{1,0:T(8,128)(2,1)}, bf16[128,1728]{1,0:T(8,128)(2,1)S(1)}, u32[]{:S(2)}, u32[]{:S(2)}) collective-permute-start(bf16[128,1728]{1,0:T(8,128)(2,1)} %get-tuple-element.61), channel_id=1, source_target_pairs={{0,8},{8,16},{16,24},{24,0},{1,9},{9,17},{17,25},{25,1},{2,10},{10... | collective-permute-start | bytes 1327112 | tf_op jit(solution)/shard_map/ppermute | solution.py:376
  92.5 26.1 %collective-permute-start.13 = (bf16[128,1728]{1,0:T(8,128)(2,1)}, bf16[128,1728]{1,0:T(8,128)(2,1)S(1)}, u32[]{:S(2)}, u32[]{:S(2)}) collective-permute-start(bf16[128,1728]{1,0:T(8,128)(2,1)} %get-tuple-element.62), channel_id=1, source_target_pairs={{0,16},{8,24},{16,0},{24,8},{1,17},{9,25},{17,1},{25,9},{2,18},{10... | collective-permute-start | bytes 1327112 | tf_op jit(solution)/shard_map/ppermute | solution.py:376
  94.9 23.7 %collective-permute-start.14 = (bf16[128,1728]{1,0:T(8,128)(2,1)}, bf16[128,1728]{1,0:T(8,128)(2,1)}, u32[]{:S(2)}, u32[]{:S(2)}) collective-permute-start(bf16[128,1728]{1,0:T(8,128)(2,1)} %get-tuple-element.63), channel_id=1, source_target_pairs={{0,24},{8,0},{16,8},{24,16},{1,25},{9,1},{17,9},{25,17},{2,26},{10... | collective-permute-start | bytes 1327112 | tf_op jit(solution)/shard_map/ppermute | solution.py:376
  109.0 9.6 %copy-start.5 = (bf16[128,1728]{1,0:T(8,128)(2,1)S(1)}, bf16[128,1728]{1,0:T(8,128)(2,1)}, u32[]{:S(2)}) copy-start(bf16[128,1728]{1,0:T(8,128)(2,1)} %get-tuple-element.65.pack_ref.rest_2_) | copy-start | bytes 1327108
  109.0 11.5 %copy-start.6 = (f32[8,128]{1,0:T(8,128)S(1)}, f32[8,128]{1,0:T(8,128)}, u32[]{:S(2)}) copy-start(f32[8,128]{1,0:T(8,128)} %get-tuple-element.64.rest_0_.spread_ref) | copy-start | bytes 12292
  109.0 30.7 %all-to-all-start.3 = ((bf16[32,4,3456]{2,1,0:T(4,128)(2,1)}), bf16[32,4,3456]{2,1,0:T(4,128)(2,1)S(1)}, u32[]{:S(2)}, u32[]{:S(2)}) async-start(bf16[32,4,3456]{2,1,0:T(4,128)(2,1)} %get-tuple-element.60), calls=%async_computation.3 | async-start | bytes 1769472 | tf_op jit(solution)/shard_map/all_to_all | solution.py:388
  116.6 6.7 %copy-start.1 = (s32[4]{0:T(128)S(1)}, s32[4]{0:T(128)}, u32[]{:S(2)}) copy-start(s32[4]{0:T(128)} %copy-done) | copy-start | bytes 52
  118.6 14.5 %copy-start.3 = (bf16[1,2,64,3456]{3,2,1,0:T(8,128)(2,1)S(1)}, bf16[1,2,64,3456]{3,2,1,0:T(8,128)(2,1)}, u32[]{:S(2)}) copy-start(bf16[1,2,64,3456]{3,2,1,0:T(8,128)(2,1)} %param.7) | copy-start | bytes 2654212
  118.6 14.5 %copy-start.7 = (f32[16,128,128]{2,1,0:T(8,128)S(1)}, f32[16,128,128]{2,1,0:T(8,128)}, u32[]{:S(2)}) copy-start(f32[16,128,128]{2,1,0:T(8,128)} %get-tuple-element.75.probs_ref) | copy-start | bytes 3145732
  118.6 14.5 %copy-start.8 = (bf16[128,1152]{1,0:T(8,128)(2,1)S(1)}, bf16[128,1152]{1,0:T(8,128)(2,1)}, u32[]{:S(2)}) copy-start(bf16[128,1152]{1,0:T(8,128)(2,1)} %space_back.1.grad_ref) | copy-start | bytes 884740
  118.6 4.6 %collective-permute-start.16 = (bf16[128,1728]{1,0:T(8,128)(2,1)S(1)}, bf16[128,1728]{1,0:T(8,128)(2,1)S(1)}, u32[]{:S(2)}, u32[]{:S(2)}) collective-permute-start(bf16[128,1728]{1,0:T(8,128)(2,1)S(1)} %copy-done.5), channel_id=1, source_target_pairs={{0,32},{32,0},{1,33},{33,1},{2,34},{34,2},{3,35},{35,3},{4,36},{36... | collective-permute-start | bytes 1327112 | tf_op jit(solution)/shard_map/ppermute | solution.py:379
  119.8 3.4 %collective-permute-start.17 = (bf16[128,1728]{1,0:T(8,128)(2,1)S(1)}, bf16[128,1728]{1,0:T(8,128)(2,1)S(1)}, u32[]{:S(2)}, u32[]{:S(2)}) collective-permute-start(bf16[128,1728]{1,0:T(8,128)(2,1)S(1)} %collective-permute-done.12.rest_3_), channel_id=1, source_target_pairs={{0,32},{32,0},{1,33},{33,1},{2,34},{34,2},{3,35},{35,3},{4,36},{36... | collective-permute-start | bytes 1327112 | tf_op jit(solution)/shard_map/ppermute | solution.py:379
  119.9 3.3 %collective-permute-start.18 = (bf16[128,1728]{1,0:T(8,128)(2,1)S(1)}, bf16[128,1728]{1,0:T(8,128)(2,1)S(1)}, u32[]{:S(2)}, u32[]{:S(2)}) collective-permute-start(bf16[128,1728]{1,0:T(8,128)(2,1)S(1)} %collective-permute-done.13.rest_4_), channel_id=1, source_target_pairs={{0,32},{32,0},{1,33},{33,1},{2,34},{34,2},{3,35},{35,3},{4,36},{36... | collective-permute-start | bytes 1327112 | tf_op jit(solution)/shard_map/ppermute | solution.py:379
  120.3 3.0 %collective-permute-start.19 = (bf16[128,1728]{1,0:T(8,128)(2,1)}, bf16[128,1728]{1,0:T(8,128)(2,1)S(1)}, u32[]{:S(2)}, u32[]{:S(2)}) collective-permute-start(bf16[128,1728]{1,0:T(8,128)(2,1)} %collective-permute-done.14.rest_5_), channel_id=1, source_target_pairs={{0,32},{32,0},{1,33},{33,1},{2,34},{34,2},{3,35},{35,3},{4,36},{36... | collective-permute-start | bytes 1327112 | tf_op jit(solution)/shard_map/ppermute | solution.py:379
  120.4 2.8 %collective-permute-start.15 = (f32[8,128]{1,0:T(8,128)S(1)}, f32[8,128]{1,0:T(8,128)S(1)}, u32[]{:S(2)}, u32[]{:S(2)}) collective-permute-start(f32[8,128]{1,0:T(8,128)S(1)} %copy-done.6), channel_id=1, source_target_pairs={{0,32},{32,0},{1,33},{33,1},{2,34},{34,2},{3,35},{35,3},{4,36},{36... | collective-permute-start | bytes 12296 | tf_op jit(solution)/shard_map/ppermute | solution.py:379
  126.7 11.9 %collective-permute-start.20 = (bf16[72,1152]{1,0:T(8,128)(2,1)S(1)}, bf16[72,1152]{1,0:T(8,128)(2,1)S(1)}, u32[]{:S(2)}, u32[]{:S(2)}) collective-permute-start(bf16[72,1152]{1,0:T(8,128)(2,1)S(1)} %get-tuple-element.70), channel_id=1, source_target_pairs={{0,64},{64,128},{128,192},{192,0},{1,65},{65,129},{129,193},{193,1... | collective-permute-start | bytes 497672 | tf_op jit(solution)/shard_map/ppermute | solution.py:376
  128.5 11.1 %collective-permute-start.21 = (bf16[72,1152]{1,0:T(8,128)(2,1)S(1)}, bf16[72,1152]{1,0:T(8,128)(2,1)S(1)}, u32[]{:S(2)}, u32[]{:S(2)}) collective-permute-start(bf16[72,1152]{1,0:T(8,128)(2,1)S(1)} %get-tuple-element.71), channel_id=1, source_target_pairs={{0,128},{64,192},{128,0},{192,64},{1,129},{65,193},{129,1},{193,65... | collective-permute-start | bytes 497672 | tf_op jit(solution)/shard_map/ppermute | solution.py:376
  132.0 7.6 %collective-permute-start.22 = (bf16[72,1152]{1,0:T(8,128)(2,1)S(1)}, bf16[72,1152]{1,0:T(8,128)(2,1)S(1)}, u32[]{:S(2)}, u32[]{:S(2)}) collective-permute-start(bf16[72,1152]{1,0:T(8,128)(2,1)S(1)} %get-tuple-element.72), channel_id=1, source_target_pairs={{0,192},{64,0},{128,64},{192,128},{1,193},{65,1},{129,65},{193,129... | collective-permute-start | bytes 497672 | tf_op jit(solution)/shard_map/ppermute | solution.py:376
  139.7 5.2 %collective-permute-start.23 = (bf16[36,1152]{1,0:T(8,128)(2,1)S(1)}, bf16[36,1152]{1,0:T(8,128)(2,1)S(1)}, u32[]{:S(2)}, u32[]{:S(2)}) collective-permute-start(bf16[36,1152]{1,0:T(8,128)(2,1)S(1)} %get-tuple-element.79), channel_id=1, source_target_pairs={{0,0},{1,1},{2,2},{3,3},{4,4},{5,5},{6,6},{7,7},{64,65},{65,66},{6... | collective-permute-start | bytes 248840 | tf_op jit(solution)/shard_map/ppermute | solution.py:373
  140.4 7.5 %collective-permute-start.24 = (bf16[36,1152]{1,0:T(8,128)(2,1)S(1)}, bf16[36,1152]{1,0:T(8,128)(2,1)S(1)}, u32[]{:S(2)}, u32[]{:S(2)}) collective-permute-start(bf16[36,1152]{1,0:T(8,128)(2,1)S(1)} %get-tuple-element.80), channel_id=1, source_target_pairs={{0,4},{1,5},{2,6},{3,7},{4,0},{5,1},{6,2},{7,3},{64,69},{65,70},{6... | collective-permute-start | bytes 248840 | tf_op jit(solution)/shard_map/ppermute | solution.py:373
  147.9 7.5 %collective-permute-start.27 = (bf16[36,1152]{1,0:T(8,128)(2,1)S(1)}, bf16[36,1152]{1,0:T(8,128)(2,1)S(1)}, u32[]{:S(2)}, u32[]{:S(2)}) collective-permute-start(bf16[36,1152]{1,0:T(8,128)(2,1)S(1)} %add_convert_fusion.1), channel_id=1, source_target_pairs={{0,192},{64,0},{128,64},{192,128},{1,193},{65,1},{129,65},{193,129... | collective-permute-start | bytes 248840 | tf_op jit(solution)/shard_map/ppermute | solution.py:376
  151.7 5.6 %collective-permute-start.26 = (bf16[36,1152]{1,0:T(8,128)(2,1)S(1)}, bf16[36,1152]{1,0:T(8,128)(2,1)S(1)}, u32[]{:S(2)}, u32[]{:S(2)}) collective-permute-start(bf16[36,1152]{1,0:T(8,128)(2,1)S(1)} %add_convert_fusion.1), channel_id=1, source_target_pairs={{0,64},{64,128},{128,192},{192,0},{1,65},{65,129},{129,193},{193,1... | collective-permute-start | bytes 248840 | tf_op jit(solution)/shard_map/ppermute | solution.py:376
  151.7 5.6 %collective-permute-start.25 = (bf16[36,1152]{1,0:T(8,128)(2,1)S(1)}, bf16[36,1152]{1,0:T(8,128)(2,1)S(1)}, u32[]{:S(2)}, u32[]{:S(2)}) collective-permute-start(bf16[36,1152]{1,0:T(8,128)(2,1)S(1)} %add_convert_fusion.1), channel_id=1, source_target_pairs={{0,128},{64,192},{128,0},{192,64},{1,129},{65,193},{129,1},{193,65... | collective-permute-start | bytes 248840 | tf_op jit(solution)/shard_map/ppermute | solution.py:376
  157.4 7.8 %collective-permute-start.28 = (bf16[36,1152]{1,0:T(8,128)(2,1)S(1)}, bf16[36,1152]{1,0:T(8,128)(2,1)S(1)}, u32[]{:S(2)}, u32[]{:S(2)}) collective-permute-start(bf16[36,1152]{1,0:T(8,128)(2,1)S(1)} %add_convert_fusion.own_ref), channel_id=1, source_target_pairs={{0,32},{32,0},{1,33},{33,1},{2,34},{34,2},{3,35},{35,3},{4,36},{36... | collective-permute-start | bytes 248840 | tf_op jit(solution)/shard_map/ppermute | solution.py:379
